TPU v7x, 32 devices: a whole 2x2x4 slice. The times are simulated.
32 devices in a mesh: groups: 2 (over y), dp: 4 (over z), mp: 2 (over x), section: 2 (over core).
Axes of the slice: x: 2, y: 2, z: 4, core: 2. Of those that a mesh axis runs over, the one named last changes fastest.
Arguments:
- online_obs: bfloat16 [64, 192, 2048], P('dp', 'groups', 'mp'), parts along dimension 1, may hold values from -6 to 6
- offline_obs: bfloat16 [64, 64, 2048], P(('groups', 'dp'), None, 'mp'), parts along dimension 0, may hold values from -6 to 6
- online_rewards: float32 [64, 192], P('dp', 'groups'), parts along dimension 1, may hold values from -6 to 6
- offline_rewards: float32 [64, 64], P(('groups', 'dp')), parts along dimension 0, may hold values from -6 to 6
- online_behaviour: float32 [64, 192], P('dp', 'groups'), parts along dimension 1, may hold values from -4.5 to -1.5
- offline_behaviour: float32 [64, 64], P(('groups', 'dp')), parts along dimension 0, may hold values from -4.5 to -1.5
- online_actions: int32 [64, 192], P('dp', 'groups'), parts along dimension 1, may hold values from 0 to 17
- offline_actions: int32 [64, 64], P(('groups', 'dp')), parts along dimension 0, may hold values from 0 to 17
- online_done: int32 [64, 192], P('dp', 'groups'), parts along dimension 1, may hold values 0 or 1
- offline_done: int32 [64, 64], P(('groups', 'dp')), parts along dimension 0, may hold values 0 or 1
- online_lengths: int32 [192], P(('groups', 'dp')), parts along dimension 0, may hold values from 16 to 64, as said below
- offline_lengths: int32 [64], P(('groups', 'dp')), parts along dimension 0, may hold values from 16 to 64, as said below
- torso_weights: bfloat16 [2, 2048, 2048], P('section', None, 'mp'), may hold values from -0.125 to 0.125
- value_head: bfloat16 [2048], P('mp'), may hold values from -0.125 to 0.125
- policy_head: bfloat16 [2048, 18], P('mp'), may hold values from -0.125 to 0.125
Outputs:
- torso_grads: float32 [4, 2048, 2048], P(('groups', 'section'), None, 'mp'), parts along dimension 0
There are 2 independent parts, one for each index of `groups`. A program takes and returns all parts, laid end to end along the dimension named above; an argument that names none is the same for every part. Nothing has to cross between parts.
Inputs may be any that keep to these rules, and one draw needn't show every extreme that they name: `online_lengths`: each array has a trajectory of full length 64. `offline_lengths`: each array has a trajectory of full length 64.
All inputs are finite; a program needn't handle non-finite values. No bound on the sum of `online_done` or of `offline_done` on one device may be relied on, other than what follows from the above.
Results may differ from a plain program's by a relative error of at most 0.003.
Values may be sent and summed in bfloat16 or wider, within the bound.
No kernel may reach another device: no remote copies, remote signals or barrier semaphores. Data moves between devices by JAX's collectives and lax.ppermute only.
A program may use at most 128 MiB of HBM per device.

v0:
```python
import functools
import math

import jax
import jax.numpy as jnp
from jax import lax
from jax.experimental import pallas as pl
from jax.experimental.pallas import tpu as pltpu
from jax.sharding import PartitionSpec as P

DISCOUNT_RATE = 0.99
TRACE_LAMBDA = 0.95


def silu_slope(pre):
    sigma = jax.nn.sigmoid(pre)
    return sigma * (1.0 + pre * (1.0 - sigma))


def importance_trace_terms(
    value_estimates,
    policy_logits,
    reward_rows,
    behaviour_probs,
    taken_actions,
    episode_finished,
    sequence_length,
    objective_scale,
):
    seq_count, step_count = value_estimates.shape
    action_count = policy_logits.shape[0]
    positions = jnp.arange(step_count, dtype=jnp.int32)
    valid_mask = (positions[None, :] < sequence_length[:, None]).astype(jnp.float32)
    zero_column = jnp.zeros((seq_count, 1), jnp.float32)
    valid_next = jnp.concatenate([valid_mask[:, 1:], zero_column], axis=1)
    log_probs = jax.nn.log_softmax(policy_logits, axis=0)
    one_hot = (
        jnp.arange(action_count, dtype=jnp.int32)[:, None, None] == taken_actions[None]
    ).astype(jnp.float32)
    chosen = jnp.sum(one_hot * log_probs, axis=0)
    clip_ratio = jnp.exp(jnp.minimum(chosen - behaviour_probs, 0.0))
    discount = DISCOUNT_RATE * (1.0 - episode_finished.astype(jnp.float32))
    next_value = jnp.concatenate([value_estimates[:, 1:], zero_column], axis=1) * valid_next
    td_error = valid_mask * clip_ratio * (reward_rows + discount * next_value - value_estimates)
    trace_coef = discount * TRACE_LAMBDA * clip_ratio * valid_next

    def backward_step(carried, inputs):
        error_now, coef_now = inputs
        updated = error_now + coef_now * carried
        return (updated, updated)

    final_state, stacked = lax.scan(
        backward_step,
        jnp.zeros((seq_count,), jnp.float32),
        (td_error.T, trace_coef.T),
        reverse=True,
    )
    correction = stacked.T
    targets = value_estimates + correction
    next_target = jnp.concatenate([targets[:, 1:], zero_column], axis=1) * valid_next
    policy_adv = clip_ratio * (reward_rows + discount * next_target - value_estimates)
    value_gradient = -objective_scale * valid_mask * correction
    logits_gradient = (
        objective_scale * (valid_mask * policy_adv)[None] * (jnp.exp(log_probs) - one_hot)
    )
    return (value_gradient, logits_gradient)


def head_terms(hidden, value_w, policy_w):
    logit_part = jnp.einsum("rh,ha->ar", hidden, policy_w, preferred_element_type=jnp.float32)
    value_part = jnp.dot(hidden, value_w, preferred_element_type=jnp.float32)
    return jnp.concatenate([logit_part, value_part[None]], axis=0)


def full_rows(online_part, offline_part):
    return (
        lax.all_gather(online_part, "mp", axis=2, tiled=True),
        lax.all_gather(offline_part, "mp", axis=2, tiled=True),
    )


def general_plan(
    online_obs,
    offline_obs,
    online_rewards,
    offline_rewards,
    online_behaviour,
    offline_behaviour,
    online_actions,
    offline_actions,
    online_done,
    offline_done,
    online_lengths,
    offline_lengths,
    torso_weights,
    value_head,
    policy_head,
):
    owned_online = online_lengths.shape[0]
    owned_offline = offline_obs.shape[0]
    step_count = offline_obs.shape[1]
    action_count = policy_head.shape[1]
    record_stack = jnp.stack(
        [
            online_rewards,
            online_behaviour,
            online_actions.astype(jnp.float32),
            online_done.astype(jnp.float32),
        ]
    )
    records = lax.all_to_all(record_stack, "dp", split_axis=2, concat_axis=1, tiled=True)
    slabs = lax.all_to_all(online_obs, "dp", split_axis=1, concat_axis=0, tiled=True)
    x_online, x_offline = full_rows(slabs, offline_obs)
    feature_count = x_online.shape[2]
    x_online = x_online.reshape(step_count * owned_online, feature_count)
    x_offline = x_offline.reshape(owned_offline * step_count, feature_count)
    weight = torso_weights[0]
    pre_online = jnp.dot(x_online, weight, preferred_element_type=jnp.float32)
    pre_offline = jnp.dot(x_offline, weight, preferred_element_type=jnp.float32)
    hidden_online = jax.nn.silu(pre_online).astype(jnp.bfloat16)
    hidden_offline = jax.nn.silu(pre_offline).astype(jnp.bfloat16)
    is_critic = (lax.axis_index("section") == 0).astype(jnp.float32)
    is_policy = 1.0 - is_critic
    row_keep = jnp.where(jnp.arange(action_count + 1) == action_count, is_critic, is_policy)
    partial_value = jnp.concatenate(
        [
            head_terms(hidden_online, value_head, policy_head),
            head_terms(hidden_offline, value_head, policy_head),
        ],
        axis=1,
    )
    partial_value = partial_value * row_keep[:, None]
    heads = lax.psum(partial_value, ("mp", "section"))
    online_count = step_count * owned_online
    logits_on = (
        heads[:action_count, :online_count]
        .reshape(action_count, step_count, owned_online)
        .transpose(0, 2, 1)
    )
    logits_off = heads[:action_count, online_count:].reshape(
        action_count, owned_offline, step_count
    )
    values_on = heads[action_count, :online_count].reshape(step_count, owned_online).T
    values_off = heads[action_count, online_count:].reshape(owned_offline, step_count)
    record_seq = records.transpose(0, 2, 1)
    value_estimates = jnp.concatenate([values_on, values_off], axis=0)
    policy_logits = jnp.concatenate([logits_on, logits_off], axis=1)
    reward_rows = jnp.concatenate([record_seq[0], offline_rewards], axis=0)
    behaviour_probs = jnp.concatenate([record_seq[1], offline_behaviour], axis=0)
    taken_actions = jnp.concatenate([record_seq[2].astype(jnp.int32), offline_actions], axis=0)
    episode_finished = jnp.concatenate([record_seq[3].astype(jnp.int32), offline_done], axis=0)
    sequence_length = jnp.concatenate([online_lengths, offline_lengths], axis=0)
    total_seqs = online_obs.shape[1] + owned_offline * lax.axis_size("dp")
    hidden_total = value_head.shape[0] * lax.axis_size("mp")
    objective_scale = math.sqrt(hidden_total / (total_seqs * step_count))
    value_gradient, logits_gradient = importance_trace_terms(
        value_estimates,
        policy_logits,
        reward_rows,
        behaviour_probs,
        taken_actions,
        episode_finished,
        sequence_length,
        objective_scale,
    )
    value_gradient = value_gradient * is_critic
    logits_gradient = logits_gradient * is_policy
    dv_on = value_gradient[:owned_online].T.reshape(online_count)
    dv_off = value_gradient[owned_online:].reshape(owned_offline * step_count)
    dl_on = logits_gradient[:, :owned_online].transpose(0, 2, 1).reshape(action_count, online_count)
    dl_off = logits_gradient[:, owned_online:].reshape(action_count, owned_offline * step_count)
    value_w = value_head.astype(jnp.float32)
    policy_w = policy_head.astype(jnp.float32)
    dh_on = dv_on[:, None] * value_w[None, :] + jnp.einsum(
        "ar,ha->rh", dl_on, policy_w, precision=lax.Precision.HIGHEST
    )
    dh_off = dv_off[:, None] * value_w[None, :] + jnp.einsum(
        "ar,ha->rh", dl_off, policy_w, precision=lax.Precision.HIGHEST
    )
    dz_online = (dh_on * silu_slope(pre_online)).astype(jnp.bfloat16)
    dz_offline = (dh_off * silu_slope(pre_offline)).astype(jnp.bfloat16)
    local_grad = jnp.einsum("rd,rh->dh", x_online, dz_online, preferred_element_type=jnp.float32)
    local_grad = local_grad + jnp.einsum(
        "rd,rh->dh", x_offline, dz_offline, preferred_element_type=jnp.float32
    )
    summed = lax.psum(local_grad, "dp")
    return summed[None]


HEAD_ROWS = 24
SPLIT_ROWS = 4 * HEAD_ROWS
COLUMN_BLOCK = 256
GRAD_BLOCK = 512
ADD_BLOCKS = 2
ROW_GROUPS = 4
GRAD_CHUNKS = 8
GRAD_LEAD = 5
LANES = 128
CODE_LIMIT = 32512.0
CODE_TAIL = 16
LOG_TWO = math.log(2.0)
SCRATCH_BYTES = 6 * 1024 * 1024
SWAP = ((0, 1), (1, 0))
TO_CENTER = ((0, 1), (3, 2))
CENTER = ((1, 2), (2, 1))
FROM_CENTER = ((1, 0), (2, 3))
VMEM = pl.BlockSpec(memory_space=pltpu.VMEM)
SMEM = pl.BlockSpec(memory_space=pltpu.SMEM)
EXPONENTS = pltpu.VMEM((CODE_TAIL, LANES), jnp.float32)


SHORT = pl.CostEstimate(flops=1, bytes_accessed=1, transcendentals=0)


def params():
    return pltpu.CompilerParams(vmem_limit_bytes=SCRATCH_BYTES)


def resident(array):
    return pltpu.with_memory_space_constraint(array, pltpu.VMEM)


def vmem_call(body, place, arrays, outs, name, deps=(), scratch=()):
    operands = list(arrays) + list(deps)

    def run(place_ref, *refs):
        body(place_ref, *refs[: len(arrays)], *refs[len(operands) :])

    return pl.pallas_call(
        run,
        in_specs=[SMEM] + [VMEM] * len(operands),
        out_specs=[VMEM] * len(outs),
        out_shape=[pltpu.VMEM(shape, dtype) for shape, dtype in outs],
        scratch_shapes=list(scratch),
        compiler_params=params(),
        cost_estimate=SHORT,
        name=name,
    )(place, *[resident(x) for x in operands])


def own_half_body(place, own_ref, weight_ref, out_ref):
    groups, width, features = own_ref.shape
    at = pl.multiple_of(place[0] * features, features)
    for first in range(0, groups, ROW_GROUPS):
        part = slice(first, first + ROW_GROUPS)
        own = own_ref[part].reshape(-1, features)
        for h in range(0, weight_ref.shape[1], COLUMN_BLOCK):
            block = slice(h, h + COLUMN_BLOCK)
            pre = jnp.dot(
                own, weight_ref[pl.ds(at, features), block], preferred_element_type=jnp.float32
            )
            out_ref[part, :, block] = pre.reshape(-1, width, COLUMN_BLOCK)


def own_half(place, own, weight, deps):
    groups, width, _ = own.shape
    return vmem_call(
        own_half_body,
        place,
        [own, weight],
        [((groups, width, weight.shape[1]), jnp.float32)],
        "own_half",
        deps,
    )[0]


def forward_body(place, pre_ref, got_ref, rest_ref, weight_ref, head_ref, *refs):
    slope_ref, heads_ref, hidden_ref = refs[-3:]
    half, width, features = got_ref.shape
    hidden_count = weight_ref.shape[1]
    m, section = place[0], place[3]
    other_at = pl.multiple_of((1 - m) * features, features)
    count = min(half, ROW_GROUPS)
    for x_ref, start in ((got_ref, section * half), (rest_ref, (1 - section) * half)):
        for first in range(0, half, count):
            at = pl.ds(start + first, count)
            other = x_ref[first : first + count].reshape(-1, features)
            for h in range(0, hidden_count, COLUMN_BLOCK):
                block = slice(h, h + COLUMN_BLOCK)
                pre = jnp.dot(
                    other,
                    weight_ref[pl.ds(other_at, features), block],
                    preferred_element_type=jnp.float32,
                )
                pre = pre + pre_ref[at, :, block].reshape(-1, COLUMN_BLOCK)
                sigma = 0.5 * jnp.tanh(0.5 * pre) + 0.5
                hidden = pre * sigma
                slope = sigma + hidden * (1.0 - sigma)
                slope_ref[at, :, block] = slope.reshape(-1, width, COLUMN_BLOCK)
                hidden_ref[:, block] = hidden.astype(jnp.bfloat16)
            for g in range(count):
                heads = lax.dot_general(
                    head_ref[...],
                    hidden_ref[g * width : (g + 1) * width],
                    (((1,), (1,)), ((), ())),
                    preferred_element_type=jnp.float32,
                )
                heads_ref[start + first + g] = heads[:HEAD_ROWS]


def forward(place, pre, got, rest, weight, head, deps):
    groups, width, hidden_count = pre.shape
    operands = [pre, got, rest, weight, head] + deps
    return pl.pallas_call(
        forward_body,
        in_specs=[SMEM] + [VMEM] * len(operands),
        out_specs=[VMEM, VMEM],
        out_shape=[
            pltpu.VMEM(pre.shape, jnp.float32),
            pltpu.VMEM((groups, HEAD_ROWS, width), jnp.float32),
        ],
        scratch_shapes=[
            pltpu.VMEM((min(groups // 2, ROW_GROUPS) * width, hidden_count), jnp.bfloat16)
        ],
        input_output_aliases={1: 0},
        compiler_params=params(),
        cost_estimate=SHORT,
        name="forward_rows",
    )(place, *[resident(x) for x in operands])


def action_terms(parts, actions, behaviour, action_count):
    heads = parts[0] + parts[1] + (parts[2] + parts[3])
    row = lax.broadcasted_iota(jnp.int32, heads.shape, 0)
    is_logit = row < action_count
    logits = jnp.where(is_logit, heads, -1e30)
    shifted = logits - jnp.max(logits, axis=0, keepdims=True)
    log_sum = jnp.log(jnp.sum(jnp.exp(shifted), axis=0, keepdims=True))
    log_probs = shifted - log_sum
    taken = row == actions
    chosen = jnp.sum(jnp.where(taken, log_probs, 0.0), axis=0, keepdims=True)
    rho = jnp.exp(jnp.minimum(chosen - behaviour, 0.0))
    spread = jnp.where(is_logit, jnp.exp(log_probs) - taken.astype(jnp.float32), 0.0)
    return heads[action_count : action_count + 1], rho, spread


def trace_terms(value, rho, reward, discount, length, position, axis, reach, scale):
    size = value.shape[axis]
    valid = (position < length).astype(jnp.float32)
    valid_next = (position + 1 < length).astype(jnp.float32)
    next_value = pltpu.roll(value, size - 1, axis) * valid_next
    correction = valid * rho * (reward + discount * next_value - value)
    coef = discount * TRACE_LAMBDA * rho * valid_next
    shift = 1
    while shift < reach:
        correction = correction + coef * pltpu.roll(correction, size - shift, axis)
        coef = coef * pltpu.roll(coef, size - shift, axis)
        shift *= 2
    targets = value + correction
    next_target = pltpu.roll(targets, size - 1, axis) * valid_next
    advantage = rho * (reward + discount * next_target - value)
    return -scale * valid * correction, scale * (valid * advantage)


def split_terms(logit_weight, value_weight, spread, action_count):
    row = lax.broadcasted_iota(jnp.int32, spread.shape, 0)
    full = jnp.where(row == action_count, value_weight, logit_weight * spread)
    high = full.astype(jnp.bfloat16).astype(jnp.float32)
    rest = full - high
    middle = rest.astype(jnp.bfloat16).astype(jnp.float32)
    low = rest - middle
    return jnp.concatenate([high, middle, low, jnp.zeros_like(full)], axis=0).astype(jnp.bfloat16)


def write_back(terms, head_ref, slope, dz_ref, g):
    dh = lax.dot_general(
        terms, head_ref[...], (((0,), (0,)), ((), ())), preferred_element_type=jnp.float32
    )
    dz_ref[g] = (dh * slope).astype(jnp.bfloat16)


def online_heads_body(action_count, place, *refs):
    parts = refs[:4]
    actions, behaviour, reward, done, lengths, pack_ref, spread_ref = refs[4:]
    steps = actions.shape[0]
    for t in range(steps):
        value, rho, spread = action_terms(
            [p[t] for p in parts],
            actions[t : t + 1, :],
            behaviour[t : t + 1, :],
            action_count,
        )
        pack_ref[t : t + 1, :] = value
        pack_ref[steps + t : steps + t + 1, :] = rho
        spread_ref[t] = spread
    pack_ref[2 * steps : 3 * steps, :] = reward[...]
    pack_ref[3 * steps : 4 * steps, :] = DISCOUNT_RATE * (1.0 - done[...].astype(jnp.float32))
    pack_ref[4 * steps :, :] = jnp.broadcast_to(lengths[...], (8, lengths.shape[1]))


def online_back_body(action_count, scale, place, *refs):
    blocks, spread, head_ref, slope_ref, dz_ref = refs[:4], *refs[4:]
    steps = spread.shape[0]
    z = place[2]

    def field(i):
        parts = []
        for hop, b in enumerate(blocks):
            part = b[i * steps : (i + 1) * steps, :]
            parts.append(jnp.where(z + hop < len(blocks), part, 0.0) if hop else part)
        return jnp.concatenate(parts, axis=0)

    length = sum(b[4 * steps : 4 * steps + 1, :] for b in blocks).astype(jnp.int32)
    value = field(0)
    position = lax.broadcasted_iota(jnp.int32, value.shape, 0) + z * steps
    value_weight, logit_weight = trace_terms(
        value,
        field(1),
        field(2),
        field(3),
        length,
        position,
        0,
        value.shape[0],
        scale,
    )
    for t in range(steps):
        terms = split_terms(
            logit_weight[t : t + 1, :], value_weight[t : t + 1, :], spread[t], action_count
        )
        write_back(terms, head_ref, slope_ref[t], dz_ref, t)


def offline_back_body(action_count, step_count, scale, place, *refs):
    parts = refs[:4]
    actions, behaviour, reward, done, length, head_ref, slope_ref, dz_ref = refs[4:]
    groups = dz_ref.shape[0]
    values, rhos, spreads = [], [], []
    for g in range(groups):
        value, rho, spread = action_terms(
            [p[g] for p in parts],
            actions[g : g + 1, :],
            behaviour[g : g + 1, :],
            action_count,
        )
        values.append(value)
        rhos.append(rho)
        spreads.append(spread)
    value = jnp.concatenate(values, axis=0)
    rho = jnp.concatenate(rhos, axis=0)
    position = lax.rem(lax.broadcasted_iota(jnp.int32, value.shape, 1), step_count)
    discount = DISCOUNT_RATE * (1.0 - done[...].astype(jnp.float32))
    value_weight, logit_weight = trace_terms(
        value, rho, reward[...], discount, length[...], position, 1, step_count, scale
    )
    for g in range(groups):
        terms = split_terms(
            logit_weight[g : g + 1, :], value_weight[g : g + 1, :], spreads[g], action_count
        )
        write_back(terms, head_ref, slope_ref[g], dz_ref, g)


def encode(v, c, message_ref, exponents_ref):
    rows = v.shape[0]
    largest = jnp.max(jnp.abs(v), axis=0, keepdims=True)
    exponent = jnp.ceil(jnp.log(jnp.maximum(largest, 1e-30)) * (1.0 / LOG_TWO) + 0.01)
    scale = jnp.exp(exponent * -LOG_TWO) * CODE_LIMIT
    code = jnp.floor(v * scale + 0.5)
    at = pl.ds(pl.multiple_of(c * rows, rows), rows)
    message_ref[at, :] = code.astype(jnp.int32).astype(jnp.int16)
    exponents_ref[pl.ds(c, 1), :] = exponent


def encode_tail(message_ref, exponents_ref):
    tail = exponents_ref[...].astype(jnp.int32)
    message_ref[message_ref.shape[0] - CODE_TAIL :, :] = tail.astype(jnp.int16)


def decode_steps(message_ref, steps_ref):
    exponents = message_ref[message_ref.shape[0] - CODE_TAIL :, :]
    exponents = exponents.astype(jnp.int32).astype(jnp.float32)
    steps_ref[...] = jnp.exp(exponents * LOG_TWO) * (1.0 / CODE_LIMIT)


def decode(message_ref, steps_ref, c, rows):
    at = pl.ds(pl.multiple_of(c * rows, rows), rows)
    code = message_ref[at, :].astype(jnp.int32).astype(jnp.float32)
    return code * steps_ref[pl.ds(c, 1), :]


def message_of(rows, columns):
    return ((rows * (columns // LANES) + CODE_TAIL, LANES), jnp.int16)


def grad_body(pieces, column, columns, place, *refs):
    xs, dzs = refs[: len(pieces)], refs[len(pieces) : len(pieces) + 2]
    message_ref, exponents_ref = refs[-2:]
    hidden_count = dzs[0].shape[2]
    section = place[3]
    at = slice(column * columns, (column + 1) * columns)
    exponents_ref[...] = jnp.zeros_like(exponents_ref)

    def step(h, carry):
        block = pl.ds(pl.multiple_of(h * GRAD_BLOCK, GRAD_BLOCK), GRAD_BLOCK)
        total = None
        for x, (which, swapped) in zip(xs, pieces):
            groups, width, _ = x.shape
            first = 0
            if swapped is not None:
                first = (1 - section if swapped else section) * groups
            part = lax.dot_general(
                x[:, :, at].reshape(groups * width, columns),
                dzs[which][pl.ds(first, groups), :, block].reshape(groups * width, GRAD_BLOCK),
                (((0,), (0,)), ((), ())),
                preferred_element_type=jnp.float32,
            )
            total = part if total is None else total + part
        per_block = GRAD_BLOCK // LANES
        for c in range(per_block):
            lanes = total[:, c * LANES : (c + 1) * LANES]
            encode(lanes, h * per_block + c, message_ref, exponents_ref)
        return carry

    lax.fori_loop(0, hidden_count // GRAD_BLOCK, step, 0)
    encode_tail(message_ref, exponents_ref)


def grad_chunk(place, pieces, dzs, column, columns, deps):
    hidden_count = dzs[0].shape[2]
    return vmem_call(
        functools.partial(grad_body, [p[1:] for p in pieces], column, columns),
        place,
        [x for x, _, _ in pieces] + dzs,
        [message_of(columns, hidden_count)],
        "grad_chunk",
        deps,
        [EXPONENTS],
    )[0]


def add_body(count, place, a_ref, b_ref, out_ref, exponents_ref, a_steps, b_steps):
    rows = (out_ref.shape[0] - CODE_TAIL) // count
    decode_steps(a_ref, a_steps)
    decode_steps(b_ref, b_steps)
    exponents_ref[...] = jnp.zeros_like(exponents_ref)

    def step(i, carry):
        for j in range(ADD_BLOCKS):
            c = i * ADD_BLOCKS + j
            v = decode(a_ref, a_steps, c, rows) + decode(b_ref, b_steps, c, rows)
            encode(v, c, out_ref, exponents_ref)
        return carry

    lax.fori_loop(0, count // ADD_BLOCKS, step, 0)
    encode_tail(out_ref, exponents_ref)


def add_chunk(place, a, b, count, deps):
    return vmem_call(
        functools.partial(add_body, count),
        place,
        [a, b],
        [(a.shape, a.dtype)],
        "add_chunk",
        deps,
        [EXPONENTS] * 3,
    )[0]


def place_body(count, rows, of_own, index, place, total, received, *refs):
    out, token, held, steps, sem = refs[-5:]
    token[...] = jnp.zeros_like(token)
    half = place[0] if of_own else 1 - place[0]
    first = pl.multiple_of(half * (out.shape[0] // 2) + index * rows, rows)
    at_end = place[1] == 1

    def write(message):
        decode_steps(message, steps)
        for c in range(count):
            held[:, c * LANES : (c + 1) * LANES] = decode(message, steps, c, rows)

    @pl.when(at_end)
    def _():
        write(received)

    @pl.when(jnp.logical_not(at_end))
    def _():
        write(total)

    copy = pltpu.make_async_copy(held, out.at[pl.ds(first, rows)], sem)
    copy.start()
    copy.wait()


def place_chunk(place, total, received, result, of_own, index, rows, shape, deps):
    hidden_count = shape[1]
    earlier = [] if result is None else [result]
    operands = [total, received] + deps
    return pl.pallas_call(
        functools.partial(place_body, hidden_count // LANES, rows, of_own, index),
        in_specs=[SMEM]
        + [VMEM] * len(operands)
        + [pl.BlockSpec(memory_space=pl.ANY) for _ in earlier],
        out_specs=[pl.BlockSpec(memory_space=pl.ANY), VMEM],
        out_shape=[
            jax.ShapeDtypeStruct(shape, jnp.float32),
            pltpu.VMEM((8, LANES), jnp.float32),
        ],
        scratch_shapes=[
            pltpu.VMEM((rows, hidden_count), jnp.float32),
            EXPONENTS,
            pltpu.SemaphoreType.DMA(()),
        ],
        input_output_aliases={1 + len(operands): 0} if earlier else {},
        compiler_params=params(),
        cost_estimate=SHORT,
        name="place_chunk",
    )(place, *[resident(x) for x in operands], *earlier)


def pipeline_order(count, lead):
    order = [("grad", k) for k in range(min(lead, count))]
    ahead = len(order)
    for k in range(count + 3):
        if k < count:
            order.append(("partial", k))
            while ahead < min(count, lead + 2 * (k + 1)):
                order.append(("grad", ahead))
                ahead += 1
        if 0 <= k - 3 < count:
            order.append(("place", k - 3))
        if 0 <= k - 1 < count:
            order.append(("total", k - 1))
    return order


def after(array, *others):
    return lax.optimization_barrier((array,) + others)[0]


def chip_pair(part, gate=()):
    across = lax.ppermute(part, "mp", SWAP)
    return [
        part,
        lax.ppermute(part, "section", SWAP),
        across,
        lax.ppermute(after(across, *gate), "section", SWAP),
    ]


def line_plan(
    online_obs,
    offline_obs,
    online_rewards,
    offline_rewards,
    online_behaviour,
    offline_behaviour,
    online_actions,
    offline_actions,
    online_done,
    offline_done,
    online_lengths,
    offline_lengths,
    torso_weights,
    value_head,
    policy_head,
):
    section = lax.axis_index("section")
    m = lax.axis_index("mp")
    z = lax.axis_index("dp")
    dp = lax.axis_size("dp")
    steps, online_count, features = online_obs.shape
    offline_count, step_count, _ = offline_obs.shape
    action_count = policy_head.shape[1]
    hidden_count = value_head.shape[0]
    at_end = ((z == 0) | (z == dp - 1)).astype(jnp.int32)
    place = jnp.stack([m, at_end, z, section]).astype(jnp.int32)
    weight = torso_weights[0]
    scale = math.sqrt(
        hidden_count
        * lax.axis_size("mp")
        / ((online_count + offline_count * dp) * step_count)
    )

    offline_groups = offline_count // 2
    offline_rows = offline_obs.reshape(offline_groups, 2 * step_count, features)
    own = [online_obs, offline_rows]
    halves = [
        lax.dynamic_slice_in_dim(x, section * (x.shape[0] // 2), x.shape[0] // 2, axis=0)
        for x in own
    ]

    policy_rows = jnp.where(section == 1, policy_head.T, 0)
    value_row = jnp.where(section == 0, value_head[None], 0)
    head = jnp.concatenate([policy_rows, value_row], axis=0).astype(jnp.bfloat16)
    head = jnp.pad(head, ((0, HEAD_ROWS - action_count - 1), (0, 0)))
    forward_head = jnp.pad(head, ((0, 32 - HEAD_ROWS), (0, 0)))
    back_head = jnp.concatenate([head, head, head, jnp.zeros_like(head)], axis=0)

    owned = online_lengths.shape[0]
    length_row = lax.dynamic_update_slice(
        jnp.zeros((online_count,), jnp.float32), online_lengths.astype(jnp.float32), (z * owned,)
    )
    length_row = length_row[None]
    lanes = (offline_groups, 2 * step_count)
    offline_length = jnp.broadcast_to(offline_lengths[:, None], (offline_count, step_count))
    offline_terms = [
        x.reshape(lanes)
        for x in (
            offline_actions,
            offline_behaviour,
            offline_rewards,
            offline_done,
            offline_length,
        )
    ]

    got = [lax.ppermute(half, "mp", SWAP) for half in halves]
    early = halves + [back_head, forward_head, length_row] + offline_terms
    pre_online = own_half(place, online_obs, weight, early)
    pre_offline = own_half(place, offline_rows, weight, [pre_online])
    rests = [lax.ppermute(after(got[0], pre_offline), "section", SWAP)]
    online_slope, online_part = forward(
        place, pre_online, got[0], rests[0], weight, forward_head, []
    )
    rests.append(lax.ppermute(after(got[1], online_part), "section", SWAP))
    offline_slope, offline_part = forward(
        place, pre_offline, got[1], rests[1], weight, forward_head, [online_part]
    )
    offline_parts = chip_pair(offline_part, [])
    pack, spread = vmem_call(
        functools.partial(online_heads_body, action_count),
        place,
        chip_pair(online_part, [offline_part, offline_parts[2]])
        + [online_actions, online_behaviour, online_rewards, online_done, length_row],
        [
            ((4 * steps + 8, online_count), jnp.float32),
            ((steps, HEAD_ROWS, online_count), jnp.float32),
        ],
        "online_heads",
        [offline_part],
    )

    (dz_offline,) = vmem_call(
        functools.partial(offline_back_body, action_count, step_count, scale),
        place,
        offline_parts + offline_terms + [back_head, offline_slope],
        [(offline_slope.shape, jnp.bfloat16)],
        "offline_back",
        [pack],
    )

    blocks = [pack]
    for hop in range(1, dp):
        pairs = [(i, (i - hop) % dp) for i in range(dp)]
        blocks.append(lax.ppermute(pack, "dp", pairs))
    (dz_online,) = vmem_call(
        functools.partial(online_back_body, action_count, scale),
        place,
        blocks + [spread, back_head, online_slope],
        [(online_slope.shape, jnp.bfloat16)],
        "online_back",
        [dz_offline],
    )

    own_x = [(online_obs, 0, None), (offline_rows, 1, None)]
    other_x = []
    for which in range(2):
        other_x += [(got[which], which, 0), (rests[which], which, 1)]
    columns = 2 * features // GRAD_CHUNKS
    per_half = GRAD_CHUNKS // 2
    lane_blocks = hidden_count // LANES

    messages, inward, partial, across, total, outward = {}, {}, {}, {}, {}, {}
    result, last = None, dz_online
    for kind, k in pipeline_order(GRAD_CHUNKS, GRAD_LEAD):
        if kind == "grad":
            last = messages[k] = grad_chunk(
                place,
                own_x if k < per_half else other_x,
                [dz_online, dz_offline],
                k % per_half,
                columns,
                [last],
            )
            inward[k] = lax.ppermute(last, "dp", TO_CENTER)
        elif kind == "partial":
            last = partial[k] = add_chunk(place, messages[k], inward[k], lane_blocks, [last])
            across[k] = lax.ppermute(last, "dp", CENTER)
        elif kind == "total":
            last = total[k] = add_chunk(place, partial[k], across[k], lane_blocks, [last])
            outward[k] = lax.ppermute(last, "dp", FROM_CENTER)
        else:
            result, last = place_chunk(
                place,
                total[k],
                outward[k],
                result,
                k < per_half,
                k % per_half,
                columns,
                (2 * features, hidden_count),
                [last],
            )
    return result[None]


def solution(mesh):
    on_line = mesh.shape["dp"] == 4 and mesh.shape["mp"] == 2 and mesh.shape["section"] == 2
    in_specs = (
        P("dp", "groups", "mp"),
        P(("groups", "dp"), None, "mp"),
        P("dp", "groups"),
        P(("groups", "dp"), None),
        P("dp", "groups"),
        P(("groups", "dp"), None),
        P("dp", "groups"),
        P(("groups", "dp"), None),
        P("dp", "groups"),
        P(("groups", "dp"), None),
        P(("groups", "dp")),
        P(("groups", "dp")),
        P("section", None, "mp"),
        P("mp"),
        P("mp", None),
    )
    out_specs = P(("groups", "section"), None, "mp")
    per_device = line_plan if on_line else general_plan
    return jax.shard_map(
        per_device, mesh=mesh, in_specs=in_specs, out_specs=out_specs, check_vma=False
    )
```

profile of v0, /device:TPU:0, one launch (start us, length us, event | category | flops | bytes accessed | tf_op | source)
XLA Modules:
  0.0 214.1 jit_solution(8266462681235152196)
XLA Ops:
  0.0 2.8 %constant_dynamic-slice_fusion.1.refs_2_ = bf16[8,96,1024]{2,1,0:T(8,128)(2,1)} fusion(bf16[16,96,1024]{2,1,0:T(8,128)(2,1)} %refs_0_.9, s32[]{:T(128)S(6)} %select_n.31), kind=kLoop, calls=%fused_computation.10 | loop fusion | bytes 3145732 | tf_op jit(solution)/shard_map/dynamic_slice | solution.py:679
  2.8 2.9 %collective-permute-start = (bf16[8,96,1024]{2,1,0:T(8,128)(2,1)}, bf16[8,96,1024]{2,1,0:T(8,128)(2,1)}, u32[]{:S(2)}, u32[]{:S(2)}) collective-permute-start(bf16[8,96,1024]{2,1,0:T(8,128)(2,1)} %constant_dynamic-slice_fusion.1.refs_2_), channel_id=1, source_target_pairs={{0,2},{2,0},{1,3},{3,1},{4,6},{6,4},{5,7},{7,5},{8,10},{10,8},{9,1... | collective-permute-start | bytes 4718600 | tf_op jit(solution)/shard_map/ppermute | solution.py:708
  12.6 2.2 %copy-done.1 = bf16[1,2048,1024]{2,1,0:T(8,128)(2,1)S(1)} copy-done((bf16[1,2048,1024]{2,1,0:T(8,128)(2,1)S(1)}, bf16[1,2048,1024]{2,1,0:T(8,128)(2,1)}, u32[]{:S(2)}) %copy-start.1) | copy-done | bytes 4194328
  14.7 4.9 %own_half.2.refs_2_.pre_ref = f32[16,96,1024]{2,1,0:T(8,128)S(1)} custom-call(s32[4]{0:T(128)S(1)} %pad_add_fusion.place_ref.place, bf16[16,96,1024]{2,1,0:T(8,128)(2,1)S(1)} %copy-done, bf16[2048,1024]{1,0:T(8,128)(2,1)S(1)} %bitcast.11, bf16[8,96,1024]{2,1,0:T(8,128)(2,1)} %constant_dynamic-slice_fusion.1.refs_2_, ...), custom_call_target="tpu_custom_call" | custom-call | flops 1 | bytes 1 | tf_op jit(solution)/shard_map/own_half/pallas_call | solution.py:229
  19.7 1.8 own_half.3.pre_ref
  21.5 19.0 %collective-permute-done.got_ref.refs_0_ = bf16[8,96,1024]{2,1,0:T(8,128)(2,1)} collective-permute-done((bf16[8,96,1024]{2,1,0:T(8,128)(2,1)}, bf16[8,96,1024]{2,1,0:T(8,128)(2,1)}, u32[]{:S(2)}, u32[]{:S(2)}) %collective-permute-start) | collective-permute-done | bytes 1572896 | tf_op jit(solution)/shard_map/ppermute | solution.py:708
  42.2 1.9 collective-permute-done.1.rest_ref.refs_1_
  44.1 7.2 %forward_rows.2 = (f32[16,96,1024]{2,1,0:T(8,128)S(1)}, f32[16,24,96]{2,1,0:T(8,128)S(1)}) custom-call(s32[4]{0:T(128)S(1)} %pad_add_fusion.place_ref.place, f32[16,96,1024]{2,1,0:T(8,128)S(1)} %own_half.2.refs_2_.pre_ref, bf16[8,96,1024]{2,1,0:T(8,128)(2,1)} %collective-permute-done.got_ref.refs_0_, ...), custom_call_target="tpu_custom_call", output_to_operand_aliasing={{0}: (1, {})} | custom-call | flops 1 | bytes 1 | tf_op jit(solution)/shard_map/forward_rows/pallas_call | solution.py:304
  51.4 3.5 %collective-permute-done.2.got_ref.refs_2_ = bf16[2,128,1024]{2,1,0:T(8,128)(2,1)S(1)} collective-permute-done((bf16[2,128,1024]{2,1,0:T(8,128)(2,1)S(1)}, bf16[2,128,1024]{2,1,0:T(8,128)(2,1)S(1)}, u32[]{:S(2)}, u32[]{:S(2)}) %collective-permute-start.2) | collective-permute-done | bytes 524320 | tf_op jit(solution)/shard_map/ppermute | solution.py:708
  56.7 2.7 %forward_rows.3 = (f32[4,128,1024]{2,1,0:T(8,128)S(1)}, f32[4,24,128]{2,1,0:T(8,128)S(1)}) custom-call(s32[4]{0:T(128)S(1)} %pad_add_fusion.place_ref.place, f32[4,128,1024]{2,1,0:T(8,128)S(1)} %own_half.3.pre_ref, bf16[2,128,1024]{2,1,0:T(8,128)(2,1)S(1)} %collective-permute-done.2.got_ref.refs_2_, ...), custom_call_target="tpu_custom_call", output_to_operand_aliasing={{0}: (1, {})} | custom-call | flops 1 | bytes 1 | tf_op jit(solution)/shard_map/forward_rows/pallas_call | solution.py:304
  65.8 1.9 collective-permute-start.10
  67.6 2.3 %collective-permute-start.8 = (f32[72,96]{1,0:T(8,128)S(1)}, f32[72,96]{1,0:T(8,128)S(1)}, u32[]{:S(2)}, u32[]{:S(2)}) collective-permute-start(f32[72,96]{1,0:T(8,128)S(1)} %get-tuple-element.34.refs_11_.refs_0_), channel_id=1, source_target_pairs={{0,12},{4,0},{8,4},{12,8},{1,13},{5,1},{9,5},{13,9},{2,14},{6,2},{... | collective-permute-start | bytes 82952 | tf_op jit(solution)/shard_map/ppermute | solution.py:746
  72.3 2.5 %collective-permute-done.9.refs_2_ = f32[72,96]{1,0:T(8,128)S(1)} collective-permute-done((f32[72,96]{1,0:T(8,128)S(1)}, f32[72,96]{1,0:T(8,128)S(1)}, u32[]{:S(2)}, u32[]{:S(2)}) %collective-permute-start.9) | collective-permute-done | bytes 27680 | tf_op jit(solution)/shard_map/ppermute | solution.py:746
  76.5 2.3 %grad_chunk.8.refs_4_.refs_0_ = s16[2064,128]{1,0:T(8,128)(2,1)S(1)} custom-call(s32[4]{0:T(128)S(1)} %pad_add_fusion.place_ref.place, bf16[16,96,1024]{2,1,0:T(8,128)(2,1)S(1)} %copy-done, bf16[4,128,1024]{2,1,0:T(8,128)(2,1)S(1)} %bitcast.17, bf16[16,96,1024]{2,1,0:T(8,128)(2,1)S(1)} %online_back.1.refs_2_.refs_4_, ...), custom_call_target="tpu_custom_call" | custom-call | flops 1 | bytes 1 | tf_op jit(solution)/shard_map/grad_chunk/pallas_call | solution.py:229
  80.6 2.3 %grad_chunk.9.refs_4_.refs_0_ = s16[2064,128]{1,0:T(8,128)(2,1)S(1)} custom-call(s32[4]{0:T(128)S(1)} %pad_add_fusion.place_ref.place, bf16[16,96,1024]{2,1,0:T(8,128)(2,1)S(1)} %copy-done, bf16[4,128,1024]{2,1,0:T(8,128)(2,1)S(1)} %bitcast.18, bf16[16,96,1024]{2,1,0:T(8,128)(2,1)S(1)} %online_back.1.refs_2_.refs_4_, ...), custom_call_target="tpu_custom_call" | custom-call | flops 1 | bytes 1 | tf_op jit(solution)/shard_map/grad_chunk/pallas_call | solution.py:229
  84.3 2.4 %grad_chunk.10.refs_4_.refs_0_ = s16[2064,128]{1,0:T(8,128)(2,1)S(1)} custom-call(s32[4]{0:T(128)S(1)} %pad_add_fusion.place_ref.place, bf16[16,96,1024]{2,1,0:T(8,128)(2,1)S(1)} %copy-done, bf16[4,128,1024]{2,1,0:T(8,128)(2,1)S(1)} %bitcast.19, bf16[16,96,1024]{2,1,0:T(8,128)(2,1)S(1)} %online_back.1.refs_2_.refs_4_, ...), custom_call_target="tpu_custom_call" | custom-call | flops 1 | bytes 1 | tf_op jit(solution)/shard_map/grad_chunk/pallas_call | solution.py:229
  86.6 2.4 %grad_chunk.11.refs_6_.refs_0_ = s16[2064,128]{1,0:T(8,128)(2,1)S(1)} custom-call(s32[4]{0:T(128)S(1)} %pad_add_fusion.place_ref.place, bf16[16,96,1024]{2,1,0:T(8,128)(2,1)S(1)} %copy-done, bf16[4,128,1024]{2,1,0:T(8,128)(2,1)S(1)} %bitcast.20, bf16[16,96,1024]{2,1,0:T(8,128)(2,1)S(1)} %online_back.1.refs_2_.refs_4_, ...), custom_call_target="tpu_custom_call" | custom-call | flops 1 | bytes 1 | tf_op jit(solution)/shard_map/grad_chunk/pallas_call | solution.py:229
  89.0 3.2 %grad_chunk.12.refs_2_.refs_0_ = s16[2064,128]{1,0:T(8,128)(2,1)S(1)} custom-call(s32[4]{0:T(128)S(1)} %pad_add_fusion.place_ref.place, bf16[8,96,1024]{2,1,0:T(8,128)(2,1)} %collective-permute-done.got_ref.refs_0_, bf16[8,96,1024]{2,1,0:T(8,128)(2,1)S(1)} %collective-permute-done.1.rest_ref.refs_1_, ...), custom_call_target="tpu_custom_call" | custom-call | flops 1 | bytes 1 | tf_op jit(solution)/shard_map/grad_chunk/pallas_call | solution.py:229
  94.9 7.1 %collective-permute-start.19 = (s16[2064,128]{1,0:T(8,128)(2,1)S(1)}, s16[2064,128]{1,0:T(8,128)(2,1)S(1)}, u32[]{:S(2)}, u32[]{:S(2)}) collective-permute-start(s16[2064,128]{1,0:T(8,128)(2,1)S(1)} %grad_chunk.10.refs_4_.refs_0_), channel_id=1, source_target_pairs={{0,4},{12,8},{1,5},{13,9},{2,6},{14,10},{3,7},{15,11},{16,20},{28,... | collective-permute-start | bytes 1585160 | tf_op jit(solution)/shard_map/ppermute | solution.py:776
  102.0 3.2 %grad_chunk.13.refs_6_.refs_0_ = s16[2064,128]{1,0:T(8,128)(2,1)S(1)} custom-call(s32[4]{0:T(128)S(1)} %pad_add_fusion.place_ref.place, bf16[8,96,1024]{2,1,0:T(8,128)(2,1)} %collective-permute-done.got_ref.refs_0_, bf16[8,96,1024]{2,1,0:T(8,128)(2,1)S(1)} %collective-permute-done.1.rest_ref.refs_1_, ...), custom_call_target="tpu_custom_call" | custom-call | flops 1 | bytes 1 | tf_op jit(solution)/shard_map/grad_chunk/pallas_call | solution.py:229
  105.2 3.2 %grad_chunk.14.refs_2_.refs_0_ = s16[2064,128]{1,0:T(8,128)(2,1)S(1)} custom-call(s32[4]{0:T(128)S(1)} %pad_add_fusion.place_ref.place, bf16[8,96,1024]{2,1,0:T(8,128)(2,1)} %collective-permute-done.got_ref.refs_0_, bf16[8,96,1024]{2,1,0:T(8,128)(2,1)S(1)} %collective-permute-done.1.rest_ref.refs_1_, ...), custom_call_target="tpu_custom_call" | custom-call | flops 1 | bytes 1 | tf_op jit(solution)/shard_map/grad_chunk/pallas_call | solution.py:229
  110.3 3.1 %collective-permute-start.17 = (s16[2064,128]{1,0:T(8,128)(2,1)S(1)}, s16[2064,128]{1,0:T(8,128)(2,1)S(1)}, u32[]{:S(2)}, u32[]{:S(2)}) collective-permute-start(s16[2064,128]{1,0:T(8,128)(2,1)S(1)} %grad_chunk.11.refs_6_.refs_0_), channel_id=1, source_target_pairs={{0,4},{12,8},{1,5},{13,9},{2,6},{14,10},{3,7},{15,11},{16,20},{28,... | collective-permute-start | bytes 1585160 | tf_op jit(solution)/shard_map/ppermute | solution.py:776
  113.4 3.2 %grad_chunk.15.refs_2_.refs_0_ = s16[2064,128]{1,0:T(8,128)(2,1)S(1)} custom-call(s32[4]{0:T(128)S(1)} %pad_add_fusion.place_ref.place, bf16[8,96,1024]{2,1,0:T(8,128)(2,1)} %collective-permute-done.got_ref.refs_0_, bf16[8,96,1024]{2,1,0:T(8,128)(2,1)S(1)} %collective-permute-done.1.rest_ref.refs_1_, ...), custom_call_target="tpu_custom_call" | custom-call | flops 1 | bytes 1 | tf_op jit(solution)/shard_map/grad_chunk/pallas_call | solution.py:229
  121.0 7.3 %collective-permute-start.23 = (s16[2064,128]{1,0:T(8,128)(2,1)S(1)}, s16[2064,128]{1,0:T(8,128)(2,1)S(1)}, u32[]{:S(2)}, u32[]{:S(2)}) collective-permute-start(s16[2064,128]{1,0:T(8,128)(2,1)S(1)} %grad_chunk.12.refs_2_.refs_0_), channel_id=1, source_target_pairs={{0,4},{12,8},{1,5},{13,9},{2,6},{14,10},{3,7},{15,11},{16,20},{28,... | collective-permute-start | bytes 1585160 | tf_op jit(solution)/shard_map/ppermute | solution.py:776
  132.6 6.4 %collective-permute-start.16 = (s16[2064,128]{1,0:T(8,128)(2,1)S(1)}, s16[2064,128]{1,0:T(8,128)(2,1)S(1)}, u32[]{:S(2)}, u32[]{:S(2)}) collective-permute-start(s16[2064,128]{1,0:T(8,128)(2,1)S(1)} %grad_chunk.13.refs_6_.refs_0_), channel_id=1, source_target_pairs={{0,4},{12,8},{1,5},{13,9},{2,6},{14,10},{3,7},{15,11},{16,20},{28,... | collective-permute-start | bytes 1585160 | tf_op jit(solution)/shard_map/ppermute | solution.py:776
  145.0 7.3 %collective-permute-start.28 = (s16[2064,128]{1,0:T(8,128)(2,1)S(1)}, s16[2064,128]{1,0:T(8,128)(2,1)S(1)}, u32[]{:S(2)}, u32[]{:S(2)}) collective-permute-start(s16[2064,128]{1,0:T(8,128)(2,1)S(1)} %grad_chunk.14.refs_2_.refs_0_), channel_id=1, source_target_pairs={{0,4},{12,8},{1,5},{13,9},{2,6},{14,10},{3,7},{15,11},{16,20},{28,... | collective-permute-start | bytes 1585160 | tf_op jit(solution)/shard_map/ppermute | solution.py:776
  158.4 6.4 %collective-permute-start.15 = (s16[2064,128]{1,0:T(8,128)(2,1)S(1)}, s16[2064,128]{1,0:T(8,128)(2,1)S(1)}, u32[]{:S(2)}, u32[]{:S(2)}) collective-permute-start(s16[2064,128]{1,0:T(8,128)(2,1)S(1)} %grad_chunk.15.refs_2_.refs_0_), channel_id=1, source_target_pairs={{0,4},{12,8},{1,5},{13,9},{2,6},{14,10},{3,7},{15,11},{16,20},{28,... | collective-permute-start | bytes 1585160 | tf_op jit(solution)/shard_map/ppermute | solution.py:776
  177.1 7.4 %collective-permute-done.34.received = s16[2064,128]{1,0:T(8,128)(2,1)S(1)} collective-permute-done((s16[2064,128]{1,0:T(8,128)(2,1)S(1)}, s16[2064,128]{1,0:T(8,128)(2,1)S(1)}, u32[]{:S(2)}, u32[]{:S(2)}) %collective-permute-start.34) | collective-permute-done | bytes 528416 | tf_op jit(solution)/shard_map/ppermute | solution.py:782
  188.6 7.2 %collective-permute-done.32.received = s16[2064,128]{1,0:T(8,128)(2,1)S(1)} collective-permute-done((s16[2064,128]{1,0:T(8,128)(2,1)S(1)}, s16[2064,128]{1,0:T(8,128)(2,1)S(1)}, u32[]{:S(2)}, u32[]{:S(2)}) %collective-permute-start.32) | collective-permute-done | bytes 528416 | tf_op jit(solution)/shard_map/ppermute | solution.py:782
  200.0 6.0 %collective-permute-done.36.received = s16[2064,128]{1,0:T(8,128)(2,1)S(1)} collective-permute-done((s16[2064,128]{1,0:T(8,128)(2,1)S(1)}, s16[2064,128]{1,0:T(8,128)(2,1)S(1)}, u32[]{:S(2)}, u32[]{:S(2)}) %collective-permute-start.36) | collective-permute-done | bytes 528416 | tf_op jit(solution)/shard_map/ppermute | solution.py:782
  207.7 4.0 %collective-permute-done.35.received = s16[2064,128]{1,0:T(8,128)(2,1)S(1)} collective-permute-done((s16[2064,128]{1,0:T(8,128)(2,1)S(1)}, s16[2064,128]{1,0:T(8,128)(2,1)S(1)}, u32[]{:S(2)}, u32[]{:S(2)}) %collective-permute-start.35) | collective-permute-done | bytes 528416 | tf_op jit(solution)/shard_map/ppermute | solution.py:782
  211.6 2.3 %place_chunk.15 = (f32[2048,1024]{1,0:T(8,128)}, f32[8,128]{1,0:T(8,128)}) custom-call(s32[4]{0:T(128)S(1)} %pad_add_fusion.place_ref.place, s16[2064,128]{1,0:T(8,128)(2,1)S(1)} %add_chunk.31.refs_0_.total, s16[2064,128]{1,0:T(8,128)(2,1)S(1)} %collective-permute-done.35.received, ...), custom_call_target="tpu_custom_call", output_to_operand_aliasing={{0}: (4, {})} | custom-call | flops 1 | bytes 1 | tf_op jit(solution)/shard_map/place_chunk/pallas_call | solution.py:589
  (116 shorter events, 71.0 us)
Async XLA Ops:
  2.8 37.6 %collective-permute-start = (bf16[8,96,1024]{2,1,0:T(8,128)(2,1)}, bf16[8,96,1024]{2,1,0:T(8,128)(2,1)}, u32[]{:S(2)}, u32[]{:S(2)}) collective-permute-start(bf16[8,96,1024]{2,1,0:T(8,128)(2,1)} %constant_dynamic-slice_fusion.1.refs_2_), channel_id=1, source_target_pairs={{0,2},{2,0},{1,3},{3,1},{4,6},{6,4},{5,7},{7,5},{8,10},{10,8},{9,1... | collective-permute-start | bytes 4718600 | tf_op jit(solution)/shard_map/ppermute | solution.py:708
  40.5 14.3 %collective-permute-start.2 = (bf16[2,128,1024]{2,1,0:T(8,128)(2,1)S(1)}, bf16[2,128,1024]{2,1,0:T(8,128)(2,1)S(1)}, u32[]{:S(2)}, u32[]{:S(2)}) collective-permute-start(bf16[2,128,1024]{2,1,0:T(8,128)(2,1)S(1)} %constant_dynamic-slice_fusion.refs_3_), channel_id=1, source_target_pairs={{0,2},{2,0},{1,3},{3,1},{4,6},{6,4},{5,7},{7,5},{8,10},{10,8},{9,1... | collective-permute-start | bytes 1572872 | tf_op jit(solution)/shard_map/ppermute | solution.py:708
  54.8 7.3 %collective-permute-start.5 = (f32[16,24,96]{2,1,0:T(8,128)S(1)}, f32[16,24,96]{2,1,0:T(8,128)S(1)}, u32[]{:S(2)}, u32[]{:S(2)}) collective-permute-start(f32[16,24,96]{2,1,0:T(8,128)S(1)} %get-tuple-element.30.refs_0_), channel_id=1, source_target_pairs={{0,2},{2,0},{1,3},{3,1},{4,6},{6,4},{5,7},{7,5},{8,10},{10,8},{9,1... | collective-permute-start | bytes 442376 | tf_op jit(solution)/shard_map/ppermute | solution.py:632
  63.6 7.1 %collective-permute-start.11 = (f32[4,24,128]{2,1,0:T(8,128)S(1)}, f32[4,24,128]{2,1,0:T(8,128)S(1)}, u32[]{:S(2)}, u32[]{:S(2)}) collective-permute-start(f32[4,24,128]{2,1,0:T(8,128)S(1)} %get-tuple-element.32.refs_9_.refs_0_), channel_id=1, source_target_pairs={{0,1},{1,0},{2,3},{3,2},{4,5},{5,4},{6,7},{7,6},{8,9},{9,8},{10,11... | collective-permute-start | bytes 147464 | tf_op jit(solution)/shard_map/ppermute | solution.py:635
  64.1 6.6 %collective-permute-start.12 = (f32[4,24,128]{2,1,0:T(8,128)S(1)}, f32[4,24,128]{2,1,0:T(8,128)S(1)}, u32[]{:S(2)}, u32[]{:S(2)}) collective-permute-start(f32[4,24,128]{2,1,0:T(8,128)S(1)} %collective-permute-done.6.refs_2_), channel_id=1, source_target_pairs={{0,1},{1,0},{2,3},{3,2},{4,5},{5,4},{6,7},{7,6},{8,9},{9,8},{10,11... | collective-permute-start | bytes 147464 | tf_op jit(solution)/shard_map/ppermute | solution.py:637
  65.8 6.5 %collective-permute-start.10 = (f32[72,96]{1,0:T(8,128)S(1)}, f32[72,96]{1,0:T(8,128)S(1)}, u32[]{:S(2)}, u32[]{:S(2)}) collective-permute-start(f32[72,96]{1,0:T(8,128)S(1)} %get-tuple-element.34.refs_11_.refs_0_), channel_id=1, source_target_pairs={{0,4},{4,8},{8,12},{12,0},{1,5},{5,9},{9,13},{13,1},{2,6},{6,10},{... | collective-permute-start | bytes 82952 | tf_op jit(solution)/shard_map/ppermute | solution.py:746
  67.6 4.6 %collective-permute-start.8 = (f32[72,96]{1,0:T(8,128)S(1)}, f32[72,96]{1,0:T(8,128)S(1)}, u32[]{:S(2)}, u32[]{:S(2)}) collective-permute-start(f32[72,96]{1,0:T(8,128)S(1)} %get-tuple-element.34.refs_11_.refs_0_), channel_id=1, source_target_pairs={{0,12},{4,0},{8,4},{12,8},{1,13},{5,1},{9,5},{13,9},{2,14},{6,2},{... | collective-permute-start | bytes 82952 | tf_op jit(solution)/shard_map/ppermute | solution.py:746
  69.9 4.9 %collective-permute-start.9 = (f32[72,96]{1,0:T(8,128)S(1)}, f32[72,96]{1,0:T(8,128)S(1)}, u32[]{:S(2)}, u32[]{:S(2)}) collective-permute-start(f32[72,96]{1,0:T(8,128)S(1)} %get-tuple-element.34.refs_11_.refs_0_), channel_id=1, source_target_pairs={{0,8},{4,12},{8,0},{12,4},{1,9},{5,13},{9,1},{13,5},{2,10},{6,14},... | collective-permute-start | bytes 82952 | tf_op jit(solution)/shard_map/ppermute | solution.py:746
  78.8 14.2 %collective-permute-start.14 = (s16[2064,128]{1,0:T(8,128)(2,1)S(1)}, s16[2064,128]{1,0:T(8,128)(2,1)S(1)}, u32[]{:S(2)}, u32[]{:S(2)}) collective-permute-start(s16[2064,128]{1,0:T(8,128)(2,1)S(1)} %grad_chunk.8.refs_4_.refs_0_), channel_id=1, source_target_pairs={{0,4},{12,8},{1,5},{13,9},{2,6},{14,10},{3,7},{15,11},{16,20},{28,... | collective-permute-start | bytes 1585160 | tf_op jit(solution)/shard_map/ppermute | solution.py:776
  82.9 25.5 %collective-permute-start.13 = (s16[2064,128]{1,0:T(8,128)(2,1)S(1)}, s16[2064,128]{1,0:T(8,128)(2,1)S(1)}, u32[]{:S(2)}, u32[]{:S(2)}) collective-permute-start(s16[2064,128]{1,0:T(8,128)(2,1)S(1)} %grad_chunk.9.refs_4_.refs_0_), channel_id=1, source_target_pairs={{0,4},{12,8},{1,5},{13,9},{2,6},{14,10},{3,7},{15,11},{16,20},{28,... | collective-permute-start | bytes 1585160 | tf_op jit(solution)/shard_map/ppermute | solution.py:776
  94.2 22.5 %collective-permute-start.20 = (s16[2064,128]{1,0:T(8,128)(2,1)S(1)}, s16[2064,128]{1,0:T(8,128)(2,1)S(1)}, u32[]{:S(2)}, u32[]{:S(2)}) collective-permute-start(s16[2064,128]{1,0:T(8,128)(2,1)S(1)} %add_chunk.16.refs_6_.refs_0_), channel_id=1, source_target_pairs={{4,8},{8,4},{5,9},{9,5},{6,10},{10,6},{7,11},{11,7},{20,24},{24,20... | collective-permute-start | bytes 1585160 | tf_op jit(solution)/shard_map/ppermute | solution.py:779
  94.9 24.2 %collective-permute-start.19 = (s16[2064,128]{1,0:T(8,128)(2,1)S(1)}, s16[2064,128]{1,0:T(8,128)(2,1)S(1)}, u32[]{:S(2)}, u32[]{:S(2)}) collective-permute-start(s16[2064,128]{1,0:T(8,128)(2,1)S(1)} %grad_chunk.10.refs_4_.refs_0_), channel_id=1, source_target_pairs={{0,4},{12,8},{1,5},{13,9},{2,6},{14,10},{3,7},{15,11},{16,20},{28,... | collective-permute-start | bytes 1585160 | tf_op jit(solution)/shard_map/ppermute | solution.py:776
  109.6 18.6 %collective-permute-start.18 = (s16[2064,128]{1,0:T(8,128)(2,1)S(1)}, s16[2064,128]{1,0:T(8,128)(2,1)S(1)}, u32[]{:S(2)}, u32[]{:S(2)}) collective-permute-start(s16[2064,128]{1,0:T(8,128)(2,1)S(1)} %add_chunk.17.refs_6_.refs_0_), channel_id=1, source_target_pairs={{4,8},{8,4},{5,9},{9,5},{6,10},{10,6},{7,11},{11,7},{20,24},{24,20... | collective-permute-start | bytes 1585160 | tf_op jit(solution)/shard_map/ppermute | solution.py:779
  110.3 20.4 %collective-permute-start.17 = (s16[2064,128]{1,0:T(8,128)(2,1)S(1)}, s16[2064,128]{1,0:T(8,128)(2,1)S(1)}, u32[]{:S(2)}, u32[]{:S(2)}) collective-permute-start(s16[2064,128]{1,0:T(8,128)(2,1)S(1)} %grad_chunk.11.refs_6_.refs_0_), channel_id=1, source_target_pairs={{0,4},{12,8},{1,5},{13,9},{2,6},{14,10},{3,7},{15,11},{16,20},{28,... | collective-permute-start | bytes 1585160 | tf_op jit(solution)/shard_map/ppermute | solution.py:776
  117.8 14.8 %collective-permute-start.25 = (s16[2064,128]{1,0:T(8,128)(2,1)S(1)}, s16[2064,128]{1,0:T(8,128)(2,1)S(1)}, u32[]{:S(2)}, u32[]{:S(2)}) collective-permute-start(s16[2064,128]{1,0:T(8,128)(2,1)S(1)} %add_chunk.18.refs_2_.total), channel_id=1, source_target_pairs={{4,0},{8,12},{5,1},{9,13},{6,2},{10,14},{7,3},{11,15},{20,16},{24,... | collective-permute-start | bytes 1585160 | tf_op jit(solution)/shard_map/ppermute | solution.py:782
  120.3 20.4 %collective-permute-start.24 = (s16[2064,128]{1,0:T(8,128)(2,1)S(1)}, s16[2064,128]{1,0:T(8,128)(2,1)S(1)}, u32[]{:S(2)}, u32[]{:S(2)}) collective-permute-start(s16[2064,128]{1,0:T(8,128)(2,1)S(1)} %add_chunk.19.refs_2_.refs_0_), channel_id=1, source_target_pairs={{4,8},{8,4},{5,9},{9,5},{6,10},{10,6},{7,11},{11,7},{20,24},{24,20... | collective-permute-start | bytes 1585160 | tf_op jit(solution)/shard_map/ppermute | solution.py:779
  121.0 22.2 %collective-permute-start.23 = (s16[2064,128]{1,0:T(8,128)(2,1)S(1)}, s16[2064,128]{1,0:T(8,128)(2,1)S(1)}, u32[]{:S(2)}, u32[]{:S(2)}) collective-permute-start(s16[2064,128]{1,0:T(8,128)(2,1)S(1)} %grad_chunk.12.refs_2_.refs_0_), channel_id=1, source_target_pairs={{0,4},{12,8},{1,5},{13,9},{2,6},{14,10},{3,7},{15,11},{16,20},{28,... | collective-permute-start | bytes 1585160 | tf_op jit(solution)/shard_map/ppermute | solution.py:776
  129.4 15.6 %collective-permute-start.22 = (s16[2064,128]{1,0:T(8,128)(2,1)S(1)}, s16[2064,128]{1,0:T(8,128)(2,1)S(1)}, u32[]{:S(2)}, u32[]{:S(2)}) collective-permute-start(s16[2064,128]{1,0:T(8,128)(2,1)S(1)} %add_chunk.20.refs_2_.total), channel_id=1, source_target_pairs={{4,0},{8,12},{5,1},{9,13},{6,2},{10,14},{7,3},{11,15},{20,16},{24,... | collective-permute-start | bytes 1585160 | tf_op jit(solution)/shard_map/ppermute | solution.py:782
  131.9 22.1 %collective-permute-start.21 = (s16[2064,128]{1,0:T(8,128)(2,1)S(1)}, s16[2064,128]{1,0:T(8,128)(2,1)S(1)}, u32[]{:S(2)}, u32[]{:S(2)}) collective-permute-start(s16[2064,128]{1,0:T(8,128)(2,1)S(1)} %add_chunk.21.refs_0_), channel_id=1, source_target_pairs={{4,8},{8,4},{5,9},{9,5},{6,10},{10,6},{7,11},{11,7},{20,24},{24,20... | collective-permute-start | bytes 1585160 | tf_op jit(solution)/shard_map/ppermute | solution.py:779
  132.6 23.9 %collective-permute-start.16 = (s16[2064,128]{1,0:T(8,128)(2,1)S(1)}, s16[2064,128]{1,0:T(8,128)(2,1)S(1)}, u32[]{:S(2)}, u32[]{:S(2)}) collective-permute-start(s16[2064,128]{1,0:T(8,128)(2,1)S(1)} %grad_chunk.13.refs_6_.refs_0_), channel_id=1, source_target_pairs={{0,4},{12,8},{1,5},{13,9},{2,6},{14,10},{3,7},{15,11},{16,20},{28,... | collective-permute-start | bytes 1585160 | tf_op jit(solution)/shard_map/ppermute | solution.py:776
  141.9 16.5 %collective-permute-start.30 = (s16[2064,128]{1,0:T(8,128)(2,1)S(1)}, s16[2064,128]{1,0:T(8,128)(2,1)S(1)}, u32[]{:S(2)}, u32[]{:S(2)}) collective-permute-start(s16[2064,128]{1,0:T(8,128)(2,1)S(1)} %add_chunk.22.refs_2_.total), channel_id=1, source_target_pairs={{4,0},{8,12},{5,1},{9,13},{6,2},{10,14},{7,3},{11,15},{20,16},{24,... | collective-permute-start | bytes 1585160 | tf_op jit(solution)/shard_map/ppermute | solution.py:782
  144.3 22.1 %collective-permute-start.29 = (s16[2064,128]{1,0:T(8,128)(2,1)S(1)}, s16[2064,128]{1,0:T(8,128)(2,1)S(1)}, u32[]{:S(2)}, u32[]{:S(2)}) collective-permute-start(s16[2064,128]{1,0:T(8,128)(2,1)S(1)} %add_chunk.23.refs_0_), channel_id=1, source_target_pairs={{4,8},{8,4},{5,9},{9,5},{6,10},{10,6},{7,11},{11,7},{20,24},{24,20... | collective-permute-start | bytes 1585160 | tf_op jit(solution)/shard_map/ppermute | solution.py:779
  145.0 23.9 %collective-permute-start.28 = (s16[2064,128]{1,0:T(8,128)(2,1)S(1)}, s16[2064,128]{1,0:T(8,128)(2,1)S(1)}, u32[]{:S(2)}, u32[]{:S(2)}) collective-permute-start(s16[2064,128]{1,0:T(8,128)(2,1)S(1)} %grad_chunk.14.refs_2_.refs_0_), channel_id=1, source_target_pairs={{0,4},{12,8},{1,5},{13,9},{2,6},{14,10},{3,7},{15,11},{16,20},{28,... | collective-permute-start | bytes 1585160 | tf_op jit(solution)/shard_map/ppermute | solution.py:776
  155.2 15.8 %collective-permute-start.27 = (s16[2064,128]{1,0:T(8,128)(2,1)S(1)}, s16[2064,128]{1,0:T(8,128)(2,1)S(1)}, u32[]{:S(2)}, u32[]{:S(2)}) collective-permute-start(s16[2064,128]{1,0:T(8,128)(2,1)S(1)} %add_chunk.24.refs_2_.total), channel_id=1, source_target_pairs={{4,0},{8,12},{5,1},{9,13},{6,2},{10,14},{7,3},{11,15},{20,16},{24,... | collective-permute-start | bytes 1585160 | tf_op jit(solution)/shard_map/ppermute | solution.py:782
  157.7 15.1 %collective-permute-start.26 = (s16[2064,128]{1,0:T(8,128)(2,1)S(1)}, s16[2064,128]{1,0:T(8,128)(2,1)S(1)}, u32[]{:S(2)}, u32[]{:S(2)}) collective-permute-start(s16[2064,128]{1,0:T(8,128)(2,1)S(1)} %add_chunk.25.refs_0_), channel_id=1, source_target_pairs={{4,8},{8,4},{5,9},{9,5},{6,10},{10,6},{7,11},{11,7},{20,24},{24,20... | collective-permute-start | bytes 1585160 | tf_op jit(solution)/shard_map/ppermute | solution.py:779
  158.4 16.8 %collective-permute-start.15 = (s16[2064,128]{1,0:T(8,128)(2,1)S(1)}, s16[2064,128]{1,0:T(8,128)(2,1)S(1)}, u32[]{:S(2)}, u32[]{:S(2)}) collective-permute-start(s16[2064,128]{1,0:T(8,128)(2,1)S(1)} %grad_chunk.15.refs_2_.refs_0_), channel_id=1, source_target_pairs={{0,4},{12,8},{1,5},{13,9},{2,6},{14,10},{3,7},{15,11},{16,20},{28,... | collective-permute-start | bytes 1585160 | tf_op jit(solution)/shard_map/ppermute | solution.py:776
  167.6 16.8 %collective-permute-start.34 = (s16[2064,128]{1,0:T(8,128)(2,1)S(1)}, s16[2064,128]{1,0:T(8,128)(2,1)S(1)}, u32[]{:S(2)}, u32[]{:S(2)}) collective-permute-start(s16[2064,128]{1,0:T(8,128)(2,1)S(1)} %add_chunk.26.refs_2_.total), channel_id=1, source_target_pairs={{4,0},{8,12},{5,1},{9,13},{6,2},{10,14},{7,3},{11,15},{20,16},{24,... | collective-permute-start | bytes 1585160 | tf_op jit(solution)/shard_map/ppermute | solution.py:782
  170.1 16.1 %collective-permute-start.33 = (s16[2064,128]{1,0:T(8,128)(2,1)S(1)}, s16[2064,128]{1,0:T(8,128)(2,1)S(1)}, u32[]{:S(2)}, u32[]{:S(2)}) collective-permute-start(s16[2064,128]{1,0:T(8,128)(2,1)S(1)} %add_chunk.27.refs_0_), channel_id=1, source_target_pairs={{4,8},{8,4},{5,9},{9,5},{6,10},{10,6},{7,11},{11,7},{20,24},{24,20... | collective-permute-start | bytes 1585160 | tf_op jit(solution)/shard_map/ppermute | solution.py:779
  173.9 21.9 %collective-permute-start.32 = (s16[2064,128]{1,0:T(8,128)(2,1)S(1)}, s16[2064,128]{1,0:T(8,128)(2,1)S(1)}, u32[]{:S(2)}, u32[]{:S(2)}) collective-permute-start(s16[2064,128]{1,0:T(8,128)(2,1)S(1)} %add_chunk.28.refs_2_.total), channel_id=1, source_target_pairs={{4,0},{8,12},{5,1},{9,13},{6,2},{10,14},{7,3},{11,15},{20,16},{24,... | collective-permute-start | bytes 1585160 | tf_op jit(solution)/shard_map/ppermute | solution.py:782
  176.4 21.1 %collective-permute-start.31 = (s16[2064,128]{1,0:T(8,128)(2,1)S(1)}, s16[2064,128]{1,0:T(8,128)(2,1)S(1)}, u32[]{:S(2)}, u32[]{:S(2)}) collective-permute-start(s16[2064,128]{1,0:T(8,128)(2,1)S(1)} %add_chunk.29.refs_0_), channel_id=1, source_target_pairs={{4,8},{8,4},{5,9},{9,5},{6,10},{10,6},{7,11},{11,7},{20,24},{24,20... | collective-permute-start | bytes 1585160 | tf_op jit(solution)/shard_map/ppermute | solution.py:779
  187.3 18.6 %collective-permute-start.36 = (s16[2064,128]{1,0:T(8,128)(2,1)S(1)}, s16[2064,128]{1,0:T(8,128)(2,1)S(1)}, u32[]{:S(2)}, u32[]{:S(2)}) collective-permute-start(s16[2064,128]{1,0:T(8,128)(2,1)S(1)} %add_chunk.30.refs_0_.total), channel_id=1, source_target_pairs={{4,0},{8,12},{5,1},{9,13},{6,2},{10,14},{7,3},{11,15},{20,16},{24,... | collective-permute-start | bytes 1585160 | tf_op jit(solution)/shard_map/ppermute | solution.py:782
  198.7 13.0 %collective-permute-start.35 = (s16[2064,128]{1,0:T(8,128)(2,1)S(1)}, s16[2064,128]{1,0:T(8,128)(2,1)S(1)}, u32[]{:S(2)}, u32[]{:S(2)}) collective-permute-start(s16[2064,128]{1,0:T(8,128)(2,1)S(1)} %add_chunk.31.refs_0_.total), channel_id=1, source_target_pairs={{4,0},{8,12},{5,1},{9,13},{6,2},{10,14},{7,3},{11,15},{20,16},{24,... | collective-permute-start | bytes 1585160 | tf_op jit(solution)/shard_map/ppermute | solution.py:782
  (12 other events, 88.3 us)
where the time goes:
time: 215 us; the launch traced here: 214 us
  Pallas kernels  75.4 us (35%)
  starting transfers between devices  70.4 us (33%)
  waiting for transfers between devices  55.6 us (26%)
  local copies, waits for them, and re-layouts  10.2 us (5%)
    pallas_call x29, Pallas kernels, vmem_call(): pl.pallas_call(run, in_specs=[SMEM] + [VMEM] * len(operands), out_specs=[...  51.4 us
    ppermute x8, starting transfers between devices, line_plan(): inward[k] = lax.ppermute(last, 'dp', TO_CENTER)  40.6 us
    ppermute x8, waiting for transfers between devices, line_plan(): outward[k] = lax.ppermute(last, 'dp', FROM_CENTER)  24.6 us
    ppermute x2, waiting for transfers between devices, line_plan(): got = [lax.ppermute(half, 'mp', SWAP) for half in halves]  22.4 us
    pallas_call x8, Pallas kernels, place_chunk(): pl.pallas_call(functools.partial(place_body, hidden_count // LANES, rows,...  14.1 us
    ppermute x8, starting transfers between devices, line_plan(): outward[k] = lax.ppermute(last, 'dp', FROM_CENTER)  10.3 us
    pallas_call x2, Pallas kernels, forward(): pl.pallas_call(forward_body, in_specs=[SMEM] + [VMEM] * len(operands), ou...  9.93 us
    ppermute x8, starting transfers between devices, line_plan(): across[k] = lax.ppermute(last, 'dp', CENTER)  5.78 us
  transfers between devices with their start and end apart: 37, of which 13 were waited for; matrix products, arithmetic and copies ran while one was open for 3% of the time, Pallas kernels for 32%

commit v1 on v0

--- a/solution.py
+++ b/solution.py
@@ -195,6 +195,7 @@
 ROW_GROUPS = 4
 GRAD_CHUNKS = 8
 GRAD_LEAD = 5
+SEND_LEAD = 3
 LANES = 128
 CODE_LIMIT = 32512.0
 CODE_TAIL = 16
@@ -205,6 +206,7 @@
 CENTER = ((1, 2), (2, 1))
 FROM_CENTER = ((1, 0), (2, 3))
 VMEM = pl.BlockSpec(memory_space=pltpu.VMEM)
+HBM = pl.BlockSpec(memory_space=pltpu.HBM)
 SMEM = pl.BlockSpec(memory_space=pltpu.SMEM)
 EXPONENTS = pltpu.VMEM((CODE_TAIL, LANES), jnp.float32)
 
@@ -238,8 +240,38 @@
     )(place, *[resident(x) for x in operands])
 
 
-def own_half_body(place, own_ref, weight_ref, out_ref):
+def in_hbm(array):
+    return pltpu.with_memory_space_constraint(array, pltpu.HBM)
+
+
+def share_body(place, source, *refs):
+    out, sem = refs[-2:]
+    count = out.shape[0]
+    copy = pltpu.make_async_copy(source.at[pl.ds(place[3] * count, count)], out, sem)
+    copy.start()
+    copy.wait()
+
+
+def section_share(place, source, deps):
+    groups, width, features = source.shape
+    return pl.pallas_call(
+        share_body,
+        in_specs=[SMEM, HBM] + [VMEM] * len(deps),
+        out_specs=VMEM,
+        out_shape=pltpu.VMEM((groups // 2, width, features), source.dtype),
+        scratch_shapes=[pltpu.SemaphoreType.DMA(())],
+        compiler_params=params(),
+        cost_estimate=SHORT,
+        name="section_share",
+    )(place, in_hbm(source), *[resident(x) for x in deps])
+
+
+def own_half_body(place, source, weight_ref, *refs):
+    own_ref, out_ref, sem = refs[-3:]
     groups, width, features = own_ref.shape
+    copy = pltpu.make_async_copy(source, own_ref, sem)
+    copy.start()
+    copy.wait()
     at = pl.multiple_of(place[0] * features, features)
     for first in range(0, groups, ROW_GROUPS):
         part = slice(first, first + ROW_GROUPS)
@@ -252,16 +284,22 @@
             out_ref[part, :, block] = pre.reshape(-1, width, COLUMN_BLOCK)
 
 
-def own_half(place, own, weight, deps):
-    groups, width, _ = own.shape
-    return vmem_call(
+def own_half(place, source, weight, deps):
+    groups, width, _ = source.shape
+    operands = [weight] + deps
+    return pl.pallas_call(
         own_half_body,
-        place,
-        [own, weight],
-        [((groups, width, weight.shape[1]), jnp.float32)],
-        "own_half",
-        deps,
-    )[0]
+        in_specs=[SMEM, HBM] + [VMEM] * len(operands),
+        out_specs=[VMEM, VMEM],
+        out_shape=[
+            pltpu.VMEM(source.shape, source.dtype),
+            pltpu.VMEM((groups, width, weight.shape[1]), jnp.float32),
+        ],
+        scratch_shapes=[pltpu.SemaphoreType.DMA(())],
+        compiler_params=params(),
+        cost_estimate=SHORT,
+        name="own_half",
+    )(place, in_hbm(source), *[resident(x) for x in operands])
 
 
 def forward_body(place, pre_ref, got_ref, rest_ref, weight_ref, head_ref, *refs):
@@ -611,16 +649,16 @@
 def pipeline_order(count, lead):
     order = [("grad", k) for k in range(min(lead, count))]
     ahead = len(order)
-    for k in range(count + 3):
+    for k in range(count + 2):
         if k < count:
             order.append(("partial", k))
             while ahead < min(count, lead + 2 * (k + 1)):
                 order.append(("grad", ahead))
                 ahead += 1
-        if 0 <= k - 3 < count:
-            order.append(("place", k - 3))
         if 0 <= k - 1 < count:
             order.append(("total", k - 1))
+        if 0 <= k - 2 < count:
+            order.append(("place", k - 2))
     return order
 
 
@@ -674,11 +712,8 @@
 
     offline_groups = offline_count // 2
     offline_rows = offline_obs.reshape(offline_groups, 2 * step_count, features)
-    own = [online_obs, offline_rows]
-    halves = [
-        lax.dynamic_slice_in_dim(x, section * (x.shape[0] // 2), x.shape[0] // 2, axis=0)
-        for x in own
-    ]
+    halves = [section_share(place, online_obs, [])]
+    halves.append(section_share(place, offline_rows, [halves[0]]))
 
     policy_rows = jnp.where(section == 1, policy_head.T, 0)
     value_row = jnp.where(section == 0, value_head[None], 0)
@@ -707,8 +742,8 @@
 
     got = [lax.ppermute(half, "mp", SWAP) for half in halves]
     early = halves + [back_head, forward_head, length_row] + offline_terms
-    pre_online = own_half(place, online_obs, weight, early)
-    pre_offline = own_half(place, offline_rows, weight, [pre_online])
+    own_online, pre_online = own_half(place, online_obs, weight, early)
+    own_offline, pre_offline = own_half(place, offline_rows, weight, [pre_online])
     rests = [lax.ppermute(after(got[0], pre_offline), "section", SWAP)]
     online_slope, online_part = forward(
         place, pre_online, got[0], rests[0], weight, forward_head, []
@@ -753,7 +788,7 @@
         [dz_offline],
     )
 
-    own_x = [(online_obs, 0, None), (offline_rows, 1, None)]
+    own_x = [(own_online, 0, None), (own_offline, 1, None)]
     other_x = []
     for which in range(2):
         other_x += [(got[which], which, 0), (rests[which], which, 1)]
@@ -773,13 +808,17 @@
                 columns,
                 [last],
             )
-            inward[k] = lax.ppermute(last, "dp", TO_CENTER)
+            if k < SEND_LEAD:
+                inward[k] = lax.ppermute(last, "dp", TO_CENTER)
         elif kind == "partial":
             last = partial[k] = add_chunk(place, messages[k], inward[k], lane_blocks, [last])
             across[k] = lax.ppermute(last, "dp", CENTER)
         elif kind == "total":
             last = total[k] = add_chunk(place, partial[k], across[k], lane_blocks, [last])
             outward[k] = lax.ppermute(last, "dp", FROM_CENTER)
+            ahead = k + SEND_LEAD
+            if ahead < GRAD_CHUNKS:
+                inward[ahead] = lax.ppermute(after(messages[ahead], last), "dp", TO_CENTER)
         else:
             result, last = place_chunk(
                 place,

time: 215 us -> 205 us (0.953)
  local copies, waits for them, and re-layouts: 10.2 us -> 4.85 us
  starting transfers between devices: 70.4 us -> 67.7 us
  waiting for transfers between devices: 55.6 us -> 53.4 us
    ppermute x8 -> x3, starting transfers between devices: 40.6 us -> 10.7 us  [line_plan(): inward[k] = lax.ppermute(last, 'dp', TO_CENTER)]
    ppermute x0 -> x5, starting transfers between devices: none -> 26.4 us  [line_plan(): inward[ahead] = lax.ppermute(after(messages[ahead], last), 'dp', TO_CENTER)]
    pallas_call x0 -> x4, Pallas kernels: none -> 12.7 us  [the longest x2 9.18 us: own_half(): pl.pallas_call(own_half_body, in_specs=[SMEM, HBM] + [VMEM] * len(operand...]
    pallas_call x29 -> x27, Pallas kernels: 51.4 us -> 41.1 us  [vmem_call(): pl.pallas_call(run, in_specs=[SMEM] + [VMEM] * len(operands), out_specs=[...]
    dynamic_slice x2 -> x0, local copies, waits for them, and re-layouts: 3.9 us -> none  [line_plan(): lax.dynamic_slice_in_dim(x, section * (x.shape[0] // 2), x.shape[0] // 2,...]
    reshape x4, local copies, waits for them, and re-layouts: 3.05 us -> 0.3 us  [line_plan(): x.reshape(lanes)]
  transfers between devices with their start and end apart: 37 -> 37, of which waited for: 13 -> 13; matrix products, arithmetic and copies ran while one was open for 3% -> 0% of each run, Pallas kernels for 32% -> 34%
where the time goes in v1:
time: 205 us; the launch traced here: 204 us
  Pallas kernels  77.3 us (38%)
  starting transfers between devices  67.7 us (33%)
  waiting for transfers between devices  53.4 us (26%)
  local copies, waits for them, and re-layouts  4.85 us (2%)
    pallas_call x27, Pallas kernels, vmem_call(): pl.pallas_call(run, in_specs=[SMEM] + [VMEM] * len(operands), out_specs=[...  41.1 us
    ppermute x5, starting transfers between devices, line_plan(): inward[ahead] = lax.ppermute(after(messages[ahead], last), 'dp', TO_CENTER)  26.4 us
    ppermute x2, waiting for transfers between devices, line_plan(): got = [lax.ppermute(half, 'mp', SWAP) for half in halves]  23 us
    ppermute x8, waiting for transfers between devices, line_plan(): outward[k] = lax.ppermute(last, 'dp', FROM_CENTER)  22.6 us
    pallas_call x8, Pallas kernels, place_chunk(): pl.pallas_call(functools.partial(place_body, hidden_count // LANES, rows,...  14.3 us
    ppermute x3, starting transfers between devices, line_plan(): inward[k] = lax.ppermute(last, 'dp', TO_CENTER)  10.7 us
    ppermute x8, starting transfers between devices, line_plan(): outward[k] = lax.ppermute(last, 'dp', FROM_CENTER)  10.3 us
    pallas_call x2, Pallas kernels, own_half(): pl.pallas_call(own_half_body, in_specs=[SMEM, HBM] + [VMEM] * len(operand...  9.18 us
  transfers between devices with their start and end apart: 37, of which 13 were waited for; matrix products, arithmetic and copies ran while one was open for 0% of the time, Pallas kernels for 34%

profile of v1, /device:TPU:0, one launch (start us, length us, event | category | flops | bytes accessed | tf_op | source)
XLA Modules:
  0.0 204.4 jit_solution(14758234059867123526)
XLA Ops:
  0.1 2.0 section_share.2.refs_0_
  2.1 3.0 %collective-permute-start = (bf16[8,96,1024]{2,1,0:T(8,128)(2,1)S(1)}, bf16[8,96,1024]{2,1,0:T(8,128)(2,1)S(1)}, u32[]{:S(2)}, u32[]{:S(2)}) collective-permute-start(bf16[8,96,1024]{2,1,0:T(8,128)(2,1)S(1)} %section_share.2.refs_0_), channel_id=1, source_target_pairs={{0,2},{2,0},{1,3},{3,1},{4,6},{6,4},{5,7},{7,5},{8,10},{10,8},{9,1... | collective-permute-start | bytes 4718600 | tf_op jit(solution)/shard_map/ppermute | solution.py:743
  8.5 2.2 %copy-done = bf16[1,2048,1024]{2,1,0:T(8,128)(2,1)S(1)} copy-done((bf16[1,2048,1024]{2,1,0:T(8,128)(2,1)S(1)}, bf16[1,2048,1024]{2,1,0:T(8,128)(2,1)}, u32[]{:S(2)}) %copy-start) | copy-done | bytes 4194328
  11.7 6.1 %own_half.2 = (bf16[16,96,1024]{2,1,0:T(8,128)(2,1)S(1)}, f32[16,96,1024]{2,1,0:T(8,128)S(1)}) custom-call(s32[4]{0:T(128)S(1)} %pad_add_fusion.place.place_ref, bf16[16,96,1024]{2,1,0:T(8,128)(2,1)} %source.3, bf16[2048,1024]{1,0:T(8,128)(2,1)S(1)} %bitcast.11, bf16[8,96,1024]{2,1,0:T(8,128)(2,1)S(1)} %section_share.2.refs_0_, ...), custom_call_target="tpu_custom_call" | custom-call | flops 1 | bytes 1 | tf_op jit(solution)/shard_map/own_half/pallas_call | solution.py:290
  17.9 3.0 %own_half.3 = (bf16[4,128,1024]{2,1,0:T(8,128)(2,1)S(1)}, f32[4,128,1024]{2,1,0:T(8,128)S(1)}) custom-call(s32[4]{0:T(128)S(1)} %pad_add_fusion.place.place_ref, bf16[4,128,1024]{2,1,0:T(8,128)(2,1)} %bitcast.16, bf16[2048,1024]{1,0:T(8,128)(2,1)S(1)} %bitcast.12, f32[16,96,1024]{2,1,0:T(8,128)S(1)} %get-tuple-element.38.refs_0_.pre_ref), custom_call_target="tpu_custom_call" | custom-call | flops 1 | bytes 1 | tf_op jit(solution)/shard_map/own_half/pallas_call | solution.py:290
  20.9 18.6 %collective-permute-done.got_ref.refs_0_ = bf16[8,96,1024]{2,1,0:T(8,128)(2,1)S(1)} collective-permute-done((bf16[8,96,1024]{2,1,0:T(8,128)(2,1)S(1)}, bf16[8,96,1024]{2,1,0:T(8,128)(2,1)S(1)}, u32[]{:S(2)}, u32[]{:S(2)}) %collective-permute-start) | collective-permute-done | bytes 1572896 | tf_op jit(solution)/shard_map/ppermute | solution.py:743
  42.9 6.5 %forward_rows.2 = (f32[16,96,1024]{2,1,0:T(8,128)S(1)}, f32[16,24,96]{2,1,0:T(8,128)S(1)}) custom-call(s32[4]{0:T(128)S(1)} %pad_add_fusion.place.place_ref, f32[16,96,1024]{2,1,0:T(8,128)S(1)} %get-tuple-element.38.refs_0_.pre_ref, bf16[8,96,1024]{2,1,0:T(8,128)(2,1)S(1)} %collective-permute-done.got_ref.refs_0_, ...), custom_call_target="tpu_custom_call", output_to_operand_aliasing={{0}: (1, {})} | custom-call | flops 1 | bytes 1 | tf_op jit(solution)/shard_map/forward_rows/pallas_call | solution.py:342
  49.4 4.4 %collective-permute-done.2.got_ref.refs_2_ = bf16[2,128,1024]{2,1,0:T(8,128)(2,1)S(1)} collective-permute-done((bf16[2,128,1024]{2,1,0:T(8,128)(2,1)S(1)}, bf16[2,128,1024]{2,1,0:T(8,128)(2,1)S(1)}, u32[]{:S(2)}, u32[]{:S(2)}) %collective-permute-start.2) | collective-permute-done | bytes 524320 | tf_op jit(solution)/shard_map/ppermute | solution.py:743
  55.8 2.7 %forward_rows.3 = (f32[4,128,1024]{2,1,0:T(8,128)S(1)}, f32[4,24,128]{2,1,0:T(8,128)S(1)}) custom-call(s32[4]{0:T(128)S(1)} %pad_add_fusion.place.place_ref, f32[4,128,1024]{2,1,0:T(8,128)S(1)} %get-tuple-element.39.pre_ref, bf16[2,128,1024]{2,1,0:T(8,128)(2,1)S(1)} %collective-permute-done.2.got_ref.refs_2_, ...), custom_call_target="tpu_custom_call", output_to_operand_aliasing={{0}: (1, {})} | custom-call | flops 1 | bytes 1 | tf_op jit(solution)/shard_map/forward_rows/pallas_call | solution.py:342
  64.8 1.9 collective-permute-start.10
  66.7 2.6 %collective-permute-start.9 = (f32[72,96]{1,0:T(8,128)S(1)}, f32[72,96]{1,0:T(8,128)S(1)}, u32[]{:S(2)}, u32[]{:S(2)}) collective-permute-start(f32[72,96]{1,0:T(8,128)S(1)} %get-tuple-element.45.refs_11_.refs_0_), channel_id=1, source_target_pairs={{0,8},{4,12},{8,0},{12,4},{1,9},{5,13},{9,1},{13,5},{2,10},{6,14},... | collective-permute-start | bytes 82952 | tf_op jit(solution)/shard_map/ppermute | solution.py:781
  74.9 2.3 %grad_chunk.8.refs_4_.refs_0_ = s16[2064,128]{1,0:T(8,128)(2,1)S(1)} custom-call(s32[4]{0:T(128)S(1)} %pad_add_fusion.place.place_ref, bf16[16,96,1024]{2,1,0:T(8,128)(2,1)S(1)} %get-tuple-element.49.refs_0_, bf16[4,128,1024]{2,1,0:T(8,128)(2,1)S(1)} %get-tuple-element.50.refs_1_, bf16[16,96,1024]{2,1,0:T(8,128)(2,1)S(1)} %online_back.1.refs_2_.refs_4_, ...), custom_call_target="tpu_custom_call" | custom-call | flops 1 | bytes 1 | tf_op jit(solution)/shard_map/grad_chunk/pallas_call | solution.py:231
  77.2 2.3 %collective-permute-start.14 = (s16[2064,128]{1,0:T(8,128)(2,1)S(1)}, s16[2064,128]{1,0:T(8,128)(2,1)S(1)}, u32[]{:S(2)}, u32[]{:S(2)}) collective-permute-start(s16[2064,128]{1,0:T(8,128)(2,1)S(1)} %grad_chunk.8.refs_4_.refs_0_), channel_id=1, source_target_pairs={{0,4},{12,8},{1,5},{13,9},{2,6},{14,10},{3,7},{15,11},{16,20},{28,... | collective-permute-start | bytes 1585160 | tf_op jit(solution)/shard_map/ppermute | solution.py:812
  79.5 2.3 %grad_chunk.9.refs_4_.refs_0_ = s16[2064,128]{1,0:T(8,128)(2,1)S(1)} custom-call(s32[4]{0:T(128)S(1)} %pad_add_fusion.place.place_ref, bf16[16,96,1024]{2,1,0:T(8,128)(2,1)S(1)} %get-tuple-element.49.refs_0_, bf16[4,128,1024]{2,1,0:T(8,128)(2,1)S(1)} %get-tuple-element.50.refs_1_, bf16[16,96,1024]{2,1,0:T(8,128)(2,1)S(1)} %online_back.1.refs_2_.refs_4_, ...), custom_call_target="tpu_custom_call" | custom-call | flops 1 | bytes 1 | tf_op jit(solution)/shard_map/grad_chunk/pallas_call | solution.py:231
  83.2 2.4 %grad_chunk.10.refs_4_.refs_0_ = s16[2064,128]{1,0:T(8,128)(2,1)S(1)} custom-call(s32[4]{0:T(128)S(1)} %pad_add_fusion.place.place_ref, bf16[16,96,1024]{2,1,0:T(8,128)(2,1)S(1)} %get-tuple-element.49.refs_0_, bf16[4,128,1024]{2,1,0:T(8,128)(2,1)S(1)} %get-tuple-element.50.refs_1_, bf16[16,96,1024]{2,1,0:T(8,128)(2,1)S(1)} %online_back.1.refs_2_.refs_4_, ...), custom_call_target="tpu_custom_call" | custom-call | flops 1 | bytes 1 | tf_op jit(solution)/shard_map/grad_chunk/pallas_call | solution.py:231
  85.5 2.4 %grad_chunk.11.refs_6_.refs_0_ = s16[2064,128]{1,0:T(8,128)(2,1)S(1)} custom-call(s32[4]{0:T(128)S(1)} %pad_add_fusion.place.place_ref, bf16[16,96,1024]{2,1,0:T(8,128)(2,1)S(1)} %get-tuple-element.49.refs_0_, bf16[4,128,1024]{2,1,0:T(8,128)(2,1)S(1)} %get-tuple-element.50.refs_1_, bf16[16,96,1024]{2,1,0:T(8,128)(2,1)S(1)} %online_back.1.refs_2_.refs_4_, ...), custom_call_target="tpu_custom_call" | custom-call | flops 1 | bytes 1 | tf_op jit(solution)/shard_map/grad_chunk/pallas_call | solution.py:231
  87.9 2.3 %grad_chunk.12.refs_2_.refs_0_ = s16[2064,128]{1,0:T(8,128)(2,1)S(1)} custom-call(s32[4]{0:T(128)S(1)} %pad_add_fusion.place.place_ref, bf16[8,96,1024]{2,1,0:T(8,128)(2,1)S(1)} %collective-permute-done.got_ref.refs_0_, bf16[8,96,1024]{2,1,0:T(8,128)(2,1)S(1)} %collective-permute-done.1.rest_ref.refs_1_, ...), custom_call_target="tpu_custom_call" | custom-call | flops 1 | bytes 1 | tf_op jit(solution)/shard_map/grad_chunk/pallas_call | solution.py:231
  93.8 7.1 %collective-permute-start.16 = (s16[2064,128]{1,0:T(8,128)(2,1)S(1)}, s16[2064,128]{1,0:T(8,128)(2,1)S(1)}, u32[]{:S(2)}, u32[]{:S(2)}) collective-permute-start(s16[2064,128]{1,0:T(8,128)(2,1)S(1)} %grad_chunk.10.refs_4_.refs_0_), channel_id=1, source_target_pairs={{0,4},{12,8},{1,5},{13,9},{2,6},{14,10},{3,7},{15,11},{16,20},{28,... | collective-permute-start | bytes 1585160 | tf_op jit(solution)/shard_map/ppermute | solution.py:812
  100.9 2.3 %grad_chunk.13.refs_6_.refs_0_ = s16[2064,128]{1,0:T(8,128)(2,1)S(1)} custom-call(s32[4]{0:T(128)S(1)} %pad_add_fusion.place.place_ref, bf16[8,96,1024]{2,1,0:T(8,128)(2,1)S(1)} %collective-permute-done.got_ref.refs_0_, bf16[8,96,1024]{2,1,0:T(8,128)(2,1)S(1)} %collective-permute-done.1.rest_ref.refs_1_, ...), custom_call_target="tpu_custom_call" | custom-call | flops 1 | bytes 1 | tf_op jit(solution)/shard_map/grad_chunk/pallas_call | solution.py:231
  103.3 2.4 %grad_chunk.14.refs_2_.refs_0_ = s16[2064,128]{1,0:T(8,128)(2,1)S(1)} custom-call(s32[4]{0:T(128)S(1)} %pad_add_fusion.place.place_ref, bf16[8,96,1024]{2,1,0:T(8,128)(2,1)S(1)} %collective-permute-done.got_ref.refs_0_, bf16[8,96,1024]{2,1,0:T(8,128)(2,1)S(1)} %collective-permute-done.1.rest_ref.refs_1_, ...), custom_call_target="tpu_custom_call" | custom-call | flops 1 | bytes 1 | tf_op jit(solution)/shard_map/grad_chunk/pallas_call | solution.py:231
  107.5 2.3 %grad_chunk.15.refs_2_.refs_0_ = s16[2064,128]{1,0:T(8,128)(2,1)S(1)} custom-call(s32[4]{0:T(128)S(1)} %pad_add_fusion.place.place_ref, bf16[8,96,1024]{2,1,0:T(8,128)(2,1)S(1)} %collective-permute-done.got_ref.refs_0_, bf16[8,96,1024]{2,1,0:T(8,128)(2,1)S(1)} %collective-permute-done.1.rest_ref.refs_1_, ...), custom_call_target="tpu_custom_call" | custom-call | flops 1 | bytes 1 | tf_op jit(solution)/shard_map/grad_chunk/pallas_call | solution.py:231
  112.3 4.8 %collective-permute-start.21 = (s16[2064,128]{1,0:T(8,128)(2,1)S(1)}, s16[2064,128]{1,0:T(8,128)(2,1)S(1)}, u32[]{:S(2)}, u32[]{:S(2)}) collective-permute-start(s16[2064,128]{1,0:T(8,128)(2,1)S(1)} %grad_chunk.11.refs_6_.refs_0_), channel_id=1, source_target_pairs={{0,4},{12,8},{1,5},{13,9},{2,6},{14,10},{3,7},{15,11},{16,20},{28,... | collective-permute-start | bytes 1585160 | tf_op jit(solution)/shard_map/ppermute | solution.py:821
  121.4 4.6 %collective-permute-start.18 = (s16[2064,128]{1,0:T(8,128)(2,1)S(1)}, s16[2064,128]{1,0:T(8,128)(2,1)S(1)}, u32[]{:S(2)}, u32[]{:S(2)}) collective-permute-start(s16[2064,128]{1,0:T(8,128)(2,1)S(1)} %grad_chunk.12.refs_2_.refs_0_), channel_id=1, source_target_pairs={{0,4},{12,8},{1,5},{13,9},{2,6},{14,10},{3,7},{15,11},{16,20},{28,... | collective-permute-start | bytes 1585160 | tf_op jit(solution)/shard_map/ppermute | solution.py:821
  132.1 5.7 %collective-permute-start.24 = (s16[2064,128]{1,0:T(8,128)(2,1)S(1)}, s16[2064,128]{1,0:T(8,128)(2,1)S(1)}, u32[]{:S(2)}, u32[]{:S(2)}) collective-permute-start(s16[2064,128]{1,0:T(8,128)(2,1)S(1)} %grad_chunk.13.refs_6_.refs_0_), channel_id=1, source_target_pairs={{0,4},{12,8},{1,5},{13,9},{2,6},{14,10},{3,7},{15,11},{16,20},{28,... | collective-permute-start | bytes 1585160 | tf_op jit(solution)/shard_map/ppermute | solution.py:821
  143.8 5.3 %collective-permute-start.30 = (s16[2064,128]{1,0:T(8,128)(2,1)S(1)}, s16[2064,128]{1,0:T(8,128)(2,1)S(1)}, u32[]{:S(2)}, u32[]{:S(2)}) collective-permute-start(s16[2064,128]{1,0:T(8,128)(2,1)S(1)} %grad_chunk.14.refs_2_.refs_0_), channel_id=1, source_target_pairs={{0,4},{12,8},{1,5},{13,9},{2,6},{14,10},{3,7},{15,11},{16,20},{28,... | collective-permute-start | bytes 1585160 | tf_op jit(solution)/shard_map/ppermute | solution.py:821
  155.2 6.1 %collective-permute-start.27 = (s16[2064,128]{1,0:T(8,128)(2,1)S(1)}, s16[2064,128]{1,0:T(8,128)(2,1)S(1)}, u32[]{:S(2)}, u32[]{:S(2)}) collective-permute-start(s16[2064,128]{1,0:T(8,128)(2,1)S(1)} %grad_chunk.15.refs_2_.refs_0_), channel_id=1, source_target_pairs={{0,4},{12,8},{1,5},{13,9},{2,6},{14,10},{3,7},{15,11},{16,20},{28,... | collective-permute-start | bytes 1585160 | tf_op jit(solution)/shard_map/ppermute | solution.py:821
  161.3 1.9 place_chunk.11
  167.5 3.7 %collective-permute-done.28.received = s16[2064,128]{1,0:T(8,128)(2,1)S(1)} collective-permute-done((s16[2064,128]{1,0:T(8,128)(2,1)S(1)}, s16[2064,128]{1,0:T(8,128)(2,1)S(1)}, u32[]{:S(2)}, u32[]{:S(2)}) %collective-permute-start.28) | collective-permute-done | bytes 528416 | tf_op jit(solution)/shard_map/ppermute | solution.py:818
  177.3 5.3 %collective-permute-done.33.received = s16[2064,128]{1,0:T(8,128)(2,1)S(1)} collective-permute-done((s16[2064,128]{1,0:T(8,128)(2,1)S(1)}, s16[2064,128]{1,0:T(8,128)(2,1)S(1)}, u32[]{:S(2)}, u32[]{:S(2)}) %collective-permute-start.33) | collective-permute-done | bytes 528416 | tf_op jit(solution)/shard_map/ppermute | solution.py:818
  186.7 6.9 %collective-permute-done.36.received = s16[2064,128]{1,0:T(8,128)(2,1)S(1)} collective-permute-done((s16[2064,128]{1,0:T(8,128)(2,1)S(1)}, s16[2064,128]{1,0:T(8,128)(2,1)S(1)}, u32[]{:S(2)}, u32[]{:S(2)}) %collective-permute-start.36) | collective-permute-done | bytes 528416 | tf_op jit(solution)/shard_map/ppermute | solution.py:818
  195.3 6.7 %collective-permute-done.35.received = s16[2064,128]{1,0:T(8,128)(2,1)S(1)} collective-permute-done((s16[2064,128]{1,0:T(8,128)(2,1)S(1)}, s16[2064,128]{1,0:T(8,128)(2,1)S(1)}, u32[]{:S(2)}, u32[]{:S(2)}) %collective-permute-start.35) | collective-permute-done | bytes 528416 | tf_op jit(solution)/shard_map/ppermute | solution.py:818
  202.0 2.3 %place_chunk.15 = (f32[2048,1024]{1,0:T(8,128)}, f32[8,128]{1,0:T(8,128)}) custom-call(s32[4]{0:T(128)S(1)} %pad_add_fusion.place.place_ref, s16[2064,128]{1,0:T(8,128)(2,1)S(1)} %add_chunk.31.refs_0_.total, s16[2064,128]{1,0:T(8,128)(2,1)S(1)} %collective-permute-done.35.received, ...), custom_call_target="tpu_custom_call", output_to_operand_aliasing={{0}: (4, {})} | custom-call | flops 1 | bytes 1 | tf_op jit(solution)/shard_map/place_chunk/pallas_call | solution.py:627
  (134 shorter events, 69.1 us)
Async XLA Ops:
  2.1 37.4 %collective-permute-start = (bf16[8,96,1024]{2,1,0:T(8,128)(2,1)S(1)}, bf16[8,96,1024]{2,1,0:T(8,128)(2,1)S(1)}, u32[]{:S(2)}, u32[]{:S(2)}) collective-permute-start(bf16[8,96,1024]{2,1,0:T(8,128)(2,1)S(1)} %section_share.2.refs_0_), channel_id=1, source_target_pairs={{0,2},{2,0},{1,3},{3,1},{4,6},{6,4},{5,7},{7,5},{8,10},{10,8},{9,1... | collective-permute-start | bytes 4718600 | tf_op jit(solution)/shard_map/ppermute | solution.py:743
  39.5 14.3 %collective-permute-start.2 = (bf16[2,128,1024]{2,1,0:T(8,128)(2,1)S(1)}, bf16[2,128,1024]{2,1,0:T(8,128)(2,1)S(1)}, u32[]{:S(2)}, u32[]{:S(2)}) collective-permute-start(bf16[2,128,1024]{2,1,0:T(8,128)(2,1)S(1)} %copy-done.3), channel_id=1, source_target_pairs={{0,2},{2,0},{1,3},{3,1},{4,6},{6,4},{5,7},{7,5},{8,10},{10,8},{9,1... | collective-permute-start | bytes 1572872 | tf_op jit(solution)/shard_map/ppermute | solution.py:743
  53.9 7.3 %collective-permute-start.5 = (f32[16,24,96]{2,1,0:T(8,128)S(1)}, f32[16,24,96]{2,1,0:T(8,128)S(1)}, u32[]{:S(2)}, u32[]{:S(2)}) collective-permute-start(f32[16,24,96]{2,1,0:T(8,128)S(1)} %get-tuple-element.41.refs_0_), channel_id=1, source_target_pairs={{0,2},{2,0},{1,3},{3,1},{4,6},{6,4},{5,7},{7,5},{8,10},{10,8},{9,1... | collective-permute-start | bytes 442376 | tf_op jit(solution)/shard_map/ppermute | solution.py:670
  58.5 4.1 %collective-permute-start.6 = (f32[4,24,128]{2,1,0:T(8,128)S(1)}, f32[4,24,128]{2,1,0:T(8,128)S(1)}, u32[]{:S(2)}, u32[]{:S(2)}) collective-permute-start(f32[4,24,128]{2,1,0:T(8,128)S(1)} %get-tuple-element.43.refs_9_.refs_0_), channel_id=1, source_target_pairs={{0,2},{2,0},{1,3},{3,1},{4,6},{6,4},{5,7},{7,5},{8,10},{10,8},{9,1... | collective-permute-start | bytes 147464 | tf_op jit(solution)/shard_map/ppermute | solution.py:670
  62.6 8.0 %collective-permute-start.11 = (f32[4,24,128]{2,1,0:T(8,128)S(1)}, f32[4,24,128]{2,1,0:T(8,128)S(1)}, u32[]{:S(2)}, u32[]{:S(2)}) collective-permute-start(f32[4,24,128]{2,1,0:T(8,128)S(1)} %get-tuple-element.43.refs_9_.refs_0_), channel_id=1, source_target_pairs={{0,1},{1,0},{2,3},{3,2},{4,5},{5,4},{6,7},{7,6},{8,9},{9,8},{10,11... | collective-permute-start | bytes 147464 | tf_op jit(solution)/shard_map/ppermute | solution.py:673
  63.1 7.5 %collective-permute-start.12 = (f32[4,24,128]{2,1,0:T(8,128)S(1)}, f32[4,24,128]{2,1,0:T(8,128)S(1)}, u32[]{:S(2)}, u32[]{:S(2)}) collective-permute-start(f32[4,24,128]{2,1,0:T(8,128)S(1)} %collective-permute-done.6.refs_2_), channel_id=1, source_target_pairs={{0,1},{1,0},{2,3},{3,2},{4,5},{5,4},{6,7},{7,6},{8,9},{9,8},{10,11... | collective-permute-start | bytes 147464 | tf_op jit(solution)/shard_map/ppermute | solution.py:675
  64.8 7.4 %collective-permute-start.10 = (f32[72,96]{1,0:T(8,128)S(1)}, f32[72,96]{1,0:T(8,128)S(1)}, u32[]{:S(2)}, u32[]{:S(2)}) collective-permute-start(f32[72,96]{1,0:T(8,128)S(1)} %get-tuple-element.45.refs_11_.refs_0_), channel_id=1, source_target_pairs={{0,4},{4,8},{8,12},{12,0},{1,5},{5,9},{9,13},{13,1},{2,6},{6,10},{... | collective-permute-start | bytes 82952 | tf_op jit(solution)/shard_map/ppermute | solution.py:781
  66.7 5.5 %collective-permute-start.9 = (f32[72,96]{1,0:T(8,128)S(1)}, f32[72,96]{1,0:T(8,128)S(1)}, u32[]{:S(2)}, u32[]{:S(2)}) collective-permute-start(f32[72,96]{1,0:T(8,128)S(1)} %get-tuple-element.45.refs_11_.refs_0_), channel_id=1, source_target_pairs={{0,8},{4,12},{8,0},{12,4},{1,9},{5,13},{9,1},{13,5},{2,10},{6,14},... | collective-permute-start | bytes 82952 | tf_op jit(solution)/shard_map/ppermute | solution.py:781
  77.2 14.7 %collective-permute-start.14 = (s16[2064,128]{1,0:T(8,128)(2,1)S(1)}, s16[2064,128]{1,0:T(8,128)(2,1)S(1)}, u32[]{:S(2)}, u32[]{:S(2)}) collective-permute-start(s16[2064,128]{1,0:T(8,128)(2,1)S(1)} %grad_chunk.8.refs_4_.refs_0_), channel_id=1, source_target_pairs={{0,4},{12,8},{1,5},{13,9},{2,6},{14,10},{3,7},{15,11},{16,20},{28,... | collective-permute-start | bytes 1585160 | tf_op jit(solution)/shard_map/ppermute | solution.py:812
  81.9 23.8 %collective-permute-start.13 = (s16[2064,128]{1,0:T(8,128)(2,1)S(1)}, s16[2064,128]{1,0:T(8,128)(2,1)S(1)}, u32[]{:S(2)}, u32[]{:S(2)}) collective-permute-start(s16[2064,128]{1,0:T(8,128)(2,1)S(1)} %grad_chunk.9.refs_4_.refs_0_), channel_id=1, source_target_pairs={{0,4},{12,8},{1,5},{13,9},{2,6},{14,10},{3,7},{15,11},{16,20},{28,... | collective-permute-start | bytes 1585160 | tf_op jit(solution)/shard_map/ppermute | solution.py:812
  93.1 16.8 %collective-permute-start.17 = (s16[2064,128]{1,0:T(8,128)(2,1)S(1)}, s16[2064,128]{1,0:T(8,128)(2,1)S(1)}, u32[]{:S(2)}, u32[]{:S(2)}) collective-permute-start(s16[2064,128]{1,0:T(8,128)(2,1)S(1)} %add_chunk.16.refs_6_.refs_0_), channel_id=1, source_target_pairs={{4,8},{8,4},{5,9},{9,5},{6,10},{10,6},{7,11},{11,7},{20,24},{24,20... | collective-permute-start | bytes 1585160 | tf_op jit(solution)/shard_map/ppermute | solution.py:815
  93.8 23.3 %collective-permute-start.16 = (s16[2064,128]{1,0:T(8,128)(2,1)S(1)}, s16[2064,128]{1,0:T(8,128)(2,1)S(1)}, u32[]{:S(2)}, u32[]{:S(2)}) collective-permute-start(s16[2064,128]{1,0:T(8,128)(2,1)S(1)} %grad_chunk.10.refs_4_.refs_0_), channel_id=1, source_target_pairs={{0,4},{12,8},{1,5},{13,9},{2,6},{14,10},{3,7},{15,11},{16,20},{28,... | collective-permute-start | bytes 1585160 | tf_op jit(solution)/shard_map/ppermute | solution.py:812
  106.8 12.2 %collective-permute-start.15 = (s16[2064,128]{1,0:T(8,128)(2,1)S(1)}, s16[2064,128]{1,0:T(8,128)(2,1)S(1)}, u32[]{:S(2)}, u32[]{:S(2)}) collective-permute-start(s16[2064,128]{1,0:T(8,128)(2,1)S(1)} %add_chunk.17.refs_6_.refs_0_), channel_id=1, source_target_pairs={{4,8},{8,4},{5,9},{9,5},{6,10},{10,6},{7,11},{11,7},{20,24},{24,20... | collective-permute-start | bytes 1585160 | tf_op jit(solution)/shard_map/ppermute | solution.py:815
  111.0 15.0 %collective-permute-start.22 = (s16[2064,128]{1,0:T(8,128)(2,1)S(1)}, s16[2064,128]{1,0:T(8,128)(2,1)S(1)}, u32[]{:S(2)}, u32[]{:S(2)}) collective-permute-start(s16[2064,128]{1,0:T(8,128)(2,1)S(1)} %add_chunk.18.refs_2_.total), channel_id=1, source_target_pairs={{4,0},{8,12},{5,1},{9,13},{6,2},{10,14},{7,3},{11,15},{20,16},{24,... | collective-permute-start | bytes 1585160 | tf_op jit(solution)/shard_map/ppermute | solution.py:818
  112.3 15.4 %collective-permute-start.21 = (s16[2064,128]{1,0:T(8,128)(2,1)S(1)}, s16[2064,128]{1,0:T(8,128)(2,1)S(1)}, u32[]{:S(2)}, u32[]{:S(2)}) collective-permute-start(s16[2064,128]{1,0:T(8,128)(2,1)S(1)} %grad_chunk.11.refs_6_.refs_0_), channel_id=1, source_target_pairs={{0,4},{12,8},{1,5},{13,9},{2,6},{14,10},{3,7},{15,11},{16,20},{28,... | collective-permute-start | bytes 1585160 | tf_op jit(solution)/shard_map/ppermute | solution.py:821
  118.3 11.4 %collective-permute-start.20 = (s16[2064,128]{1,0:T(8,128)(2,1)S(1)}, s16[2064,128]{1,0:T(8,128)(2,1)S(1)}, u32[]{:S(2)}, u32[]{:S(2)}) collective-permute-start(s16[2064,128]{1,0:T(8,128)(2,1)S(1)} %add_chunk.19.refs_2_.refs_0_), channel_id=1, source_target_pairs={{4,8},{8,4},{5,9},{9,5},{6,10},{10,6},{7,11},{11,7},{20,24},{24,20... | collective-permute-start | bytes 1585160 | tf_op jit(solution)/shard_map/ppermute | solution.py:815
  120.1 17.7 %collective-permute-start.19 = (s16[2064,128]{1,0:T(8,128)(2,1)S(1)}, s16[2064,128]{1,0:T(8,128)(2,1)S(1)}, u32[]{:S(2)}, u32[]{:S(2)}) collective-permute-start(s16[2064,128]{1,0:T(8,128)(2,1)S(1)} %add_chunk.20.refs_0_.total), channel_id=1, source_target_pairs={{4,0},{8,12},{5,1},{9,13},{6,2},{10,14},{7,3},{11,15},{20,16},{24,... | collective-permute-start | bytes 1585160 | tf_op jit(solution)/shard_map/ppermute | solution.py:818
  121.4 18.1 %collective-permute-start.18 = (s16[2064,128]{1,0:T(8,128)(2,1)S(1)}, s16[2064,128]{1,0:T(8,128)(2,1)S(1)}, u32[]{:S(2)}, u32[]{:S(2)}) collective-permute-start(s16[2064,128]{1,0:T(8,128)(2,1)S(1)} %grad_chunk.12.refs_2_.refs_0_), channel_id=1, source_target_pairs={{0,4},{12,8},{1,5},{13,9},{2,6},{14,10},{3,7},{15,11},{16,20},{28,... | collective-permute-start | bytes 1585160 | tf_op jit(solution)/shard_map/ppermute | solution.py:821
  128.9 12.5 %collective-permute-start.26 = (s16[2064,128]{1,0:T(8,128)(2,1)S(1)}, s16[2064,128]{1,0:T(8,128)(2,1)S(1)}, u32[]{:S(2)}, u32[]{:S(2)}) collective-permute-start(s16[2064,128]{1,0:T(8,128)(2,1)S(1)} %add_chunk.21.refs_2_.refs_0_), channel_id=1, source_target_pairs={{4,8},{8,4},{5,9},{9,5},{6,10},{10,6},{7,11},{11,7},{20,24},{24,20... | collective-permute-start | bytes 1585160 | tf_op jit(solution)/shard_map/ppermute | solution.py:815
  130.8 18.3 %collective-permute-start.25 = (s16[2064,128]{1,0:T(8,128)(2,1)S(1)}, s16[2064,128]{1,0:T(8,128)(2,1)S(1)}, u32[]{:S(2)}, u32[]{:S(2)}) collective-permute-start(s16[2064,128]{1,0:T(8,128)(2,1)S(1)} %add_chunk.22.refs_0_.total), channel_id=1, source_target_pairs={{4,0},{8,12},{5,1},{9,13},{6,2},{10,14},{7,3},{11,15},{20,16},{24,... | collective-permute-start | bytes 1585160 | tf_op jit(solution)/shard_map/ppermute | solution.py:818
  132.1 18.7 %collective-permute-start.24 = (s16[2064,128]{1,0:T(8,128)(2,1)S(1)}, s16[2064,128]{1,0:T(8,128)(2,1)S(1)}, u32[]{:S(2)}, u32[]{:S(2)}) collective-permute-start(s16[2064,128]{1,0:T(8,128)(2,1)S(1)} %grad_chunk.13.refs_6_.refs_0_), channel_id=1, source_target_pairs={{0,4},{12,8},{1,5},{13,9},{2,6},{14,10},{3,7},{15,11},{16,20},{28,... | collective-permute-start | bytes 1585160 | tf_op jit(solution)/shard_map/ppermute | solution.py:821
  140.7 12.0 %collective-permute-start.23 = (s16[2064,128]{1,0:T(8,128)(2,1)S(1)}, s16[2064,128]{1,0:T(8,128)(2,1)S(1)}, u32[]{:S(2)}, u32[]{:S(2)}) collective-permute-start(s16[2064,128]{1,0:T(8,128)(2,1)S(1)} %add_chunk.23.refs_2_.refs_0_), channel_id=1, source_target_pairs={{4,8},{8,4},{5,9},{9,5},{6,10},{10,6},{7,11},{11,7},{20,24},{24,20... | collective-permute-start | bytes 1585160 | tf_op jit(solution)/shard_map/ppermute | solution.py:815
  142.5 18.7 %collective-permute-start.31 = (s16[2064,128]{1,0:T(8,128)(2,1)S(1)}, s16[2064,128]{1,0:T(8,128)(2,1)S(1)}, u32[]{:S(2)}, u32[]{:S(2)}) collective-permute-start(s16[2064,128]{1,0:T(8,128)(2,1)S(1)} %add_chunk.24.refs_0_.total), channel_id=1, source_target_pairs={{4,0},{8,12},{5,1},{9,13},{6,2},{10,14},{7,3},{11,15},{20,16},{24,... | collective-permute-start | bytes 1585160 | tf_op jit(solution)/shard_map/ppermute | solution.py:818
  143.8 19.4 %collective-permute-start.30 = (s16[2064,128]{1,0:T(8,128)(2,1)S(1)}, s16[2064,128]{1,0:T(8,128)(2,1)S(1)}, u32[]{:S(2)}, u32[]{:S(2)}) collective-permute-start(s16[2064,128]{1,0:T(8,128)(2,1)S(1)} %grad_chunk.14.refs_2_.refs_0_), channel_id=1, source_target_pairs={{0,4},{12,8},{1,5},{13,9},{2,6},{14,10},{3,7},{15,11},{16,20},{28,... | collective-permute-start | bytes 1585160 | tf_op jit(solution)/shard_map/ppermute | solution.py:821
  152.0 13.1 %collective-permute-start.29 = (s16[2064,128]{1,0:T(8,128)(2,1)S(1)}, s16[2064,128]{1,0:T(8,128)(2,1)S(1)}, u32[]{:S(2)}, u32[]{:S(2)}) collective-permute-start(s16[2064,128]{1,0:T(8,128)(2,1)S(1)} %add_chunk.25.refs_2_.refs_0_), channel_id=1, source_target_pairs={{4,8},{8,4},{5,9},{9,5},{6,10},{10,6},{7,11},{11,7},{20,24},{24,20... | collective-permute-start | bytes 1585160 | tf_op jit(solution)/shard_map/ppermute | solution.py:815
  153.9 17.4 %collective-permute-start.28 = (s16[2064,128]{1,0:T(8,128)(2,1)S(1)}, s16[2064,128]{1,0:T(8,128)(2,1)S(1)}, u32[]{:S(2)}, u32[]{:S(2)}) collective-permute-start(s16[2064,128]{1,0:T(8,128)(2,1)S(1)} %add_chunk.26.refs_0_.total), channel_id=1, source_target_pairs={{4,0},{8,12},{5,1},{9,13},{6,2},{10,14},{7,3},{11,15},{20,16},{24,... | collective-permute-start | bytes 1585160 | tf_op jit(solution)/shard_map/ppermute | solution.py:818
  155.2 17.8 %collective-permute-start.27 = (s16[2064,128]{1,0:T(8,128)(2,1)S(1)}, s16[2064,128]{1,0:T(8,128)(2,1)S(1)}, u32[]{:S(2)}, u32[]{:S(2)}) collective-permute-start(s16[2064,128]{1,0:T(8,128)(2,1)S(1)} %grad_chunk.15.refs_2_.refs_0_), channel_id=1, source_target_pairs={{0,4},{12,8},{1,5},{13,9},{2,6},{14,10},{3,7},{15,11},{16,20},{28,... | collective-permute-start | bytes 1585160 | tf_op jit(solution)/shard_map/ppermute | solution.py:821
  164.4 10.4 %collective-permute-start.34 = (s16[2064,128]{1,0:T(8,128)(2,1)S(1)}, s16[2064,128]{1,0:T(8,128)(2,1)S(1)}, u32[]{:S(2)}, u32[]{:S(2)}) collective-permute-start(s16[2064,128]{1,0:T(8,128)(2,1)S(1)} %add_chunk.27.refs_2_.refs_0_), channel_id=1, source_target_pairs={{4,8},{8,4},{5,9},{9,5},{6,10},{10,6},{7,11},{11,7},{20,24},{24,20... | collective-permute-start | bytes 1585160 | tf_op jit(solution)/shard_map/ppermute | solution.py:815
  166.2 16.3 %collective-permute-start.33 = (s16[2064,128]{1,0:T(8,128)(2,1)S(1)}, s16[2064,128]{1,0:T(8,128)(2,1)S(1)}, u32[]{:S(2)}, u32[]{:S(2)}) collective-permute-start(s16[2064,128]{1,0:T(8,128)(2,1)S(1)} %add_chunk.28.refs_0_.total), channel_id=1, source_target_pairs={{4,0},{8,12},{5,1},{9,13},{6,2},{10,14},{7,3},{11,15},{20,16},{24,... | collective-permute-start | bytes 1585160 | tf_op jit(solution)/shard_map/ppermute | solution.py:818
  174.1 10.1 %collective-permute-start.32 = (s16[2064,128]{1,0:T(8,128)(2,1)S(1)}, s16[2064,128]{1,0:T(8,128)(2,1)S(1)}, u32[]{:S(2)}, u32[]{:S(2)}) collective-permute-start(s16[2064,128]{1,0:T(8,128)(2,1)S(1)} %add_chunk.29.refs_2_.refs_0_), channel_id=1, source_target_pairs={{4,8},{8,4},{5,9},{9,5},{6,10},{10,6},{7,11},{11,7},{20,24},{24,20... | collective-permute-start | bytes 1585160 | tf_op jit(solution)/shard_map/ppermute | solution.py:815
  176.0 17.6 %collective-permute-start.36 = (s16[2064,128]{1,0:T(8,128)(2,1)S(1)}, s16[2064,128]{1,0:T(8,128)(2,1)S(1)}, u32[]{:S(2)}, u32[]{:S(2)}) collective-permute-start(s16[2064,128]{1,0:T(8,128)(2,1)S(1)} %add_chunk.30.refs_0_.total), channel_id=1, source_target_pairs={{4,0},{8,12},{5,1},{9,13},{6,2},{10,14},{7,3},{11,15},{20,16},{24,... | collective-permute-start | bytes 1585160 | tf_op jit(solution)/shard_map/ppermute | solution.py:818
  185.4 16.6 %collective-permute-start.35 = (s16[2064,128]{1,0:T(8,128)(2,1)S(1)}, s16[2064,128]{1,0:T(8,128)(2,1)S(1)}, u32[]{:S(2)}, u32[]{:S(2)}) collective-permute-start(s16[2064,128]{1,0:T(8,128)(2,1)S(1)} %add_chunk.31.refs_0_.total), channel_id=1, source_target_pairs={{4,0},{8,12},{5,1},{9,13},{6,2},{10,14},{7,3},{11,15},{20,16},{24,... | collective-permute-start | bytes 1585160 | tf_op jit(solution)/shard_map/ppermute | solution.py:818
  (21 other events, 144.9 us)

commit v2 on v1

--- a/solution.py
+++ b/solution.py
@@ -275,13 +275,18 @@
     at = pl.multiple_of(place[0] * features, features)
     for first in range(0, groups, ROW_GROUPS):
         part = slice(first, first + ROW_GROUPS)
-        own = own_ref[part].reshape(-1, features)
-        for h in range(0, weight_ref.shape[1], COLUMN_BLOCK):
-            block = slice(h, h + COLUMN_BLOCK)
+
+        def step(h, carry, part=part):
+            block = pl.ds(pl.multiple_of(h * COLUMN_BLOCK, COLUMN_BLOCK), COLUMN_BLOCK)
             pre = jnp.dot(
-                own, weight_ref[pl.ds(at, features), block], preferred_element_type=jnp.float32
+                own_ref[part].reshape(-1, features),
+                weight_ref[pl.ds(at, features), block],
+                preferred_element_type=jnp.float32,
             )
             out_ref[part, :, block] = pre.reshape(-1, width, COLUMN_BLOCK)
+            return carry
+
+        lax.fori_loop(0, weight_ref.shape[1] // COLUMN_BLOCK, step, 0)
 
 
 def own_half(place, source, weight, deps):
@@ -358,7 +363,7 @@
 
 
 def action_terms(parts, actions, behaviour, action_count):
-    heads = parts[0] + parts[1] + (parts[2] + parts[3])
+    heads = sum(parts[1:], start=parts[0])
     row = lax.broadcasted_iota(jnp.int32, heads.shape, 0)
     is_logit = row < action_count
     logits = jnp.where(is_logit, heads, -1e30)
@@ -407,13 +412,22 @@
     dz_ref[g] = (dh * slope).astype(jnp.bfloat16)
 
 
+def chip_heads_body(place, own, other, both_ref, share_ref):
+    both_ref[...] = own[...] + other[...]
+    count = share_ref.shape[0]
+    share_ref[...] = both_ref[pl.ds(place[3] * count, count)]
+
+
 def online_heads_body(action_count, place, *refs):
-    parts = refs[:4]
-    actions, behaviour, reward, done, lengths, pack_ref, spread_ref = refs[4:]
+    both, across, far, actions, behaviour, reward, done, lengths = refs[:8]
+    pack_ref, spread_ref, other = refs[8:]
     steps = actions.shape[0]
+    half, section = steps // 2, place[3]
+    other[pl.ds(section * half, half)] = across[...]
+    other[pl.ds((1 - section) * half, half)] = far[...]
     for t in range(steps):
         value, rho, spread = action_terms(
-            [p[t] for p in parts],
+            [both[t], other[t]],
             actions[t : t + 1, :],
             behaviour[t : t + 1, :],
             action_count,
@@ -664,16 +678,6 @@
 
 def after(array, *others):
     return lax.optimization_barrier((array,) + others)[0]
-
-
-def chip_pair(part, gate=()):
-    across = lax.ppermute(part, "mp", SWAP)
-    return [
-        part,
-        lax.ppermute(part, "section", SWAP),
-        across,
-        lax.ppermute(after(across, *gate), "section", SWAP),
-    ]
 
 
 def line_plan(
@@ -748,15 +752,28 @@
     online_slope, online_part = forward(
         place, pre_online, got[0], rests[0], weight, forward_head, []
     )
-    rests.append(lax.ppermute(after(got[1], online_part), "section", SWAP))
+    both, share = vmem_call(
+        chip_heads_body,
+        place,
+        [online_part, lax.ppermute(online_part, "section", SWAP)],
+        [
+            (online_part.shape, jnp.float32),
+            ((steps // 2, HEAD_ROWS, online_count), jnp.float32),
+        ],
+        "chip_heads",
+    )
+    across_heads = lax.ppermute(share, "mp", SWAP)
+    rests.append(lax.ppermute(after(got[1], both), "section", SWAP))
     offline_slope, offline_part = forward(
-        place, pre_offline, got[1], rests[1], weight, forward_head, [online_part]
-    )
-    offline_parts = chip_pair(offline_part, [])
+        place, pre_offline, got[1], rests[1], weight, forward_head, [both]
+    )
+    across_offline = lax.ppermute(offline_part, "mp", SWAP)
+    offline_parts = [offline_part, lax.ppermute(offline_part, "section", SWAP), across_offline]
+    far_heads = lax.ppermute(after(across_heads, offline_part), "section", SWAP)
     pack, spread = vmem_call(
         functools.partial(online_heads_body, action_count),
         place,
-        chip_pair(online_part, [offline_part, offline_parts[2]])
+        [both, across_heads, far_heads]
         + [online_actions, online_behaviour, online_rewards, online_done, length_row],
         [
             ((4 * steps + 8, online_count), jnp.float32),
@@ -764,8 +781,14 @@
         ],
         "online_heads",
         [offline_part],
-    )
-
+        [pltpu.VMEM((steps, HEAD_ROWS, online_count), jnp.float32)],
+    )
+
+    blocks = [pack]
+    for hop in range(1, dp):
+        pairs = [(i, (i - hop) % dp) for i in range(dp)]
+        blocks.append(lax.ppermute(pack, "dp", pairs))
+    offline_parts.append(lax.ppermute(after(across_offline, pack), "section", SWAP))
     (dz_offline,) = vmem_call(
         functools.partial(offline_back_body, action_count, step_count, scale),
         place,
@@ -775,10 +798,6 @@
         [pack],
     )
 
-    blocks = [pack]
-    for hop in range(1, dp):
-        pairs = [(i, (i - hop) % dp) for i in range(dp)]
-        blocks.append(lax.ppermute(pack, "dp", pairs))
     (dz_online,) = vmem_call(
         functools.partial(online_back_body, action_count, scale),
         place,

time: 205 us -> 205 us (level)
  Pallas kernels: 77.3 us -> 82.5 us
  waiting for transfers between devices: 53.4 us -> 49.8 us
    ppermute x2, waiting for transfers between devices: 23 us -> 18.3 us  [line_plan(): got = [lax.ppermute(half, 'mp', SWAP) for half in halves]]
    pallas_call x2, Pallas kernels: 9.18 us -> 13 us  [own_half(): pl.pallas_call(own_half_body, in_specs=[SMEM, HBM] + [VMEM] * len(operand...]
    pallas_call x27 -> x28, Pallas kernels: 41.1 us -> 41.6 us  [vmem_call(): pl.pallas_call(run, in_specs=[SMEM] + [VMEM] * len(operands), out_specs=[...]
  transfers between devices with their start and end apart: 37 -> 37, of which waited for: 13 -> 14; matrix products, arithmetic and copies ran while one was open for 0% -> 0% of each run, Pallas kernels for 34% -> 36%
where the time goes in v2:
time: 205 us; the launch traced here: 204 us
  Pallas kernels  82.5 us (40%)
  starting transfers between devices  67.8 us (33%)
  waiting for transfers between devices  49.8 us (24%)
  local copies, waits for them, and re-layouts  3.02 us (1%)
    pallas_call x28, Pallas kernels, vmem_call(): pl.pallas_call(run, in_specs=[SMEM] + [VMEM] * len(operands), out_specs=[...  41.6 us
    ppermute x5, starting transfers between devices, line_plan(): inward[ahead] = lax.ppermute(after(messages[ahead], last), 'dp', TO_CENTER)  26.9 us
    ppermute x8, waiting for transfers between devices, line_plan(): outward[k] = lax.ppermute(last, 'dp', FROM_CENTER)  23.7 us
    ppermute x2, waiting for transfers between devices, line_plan(): got = [lax.ppermute(half, 'mp', SWAP) for half in halves]  18.3 us
    pallas_call x8, Pallas kernels, place_chunk(): pl.pallas_call(functools.partial(place_body, hidden_count // LANES, rows,...  14.3 us
    pallas_call x2, Pallas kernels, own_half(): pl.pallas_call(own_half_body, in_specs=[SMEM, HBM] + [VMEM] * len(operand...  13 us
    ppermute x3, starting transfers between devices, line_plan(): inward[k] = lax.ppermute(last, 'dp', TO_CENTER)  10.6 us
    ppermute x8, starting transfers between devices, line_plan(): outward[k] = lax.ppermute(last, 'dp', FROM_CENTER)  10.3 us
  transfers between devices with their start and end apart: 37, of which 14 were waited for; matrix products, arithmetic and copies ran while one was open for 0% of the time, Pallas kernels for 36%

profile of v2, /device:TPU:0, one launch (start us, length us, event | category | flops | bytes accessed | tf_op | source)
XLA Modules:
  0.0 204.3 jit_solution(1319220544661053480)
XLA Ops:
  0.1 2.0 section_share.2.refs_0_
  2.1 3.0 %collective-permute-start = (bf16[8,96,1024]{2,1,0:T(8,128)(2,1)S(1)}, bf16[8,96,1024]{2,1,0:T(8,128)(2,1)S(1)}, u32[]{:S(2)}, u32[]{:S(2)}) collective-permute-start(bf16[8,96,1024]{2,1,0:T(8,128)(2,1)S(1)} %section_share.2.refs_0_), channel_id=1, source_target_pairs={{0,2},{2,0},{1,3},{3,1},{4,6},{6,4},{5,7},{7,5},{8,10},{10,8},{9,1... | collective-permute-start | bytes 4718600 | tf_op jit(solution)/shard_map/ppermute | solution.py:747
  5.1 2.4 %section_share.3.refs_1_ = bf16[2,128,1024]{2,1,0:T(8,128)(2,1)} custom-call(s32[4]{0:T(128)S(1)} %pad_add_fusion.place.place_ref, bf16[4,128,1024]{2,1,0:T(8,128)(2,1)} %bitcast.15, bf16[8,96,1024]{2,1,0:T(8,128)(2,1)S(1)} %section_share.2.refs_0_), custom_call_target="tpu_custom_call" | custom-call | flops 1 | bytes 1 | tf_op jit(solution)/shard_map/section_share/pallas_call | solution.py:257
  8.5 2.2 %copy-done = bf16[1,2048,1024]{2,1,0:T(8,128)(2,1)S(1)} copy-done((bf16[1,2048,1024]{2,1,0:T(8,128)(2,1)S(1)}, bf16[1,2048,1024]{2,1,0:T(8,128)(2,1)}, u32[]{:S(2)}) %copy-start) | copy-done | bytes 4194328
  10.7 9.4 %own_half.2 = (bf16[16,96,1024]{2,1,0:T(8,128)(2,1)S(1)}, f32[16,96,1024]{2,1,0:T(8,128)S(1)}) custom-call(s32[4]{0:T(128)S(1)} %pad_add_fusion.place.place_ref, bf16[16,96,1024]{2,1,0:T(8,128)(2,1)} %source.3, bf16[2048,1024]{1,0:T(8,128)(2,1)S(1)} %bitcast.11, bf16[8,96,1024]{2,1,0:T(8,128)(2,1)S(1)} %section_share.2.refs_0_, ...), custom_call_target="tpu_custom_call" | custom-call | flops 1 | bytes 1 | tf_op jit(solution)/shard_map/own_half/pallas_call | solution.py:295
  20.2 3.6 %own_half.3 = (bf16[4,128,1024]{2,1,0:T(8,128)(2,1)S(1)}, f32[4,128,1024]{2,1,0:T(8,128)S(1)}) custom-call(s32[4]{0:T(128)S(1)} %pad_add_fusion.place.place_ref, bf16[4,128,1024]{2,1,0:T(8,128)(2,1)} %bitcast.16, bf16[2048,1024]{1,0:T(8,128)(2,1)S(1)} %bitcast.12, f32[16,96,1024]{2,1,0:T(8,128)S(1)} %get-tuple-element.41.refs_0_.pre_ref), custom_call_target="tpu_custom_call" | custom-call | flops 1 | bytes 1 | tf_op jit(solution)/shard_map/own_half/pallas_call | solution.py:295
  23.7 15.8 %collective-permute-done.got_ref.refs_0_ = bf16[8,96,1024]{2,1,0:T(8,128)(2,1)S(1)} collective-permute-done((bf16[8,96,1024]{2,1,0:T(8,128)(2,1)S(1)}, bf16[8,96,1024]{2,1,0:T(8,128)(2,1)S(1)}, u32[]{:S(2)}, u32[]{:S(2)}) %collective-permute-start) | collective-permute-done | bytes 1572896 | tf_op jit(solution)/shard_map/ppermute | solution.py:747
  42.9 6.5 %forward_rows.2 = (f32[16,96,1024]{2,1,0:T(8,128)S(1)}, f32[16,24,96]{2,1,0:T(8,128)S(1)}) custom-call(s32[4]{0:T(128)S(1)} %pad_add_fusion.place.place_ref, f32[16,96,1024]{2,1,0:T(8,128)S(1)} %get-tuple-element.41.refs_0_.pre_ref, bf16[8,96,1024]{2,1,0:T(8,128)(2,1)S(1)} %collective-permute-done.got_ref.refs_0_, ...), custom_call_target="tpu_custom_call", output_to_operand_aliasing={{0}: (1, {})} | custom-call | flops 1 | bytes 1 | tf_op jit(solution)/shard_map/forward_rows/pallas_call | solution.py:347
  51.5 2.6 %collective-permute-done.2.got_ref.refs_2_ = bf16[2,128,1024]{2,1,0:T(8,128)(2,1)S(1)} collective-permute-done((bf16[2,128,1024]{2,1,0:T(8,128)(2,1)}, bf16[2,128,1024]{2,1,0:T(8,128)(2,1)S(1)}, u32[]{:S(2)}, u32[]{:S(2)}) %collective-permute-start.2) | collective-permute-done | bytes 524320 | tf_op jit(solution)/shard_map/ppermute | solution.py:747
  56.0 2.7 %forward_rows.3 = (f32[4,128,1024]{2,1,0:T(8,128)S(1)}, f32[4,24,128]{2,1,0:T(8,128)S(1)}) custom-call(s32[4]{0:T(128)S(1)} %pad_add_fusion.place.place_ref, f32[4,128,1024]{2,1,0:T(8,128)S(1)} %get-tuple-element.42.pre_ref, bf16[2,128,1024]{2,1,0:T(8,128)(2,1)S(1)} %collective-permute-done.2.got_ref.refs_2_, ...), custom_call_target="tpu_custom_call", output_to_operand_aliasing={{0}: (1, {})} | custom-call | flops 1 | bytes 1 | tf_op jit(solution)/shard_map/forward_rows/pallas_call | solution.py:347
  65.3 2.6 %collective-permute-start.8 = (f32[72,96]{1,0:T(8,128)S(1)}, f32[72,96]{1,0:T(8,128)S(1)}, u32[]{:S(2)}, u32[]{:S(2)}) collective-permute-start(f32[72,96]{1,0:T(8,128)S(1)} %get-tuple-element.50.refs_11_.refs_0_), channel_id=1, source_target_pairs={{0,8},{4,12},{8,0},{12,4},{1,9},{5,13},{9,1},{13,5},{2,10},{6,14},... | collective-permute-start | bytes 82952 | tf_op jit(solution)/shard_map/ppermute | solution.py:790
  73.5 2.3 %grad_chunk.8.refs_4_.refs_0_ = s16[2064,128]{1,0:T(8,128)(2,1)S(1)} custom-call(s32[4]{0:T(128)S(1)} %pad_add_fusion.place.place_ref, bf16[16,96,1024]{2,1,0:T(8,128)(2,1)S(1)} %get-tuple-element.55.refs_0_, bf16[4,128,1024]{2,1,0:T(8,128)(2,1)S(1)} %get-tuple-element.56.refs_1_, bf16[16,96,1024]{2,1,0:T(8,128)(2,1)S(1)} %online_back.1.refs_2_.refs_4_, ...), custom_call_target="tpu_custom_call" | custom-call | flops 1 | bytes 1 | tf_op jit(solution)/shard_map/grad_chunk/pallas_call | solution.py:231
  75.8 2.5 %collective-permute-start.14 = (s16[2064,128]{1,0:T(8,128)(2,1)S(1)}, s16[2064,128]{1,0:T(8,128)(2,1)S(1)}, u32[]{:S(2)}, u32[]{:S(2)}) collective-permute-start(s16[2064,128]{1,0:T(8,128)(2,1)S(1)} %grad_chunk.8.refs_4_.refs_0_), channel_id=1, source_target_pairs={{0,4},{12,8},{1,5},{13,9},{2,6},{14,10},{3,7},{15,11},{16,20},{28,... | collective-permute-start | bytes 1585160 | tf_op jit(solution)/shard_map/ppermute | solution.py:831
  78.3 2.3 %grad_chunk.9.refs_4_.refs_0_ = s16[2064,128]{1,0:T(8,128)(2,1)S(1)} custom-call(s32[4]{0:T(128)S(1)} %pad_add_fusion.place.place_ref, bf16[16,96,1024]{2,1,0:T(8,128)(2,1)S(1)} %get-tuple-element.55.refs_0_, bf16[4,128,1024]{2,1,0:T(8,128)(2,1)S(1)} %get-tuple-element.56.refs_1_, bf16[16,96,1024]{2,1,0:T(8,128)(2,1)S(1)} %online_back.1.refs_2_.refs_4_, ...), custom_call_target="tpu_custom_call" | custom-call | flops 1 | bytes 1 | tf_op jit(solution)/shard_map/grad_chunk/pallas_call | solution.py:231
  82.0 2.3 %grad_chunk.10.refs_4_.refs_0_ = s16[2064,128]{1,0:T(8,128)(2,1)S(1)} custom-call(s32[4]{0:T(128)S(1)} %pad_add_fusion.place.place_ref, bf16[16,96,1024]{2,1,0:T(8,128)(2,1)S(1)} %get-tuple-element.55.refs_0_, bf16[4,128,1024]{2,1,0:T(8,128)(2,1)S(1)} %get-tuple-element.56.refs_1_, bf16[16,96,1024]{2,1,0:T(8,128)(2,1)S(1)} %online_back.1.refs_2_.refs_4_, ...), custom_call_target="tpu_custom_call" | custom-call | flops 1 | bytes 1 | tf_op jit(solution)/shard_map/grad_chunk/pallas_call | solution.py:231
  84.3 2.4 %grad_chunk.11.refs_6_.refs_0_ = s16[2064,128]{1,0:T(8,128)(2,1)S(1)} custom-call(s32[4]{0:T(128)S(1)} %pad_add_fusion.place.place_ref, bf16[16,96,1024]{2,1,0:T(8,128)(2,1)S(1)} %get-tuple-element.55.refs_0_, bf16[4,128,1024]{2,1,0:T(8,128)(2,1)S(1)} %get-tuple-element.56.refs_1_, bf16[16,96,1024]{2,1,0:T(8,128)(2,1)S(1)} %online_back.1.refs_2_.refs_4_, ...), custom_call_target="tpu_custom_call" | custom-call | flops 1 | bytes 1 | tf_op jit(solution)/shard_map/grad_chunk/pallas_call | solution.py:231
  86.7 2.3 %grad_chunk.12.refs_2_.refs_0_ = s16[2064,128]{1,0:T(8,128)(2,1)S(1)} custom-call(s32[4]{0:T(128)S(1)} %pad_add_fusion.place.place_ref, bf16[8,96,1024]{2,1,0:T(8,128)(2,1)S(1)} %collective-permute-done.got_ref.refs_0_, bf16[8,96,1024]{2,1,0:T(8,128)(2,1)S(1)} %collective-permute-done.1.rest_ref.refs_1_, ...), custom_call_target="tpu_custom_call" | custom-call | flops 1 | bytes 1 | tf_op jit(solution)/shard_map/grad_chunk/pallas_call | solution.py:231
  92.5 6.8 %collective-permute-start.16 = (s16[2064,128]{1,0:T(8,128)(2,1)S(1)}, s16[2064,128]{1,0:T(8,128)(2,1)S(1)}, u32[]{:S(2)}, u32[]{:S(2)}) collective-permute-start(s16[2064,128]{1,0:T(8,128)(2,1)S(1)} %grad_chunk.10.refs_4_.refs_0_), channel_id=1, source_target_pairs={{0,4},{12,8},{1,5},{13,9},{2,6},{14,10},{3,7},{15,11},{16,20},{28,... | collective-permute-start | bytes 1585160 | tf_op jit(solution)/shard_map/ppermute | solution.py:831
  99.3 2.3 %grad_chunk.13.refs_6_.refs_0_ = s16[2064,128]{1,0:T(8,128)(2,1)S(1)} custom-call(s32[4]{0:T(128)S(1)} %pad_add_fusion.place.place_ref, bf16[8,96,1024]{2,1,0:T(8,128)(2,1)S(1)} %collective-permute-done.got_ref.refs_0_, bf16[8,96,1024]{2,1,0:T(8,128)(2,1)S(1)} %collective-permute-done.1.rest_ref.refs_1_, ...), custom_call_target="tpu_custom_call" | custom-call | flops 1 | bytes 1 | tf_op jit(solution)/shard_map/grad_chunk/pallas_call | solution.py:231
  101.6 2.4 %grad_chunk.14.refs_2_.refs_0_ = s16[2064,128]{1,0:T(8,128)(2,1)S(1)} custom-call(s32[4]{0:T(128)S(1)} %pad_add_fusion.place.place_ref, bf16[8,96,1024]{2,1,0:T(8,128)(2,1)S(1)} %collective-permute-done.got_ref.refs_0_, bf16[8,96,1024]{2,1,0:T(8,128)(2,1)S(1)} %collective-permute-done.1.rest_ref.refs_1_, ...), custom_call_target="tpu_custom_call" | custom-call | flops 1 | bytes 1 | tf_op jit(solution)/shard_map/grad_chunk/pallas_call | solution.py:231
  105.9 2.3 %grad_chunk.15.refs_2_.refs_0_ = s16[2064,128]{1,0:T(8,128)(2,1)S(1)} custom-call(s32[4]{0:T(128)S(1)} %pad_add_fusion.place.place_ref, bf16[8,96,1024]{2,1,0:T(8,128)(2,1)S(1)} %collective-permute-done.got_ref.refs_0_, bf16[8,96,1024]{2,1,0:T(8,128)(2,1)S(1)} %collective-permute-done.1.rest_ref.refs_1_, ...), custom_call_target="tpu_custom_call" | custom-call | flops 1 | bytes 1 | tf_op jit(solution)/shard_map/grad_chunk/pallas_call | solution.py:231
  110.7 4.8 %collective-permute-start.21 = (s16[2064,128]{1,0:T(8,128)(2,1)S(1)}, s16[2064,128]{1,0:T(8,128)(2,1)S(1)}, u32[]{:S(2)}, u32[]{:S(2)}) collective-permute-start(s16[2064,128]{1,0:T(8,128)(2,1)S(1)} %grad_chunk.11.refs_6_.refs_0_), channel_id=1, source_target_pairs={{0,4},{12,8},{1,5},{13,9},{2,6},{14,10},{3,7},{15,11},{16,20},{28,... | collective-permute-start | bytes 1585160 | tf_op jit(solution)/shard_map/ppermute | solution.py:840
  119.8 4.6 %collective-permute-start.18 = (s16[2064,128]{1,0:T(8,128)(2,1)S(1)}, s16[2064,128]{1,0:T(8,128)(2,1)S(1)}, u32[]{:S(2)}, u32[]{:S(2)}) collective-permute-start(s16[2064,128]{1,0:T(8,128)(2,1)S(1)} %grad_chunk.12.refs_2_.refs_0_), channel_id=1, source_target_pairs={{0,4},{12,8},{1,5},{13,9},{2,6},{14,10},{3,7},{15,11},{16,20},{28,... | collective-permute-start | bytes 1585160 | tf_op jit(solution)/shard_map/ppermute | solution.py:840
  130.9 6.9 %collective-permute-start.24 = (s16[2064,128]{1,0:T(8,128)(2,1)S(1)}, s16[2064,128]{1,0:T(8,128)(2,1)S(1)}, u32[]{:S(2)}, u32[]{:S(2)}) collective-permute-start(s16[2064,128]{1,0:T(8,128)(2,1)S(1)} %grad_chunk.13.refs_6_.refs_0_), channel_id=1, source_target_pairs={{0,4},{12,8},{1,5},{13,9},{2,6},{14,10},{3,7},{15,11},{16,20},{28,... | collective-permute-start | bytes 1585160 | tf_op jit(solution)/shard_map/ppermute | solution.py:840
  143.9 5.3 %collective-permute-start.30 = (s16[2064,128]{1,0:T(8,128)(2,1)S(1)}, s16[2064,128]{1,0:T(8,128)(2,1)S(1)}, u32[]{:S(2)}, u32[]{:S(2)}) collective-permute-start(s16[2064,128]{1,0:T(8,128)(2,1)S(1)} %grad_chunk.14.refs_2_.refs_0_), channel_id=1, source_target_pairs={{0,4},{12,8},{1,5},{13,9},{2,6},{14,10},{3,7},{15,11},{16,20},{28,... | collective-permute-start | bytes 1585160 | tf_op jit(solution)/shard_map/ppermute | solution.py:840
  155.2 5.3 %collective-permute-start.27 = (s16[2064,128]{1,0:T(8,128)(2,1)S(1)}, s16[2064,128]{1,0:T(8,128)(2,1)S(1)}, u32[]{:S(2)}, u32[]{:S(2)}) collective-permute-start(s16[2064,128]{1,0:T(8,128)(2,1)S(1)} %grad_chunk.15.refs_2_.refs_0_), channel_id=1, source_target_pairs={{0,4},{12,8},{1,5},{13,9},{2,6},{14,10},{3,7},{15,11},{16,20},{28,... | collective-permute-start | bytes 1585160 | tf_op jit(solution)/shard_map/ppermute | solution.py:840
  160.6 1.9 place_chunk.11
  166.8 3.1 %collective-permute-done.28.received = s16[2064,128]{1,0:T(8,128)(2,1)S(1)} collective-permute-done((s16[2064,128]{1,0:T(8,128)(2,1)S(1)}, s16[2064,128]{1,0:T(8,128)(2,1)S(1)}, u32[]{:S(2)}, u32[]{:S(2)}) %collective-permute-start.28) | collective-permute-done | bytes 528416 | tf_op jit(solution)/shard_map/ppermute | solution.py:837
  175.9 5.3 %collective-permute-done.33.received = s16[2064,128]{1,0:T(8,128)(2,1)S(1)} collective-permute-done((s16[2064,128]{1,0:T(8,128)(2,1)S(1)}, s16[2064,128]{1,0:T(8,128)(2,1)S(1)}, u32[]{:S(2)}, u32[]{:S(2)}) %collective-permute-start.33) | collective-permute-done | bytes 528416 | tf_op jit(solution)/shard_map/ppermute | solution.py:837
  185.4 7.0 %collective-permute-done.36.received = s16[2064,128]{1,0:T(8,128)(2,1)S(1)} collective-permute-done((s16[2064,128]{1,0:T(8,128)(2,1)S(1)}, s16[2064,128]{1,0:T(8,128)(2,1)S(1)}, u32[]{:S(2)}, u32[]{:S(2)}) %collective-permute-start.36) | collective-permute-done | bytes 528416 | tf_op jit(solution)/shard_map/ppermute | solution.py:837
  194.0 7.8 %collective-permute-done.35.received = s16[2064,128]{1,0:T(8,128)(2,1)S(1)} collective-permute-done((s16[2064,128]{1,0:T(8,128)(2,1)S(1)}, s16[2064,128]{1,0:T(8,128)(2,1)S(1)}, u32[]{:S(2)}, u32[]{:S(2)}) %collective-permute-start.35) | collective-permute-done | bytes 528416 | tf_op jit(solution)/shard_map/ppermute | solution.py:837
  201.9 2.3 %place_chunk.15 = (f32[2048,1024]{1,0:T(8,128)}, f32[8,128]{1,0:T(8,128)}) custom-call(s32[4]{0:T(128)S(1)} %pad_add_fusion.place.place_ref, s16[2064,128]{1,0:T(8,128)(2,1)S(1)} %add_chunk.31.refs_0_.total, s16[2064,128]{1,0:T(8,128)(2,1)S(1)} %collective-permute-done.35.received, ...), custom_call_target="tpu_custom_call", output_to_operand_aliasing={{0}: (4, {})} | custom-call | flops 1 | bytes 1 | tf_op jit(solution)/shard_map/place_chunk/pallas_call | solution.py:641
  (131 shorter events, 68.4 us)
Async XLA Ops:
  2.1 37.4 %collective-permute-start = (bf16[8,96,1024]{2,1,0:T(8,128)(2,1)S(1)}, bf16[8,96,1024]{2,1,0:T(8,128)(2,1)S(1)}, u32[]{:S(2)}, u32[]{:S(2)}) collective-permute-start(bf16[8,96,1024]{2,1,0:T(8,128)(2,1)S(1)} %section_share.2.refs_0_), channel_id=1, source_target_pairs={{0,2},{2,0},{1,3},{3,1},{4,6},{6,4},{5,7},{7,5},{8,10},{10,8},{9,1... | collective-permute-start | bytes 4718600 | tf_op jit(solution)/shard_map/ppermute | solution.py:747
  39.5 14.5 %collective-permute-start.2 = (bf16[2,128,1024]{2,1,0:T(8,128)(2,1)}, bf16[2,128,1024]{2,1,0:T(8,128)(2,1)S(1)}, u32[]{:S(2)}, u32[]{:S(2)}) collective-permute-start(bf16[2,128,1024]{2,1,0:T(8,128)(2,1)} %section_share.3.refs_1_), channel_id=1, source_target_pairs={{0,2},{2,0},{1,3},{3,1},{4,6},{6,4},{5,7},{7,5},{8,10},{10,8},{9,1... | collective-permute-start | bytes 1572872 | tf_op jit(solution)/shard_map/ppermute | solution.py:747
  54.1 5.2 %collective-permute-start.5 = (f32[8,24,96]{2,1,0:T(8,128)S(1)}, f32[8,24,96]{2,1,0:T(8,128)S(1)}, u32[]{:S(2)}, u32[]{:S(2)}) collective-permute-start(f32[8,24,96]{2,1,0:T(8,128)S(1)} %get-tuple-element.47), channel_id=1, source_target_pairs={{0,2},{2,0},{1,3},{3,1},{4,6},{6,4},{5,7},{7,5},{8,10},{10,8},{9,1... | collective-permute-start | bytes 221192 | tf_op jit(solution)/shard_map/ppermute | solution.py:765
  59.3 4.2 %collective-permute-start.11 = (f32[4,24,128]{2,1,0:T(8,128)S(1)}, f32[4,24,128]{2,1,0:T(8,128)S(1)}, u32[]{:S(2)}, u32[]{:S(2)}) collective-permute-start(f32[4,24,128]{2,1,0:T(8,128)S(1)} %get-tuple-element.48.refs_8_.refs_0_), channel_id=1, source_target_pairs={{0,2},{2,0},{1,3},{3,1},{4,6},{6,4},{5,7},{7,5},{8,10},{10,8},{9,1... | collective-permute-start | bytes 147464 | tf_op jit(solution)/shard_map/ppermute | solution.py:770
  61.0 8.2 %collective-permute-start.10 = (f32[4,24,128]{2,1,0:T(8,128)S(1)}, f32[4,24,128]{2,1,0:T(8,128)S(1)}, u32[]{:S(2)}, u32[]{:S(2)}) collective-permute-start(f32[4,24,128]{2,1,0:T(8,128)S(1)} %get-tuple-element.48.refs_8_.refs_0_), channel_id=1, source_target_pairs={{0,1},{1,0},{2,3},{3,2},{4,5},{5,4},{6,7},{7,6},{8,9},{9,8},{10,11... | collective-permute-start | bytes 147464 | tf_op jit(solution)/shard_map/ppermute | solution.py:771
  63.4 5.8 %collective-permute-start.12 = (f32[4,24,128]{2,1,0:T(8,128)S(1)}, f32[4,24,128]{2,1,0:T(8,128)S(1)}, u32[]{:S(2)}, u32[]{:S(2)}) collective-permute-start(f32[4,24,128]{2,1,0:T(8,128)S(1)} %collective-permute-done.11.refs_2_), channel_id=1, source_target_pairs={{0,1},{1,0},{2,3},{3,2},{4,5},{5,4},{6,7},{7,6},{8,9},{9,8},{10,11... | collective-permute-start | bytes 147464 | tf_op jit(solution)/shard_map/ppermute | solution.py:791
  63.4 7.4 %collective-permute-start.9 = (f32[72,96]{1,0:T(8,128)S(1)}, f32[72,96]{1,0:T(8,128)S(1)}, u32[]{:S(2)}, u32[]{:S(2)}) collective-permute-start(f32[72,96]{1,0:T(8,128)S(1)} %get-tuple-element.50.refs_11_.refs_0_), channel_id=1, source_target_pairs={{0,4},{4,8},{8,12},{12,0},{1,5},{5,9},{9,13},{13,1},{2,6},{6,10},{... | collective-permute-start | bytes 82952 | tf_op jit(solution)/shard_map/ppermute | solution.py:790
  65.3 5.5 %collective-permute-start.8 = (f32[72,96]{1,0:T(8,128)S(1)}, f32[72,96]{1,0:T(8,128)S(1)}, u32[]{:S(2)}, u32[]{:S(2)}) collective-permute-start(f32[72,96]{1,0:T(8,128)S(1)} %get-tuple-element.50.refs_11_.refs_0_), channel_id=1, source_target_pairs={{0,8},{4,12},{8,0},{12,4},{1,9},{5,13},{9,1},{13,5},{2,10},{6,14},... | collective-permute-start | bytes 82952 | tf_op jit(solution)/shard_map/ppermute | solution.py:790
  75.8 14.9 %collective-permute-start.14 = (s16[2064,128]{1,0:T(8,128)(2,1)S(1)}, s16[2064,128]{1,0:T(8,128)(2,1)S(1)}, u32[]{:S(2)}, u32[]{:S(2)}) collective-permute-start(s16[2064,128]{1,0:T(8,128)(2,1)S(1)} %grad_chunk.8.refs_4_.refs_0_), channel_id=1, source_target_pairs={{0,4},{12,8},{1,5},{13,9},{2,6},{14,10},{3,7},{15,11},{16,20},{28,... | collective-permute-start | bytes 1585160 | tf_op jit(solution)/shard_map/ppermute | solution.py:831
  80.7 23.3 %collective-permute-start.13 = (s16[2064,128]{1,0:T(8,128)(2,1)S(1)}, s16[2064,128]{1,0:T(8,128)(2,1)S(1)}, u32[]{:S(2)}, u32[]{:S(2)}) collective-permute-start(s16[2064,128]{1,0:T(8,128)(2,1)S(1)} %grad_chunk.9.refs_4_.refs_0_), channel_id=1, source_target_pairs={{0,4},{12,8},{1,5},{13,9},{2,6},{14,10},{3,7},{15,11},{16,20},{28,... | collective-permute-start | bytes 1585160 | tf_op jit(solution)/shard_map/ppermute | solution.py:831
  91.8 16.4 %collective-permute-start.17 = (s16[2064,128]{1,0:T(8,128)(2,1)S(1)}, s16[2064,128]{1,0:T(8,128)(2,1)S(1)}, u32[]{:S(2)}, u32[]{:S(2)}) collective-permute-start(s16[2064,128]{1,0:T(8,128)(2,1)S(1)} %add_chunk.16.refs_6_.refs_0_), channel_id=1, source_target_pairs={{4,8},{8,4},{5,9},{9,5},{6,10},{10,6},{7,11},{11,7},{20,24},{24,20... | collective-permute-start | bytes 1585160 | tf_op jit(solution)/shard_map/ppermute | solution.py:834
  92.5 22.9 %collective-permute-start.16 = (s16[2064,128]{1,0:T(8,128)(2,1)S(1)}, s16[2064,128]{1,0:T(8,128)(2,1)S(1)}, u32[]{:S(2)}, u32[]{:S(2)}) collective-permute-start(s16[2064,128]{1,0:T(8,128)(2,1)S(1)} %grad_chunk.10.refs_4_.refs_0_), channel_id=1, source_target_pairs={{0,4},{12,8},{1,5},{13,9},{2,6},{14,10},{3,7},{15,11},{16,20},{28,... | collective-permute-start | bytes 1585160 | tf_op jit(solution)/shard_map/ppermute | solution.py:831
  105.2 12.2 %collective-permute-start.15 = (s16[2064,128]{1,0:T(8,128)(2,1)S(1)}, s16[2064,128]{1,0:T(8,128)(2,1)S(1)}, u32[]{:S(2)}, u32[]{:S(2)}) collective-permute-start(s16[2064,128]{1,0:T(8,128)(2,1)S(1)} %add_chunk.17.refs_6_.refs_0_), channel_id=1, source_target_pairs={{4,8},{8,4},{5,9},{9,5},{6,10},{10,6},{7,11},{11,7},{20,24},{24,20... | collective-permute-start | bytes 1585160 | tf_op jit(solution)/shard_map/ppermute | solution.py:834
  109.4 15.5 %collective-permute-start.22 = (s16[2064,128]{1,0:T(8,128)(2,1)S(1)}, s16[2064,128]{1,0:T(8,128)(2,1)S(1)}, u32[]{:S(2)}, u32[]{:S(2)}) collective-permute-start(s16[2064,128]{1,0:T(8,128)(2,1)S(1)} %add_chunk.18.refs_2_.total), channel_id=1, source_target_pairs={{4,0},{8,12},{5,1},{9,13},{6,2},{10,14},{7,3},{11,15},{20,16},{24,... | collective-permute-start | bytes 1585160 | tf_op jit(solution)/shard_map/ppermute | solution.py:837
  110.7 15.9 %collective-permute-start.21 = (s16[2064,128]{1,0:T(8,128)(2,1)S(1)}, s16[2064,128]{1,0:T(8,128)(2,1)S(1)}, u32[]{:S(2)}, u32[]{:S(2)}) collective-permute-start(s16[2064,128]{1,0:T(8,128)(2,1)S(1)} %grad_chunk.11.refs_6_.refs_0_), channel_id=1, source_target_pairs={{0,4},{12,8},{1,5},{13,9},{2,6},{14,10},{3,7},{15,11},{16,20},{28,... | collective-permute-start | bytes 1585160 | tf_op jit(solution)/shard_map/ppermute | solution.py:840
  116.6 11.8 %collective-permute-start.20 = (s16[2064,128]{1,0:T(8,128)(2,1)S(1)}, s16[2064,128]{1,0:T(8,128)(2,1)S(1)}, u32[]{:S(2)}, u32[]{:S(2)}) collective-permute-start(s16[2064,128]{1,0:T(8,128)(2,1)S(1)} %add_chunk.19.refs_2_.refs_0_), channel_id=1, source_target_pairs={{4,8},{8,4},{5,9},{9,5},{6,10},{10,6},{7,11},{11,7},{20,24},{24,20... | collective-permute-start | bytes 1585160 | tf_op jit(solution)/shard_map/ppermute | solution.py:834
  118.5 19.3 %collective-permute-start.19 = (s16[2064,128]{1,0:T(8,128)(2,1)S(1)}, s16[2064,128]{1,0:T(8,128)(2,1)S(1)}, u32[]{:S(2)}, u32[]{:S(2)}) collective-permute-start(s16[2064,128]{1,0:T(8,128)(2,1)S(1)} %add_chunk.20.refs_0_.total), channel_id=1, source_target_pairs={{4,0},{8,12},{5,1},{9,13},{6,2},{10,14},{7,3},{11,15},{20,16},{24,... | collective-permute-start | bytes 1585160 | tf_op jit(solution)/shard_map/ppermute | solution.py:837
  119.8 19.7 %collective-permute-start.18 = (s16[2064,128]{1,0:T(8,128)(2,1)S(1)}, s16[2064,128]{1,0:T(8,128)(2,1)S(1)}, u32[]{:S(2)}, u32[]{:S(2)}) collective-permute-start(s16[2064,128]{1,0:T(8,128)(2,1)S(1)} %grad_chunk.12.refs_2_.refs_0_), channel_id=1, source_target_pairs={{0,4},{12,8},{1,5},{13,9},{2,6},{14,10},{3,7},{15,11},{16,20},{28,... | collective-permute-start | bytes 1585160 | tf_op jit(solution)/shard_map/ppermute | solution.py:840
  127.7 13.7 %collective-permute-start.26 = (s16[2064,128]{1,0:T(8,128)(2,1)S(1)}, s16[2064,128]{1,0:T(8,128)(2,1)S(1)}, u32[]{:S(2)}, u32[]{:S(2)}) collective-permute-start(s16[2064,128]{1,0:T(8,128)(2,1)S(1)} %add_chunk.21.refs_2_.refs_0_), channel_id=1, source_target_pairs={{4,8},{8,4},{5,9},{9,5},{6,10},{10,6},{7,11},{11,7},{20,24},{24,20... | collective-permute-start | bytes 1585160 | tf_op jit(solution)/shard_map/ppermute | solution.py:834
  129.6 19.5 %collective-permute-start.25 = (s16[2064,128]{1,0:T(8,128)(2,1)S(1)}, s16[2064,128]{1,0:T(8,128)(2,1)S(1)}, u32[]{:S(2)}, u32[]{:S(2)}) collective-permute-start(s16[2064,128]{1,0:T(8,128)(2,1)S(1)} %add_chunk.22.refs_0_.total), channel_id=1, source_target_pairs={{4,0},{8,12},{5,1},{9,13},{6,2},{10,14},{7,3},{11,15},{20,16},{24,... | collective-permute-start | bytes 1585160 | tf_op jit(solution)/shard_map/ppermute | solution.py:837
  130.9 19.9 %collective-permute-start.24 = (s16[2064,128]{1,0:T(8,128)(2,1)S(1)}, s16[2064,128]{1,0:T(8,128)(2,1)S(1)}, u32[]{:S(2)}, u32[]{:S(2)}) collective-permute-start(s16[2064,128]{1,0:T(8,128)(2,1)S(1)} %grad_chunk.13.refs_6_.refs_0_), channel_id=1, source_target_pairs={{0,4},{12,8},{1,5},{13,9},{2,6},{14,10},{3,7},{15,11},{16,20},{28,... | collective-permute-start | bytes 1585160 | tf_op jit(solution)/shard_map/ppermute | solution.py:840
  140.7 12.0 %collective-permute-start.23 = (s16[2064,128]{1,0:T(8,128)(2,1)S(1)}, s16[2064,128]{1,0:T(8,128)(2,1)S(1)}, u32[]{:S(2)}, u32[]{:S(2)}) collective-permute-start(s16[2064,128]{1,0:T(8,128)(2,1)S(1)} %add_chunk.23.refs_2_.refs_0_), channel_id=1, source_target_pairs={{4,8},{8,4},{5,9},{9,5},{6,10},{10,6},{7,11},{11,7},{20,24},{24,20... | collective-permute-start | bytes 1585160 | tf_op jit(solution)/shard_map/ppermute | solution.py:834
  142.6 18.0 %collective-permute-start.31 = (s16[2064,128]{1,0:T(8,128)(2,1)S(1)}, s16[2064,128]{1,0:T(8,128)(2,1)S(1)}, u32[]{:S(2)}, u32[]{:S(2)}) collective-permute-start(s16[2064,128]{1,0:T(8,128)(2,1)S(1)} %add_chunk.24.refs_0_.total), channel_id=1, source_target_pairs={{4,0},{8,12},{5,1},{9,13},{6,2},{10,14},{7,3},{11,15},{20,16},{24,... | collective-permute-start | bytes 1585160 | tf_op jit(solution)/shard_map/ppermute | solution.py:837
  143.9 18.6 %collective-permute-start.30 = (s16[2064,128]{1,0:T(8,128)(2,1)S(1)}, s16[2064,128]{1,0:T(8,128)(2,1)S(1)}, u32[]{:S(2)}, u32[]{:S(2)}) collective-permute-start(s16[2064,128]{1,0:T(8,128)(2,1)S(1)} %grad_chunk.14.refs_2_.refs_0_), channel_id=1, source_target_pairs={{0,4},{12,8},{1,5},{13,9},{2,6},{14,10},{3,7},{15,11},{16,20},{28,... | collective-permute-start | bytes 1585160 | tf_op jit(solution)/shard_map/ppermute | solution.py:840
  152.0 12.3 %collective-permute-start.29 = (s16[2064,128]{1,0:T(8,128)(2,1)S(1)}, s16[2064,128]{1,0:T(8,128)(2,1)S(1)}, u32[]{:S(2)}, u32[]{:S(2)}) collective-permute-start(s16[2064,128]{1,0:T(8,128)(2,1)S(1)} %add_chunk.25.refs_2_.refs_0_), channel_id=1, source_target_pairs={{4,8},{8,4},{5,9},{9,5},{6,10},{10,6},{7,11},{11,7},{20,24},{24,20... | collective-permute-start | bytes 1585160 | tf_op jit(solution)/shard_map/ppermute | solution.py:834
  153.9 16.0 %collective-permute-start.28 = (s16[2064,128]{1,0:T(8,128)(2,1)S(1)}, s16[2064,128]{1,0:T(8,128)(2,1)S(1)}, u32[]{:S(2)}, u32[]{:S(2)}) collective-permute-start(s16[2064,128]{1,0:T(8,128)(2,1)S(1)} %add_chunk.26.refs_0_.total), channel_id=1, source_target_pairs={{4,0},{8,12},{5,1},{9,13},{6,2},{10,14},{7,3},{11,15},{20,16},{24,... | collective-permute-start | bytes 1585160 | tf_op jit(solution)/shard_map/ppermute | solution.py:837
  155.2 16.4 %collective-permute-start.27 = (s16[2064,128]{1,0:T(8,128)(2,1)S(1)}, s16[2064,128]{1,0:T(8,128)(2,1)S(1)}, u32[]{:S(2)}, u32[]{:S(2)}) collective-permute-start(s16[2064,128]{1,0:T(8,128)(2,1)S(1)} %grad_chunk.15.refs_2_.refs_0_), channel_id=1, source_target_pairs={{0,4},{12,8},{1,5},{13,9},{2,6},{14,10},{3,7},{15,11},{16,20},{28,... | collective-permute-start | bytes 1585160 | tf_op jit(solution)/shard_map/ppermute | solution.py:840
  163.6 9.8 %collective-permute-start.34 = (s16[2064,128]{1,0:T(8,128)(2,1)S(1)}, s16[2064,128]{1,0:T(8,128)(2,1)S(1)}, u32[]{:S(2)}, u32[]{:S(2)}) collective-permute-start(s16[2064,128]{1,0:T(8,128)(2,1)S(1)} %add_chunk.27.refs_2_.refs_0_), channel_id=1, source_target_pairs={{4,8},{8,4},{5,9},{9,5},{6,10},{10,6},{7,11},{11,7},{20,24},{24,20... | collective-permute-start | bytes 1585160 | tf_op jit(solution)/shard_map/ppermute | solution.py:834
  165.5 15.7 %collective-permute-start.33 = (s16[2064,128]{1,0:T(8,128)(2,1)S(1)}, s16[2064,128]{1,0:T(8,128)(2,1)S(1)}, u32[]{:S(2)}, u32[]{:S(2)}) collective-permute-start(s16[2064,128]{1,0:T(8,128)(2,1)S(1)} %add_chunk.28.refs_0_.total), channel_id=1, source_target_pairs={{4,0},{8,12},{5,1},{9,13},{6,2},{10,14},{7,3},{11,15},{20,16},{24,... | collective-permute-start | bytes 1585160 | tf_op jit(solution)/shard_map/ppermute | solution.py:837
  172.7 10.2 %collective-permute-start.32 = (s16[2064,128]{1,0:T(8,128)(2,1)S(1)}, s16[2064,128]{1,0:T(8,128)(2,1)S(1)}, u32[]{:S(2)}, u32[]{:S(2)}) collective-permute-start(s16[2064,128]{1,0:T(8,128)(2,1)S(1)} %add_chunk.29.refs_2_.refs_0_), channel_id=1, source_target_pairs={{4,8},{8,4},{5,9},{9,5},{6,10},{10,6},{7,11},{11,7},{20,24},{24,20... | collective-permute-start | bytes 1585160 | tf_op jit(solution)/shard_map/ppermute | solution.py:834
  174.6 17.7 %collective-permute-start.36 = (s16[2064,128]{1,0:T(8,128)(2,1)S(1)}, s16[2064,128]{1,0:T(8,128)(2,1)S(1)}, u32[]{:S(2)}, u32[]{:S(2)}) collective-permute-start(s16[2064,128]{1,0:T(8,128)(2,1)S(1)} %add_chunk.30.refs_0_.total), channel_id=1, source_target_pairs={{4,0},{8,12},{5,1},{9,13},{6,2},{10,14},{7,3},{11,15},{20,16},{24,... | collective-permute-start | bytes 1585160 | tf_op jit(solution)/shard_map/ppermute | solution.py:837
  184.1 17.8 %collective-permute-start.35 = (s16[2064,128]{1,0:T(8,128)(2,1)S(1)}, s16[2064,128]{1,0:T(8,128)(2,1)S(1)}, u32[]{:S(2)}, u32[]{:S(2)}) collective-permute-start(s16[2064,128]{1,0:T(8,128)(2,1)S(1)} %add_chunk.31.refs_0_.total), channel_id=1, source_target_pairs={{4,0},{8,12},{5,1},{9,13},{6,2},{10,14},{7,3},{11,15},{20,16},{24,... | collective-permute-start | bytes 1585160 | tf_op jit(solution)/shard_map/ppermute | solution.py:837
  (19 other events, 134.5 us)

commit v3 on v2

--- a/solution.py
+++ b/solution.py
@@ -194,7 +194,7 @@
 ADD_BLOCKS = 2
 ROW_GROUPS = 4
 GRAD_CHUNKS = 8
-GRAD_LEAD = 5
+GRAD_LEAD = 6
 SEND_LEAD = 3
 LANES = 128
 CODE_LIMIT = 32512.0

time: 205 us -> 203 us (level)
  waiting for transfers between devices: 49.8 us -> 47.7 us
  transfers between devices with their start and end apart: 37 -> 37, of which waited for: 14 -> 14; matrix products, arithmetic and copies ran while one was open for 0% -> 0% of each run, Pallas kernels for 36% -> 37%
where the time goes in v3:
time: 203 us
  Pallas kernels  82.5 us (41%)
  starting transfers between devices  68.2 us (34%)
  waiting for transfers between devices  47.7 us (23%)
  local copies, waits for them, and re-layouts  3.02 us (1%)
    pallas_call x28, Pallas kernels, vmem_call(): pl.pallas_call(run, in_specs=[SMEM] + [VMEM] * len(operands), out_specs=[...  41.7 us
    ppermute x5, starting transfers between devices, line_plan(): inward[ahead] = lax.ppermute(after(messages[ahead], last), 'dp', TO_CENTER)  28 us
    ppermute x8, waiting for transfers between devices, line_plan(): outward[k] = lax.ppermute(last, 'dp', FROM_CENTER)  22.5 us
    ppermute x2, waiting for transfers between devices, line_plan(): got = [lax.ppermute(half, 'mp', SWAP) for half in halves]  18.3 us
    pallas_call x8, Pallas kernels, place_chunk(): pl.pallas_call(functools.partial(place_body, hidden_count // LANES, rows,...  14.3 us
    pallas_call x2, Pallas kernels, own_half(): pl.pallas_call(own_half_body, in_specs=[SMEM, HBM] + [VMEM] * len(operand...  13 us
    ppermute x8, starting transfers between devices, line_plan(): outward[k] = lax.ppermute(last, 'dp', FROM_CENTER)  10.3 us
    ppermute x3, starting transfers between devices, line_plan(): inward[k] = lax.ppermute(last, 'dp', TO_CENTER)  9.83 us
  transfers between devices with their start and end apart: 37, of which 14 were waited for; matrix products, arithmetic and copies ran while one was open for 0% of the time, Pallas kernels for 37%

profile of v3, /device:TPU:0, one launch (start us, length us, event | category | flops | bytes accessed | tf_op | source)
XLA Modules:
  0.0 202.7 jit_solution(18173832489610548521)
XLA Ops:
  0.1 2.0 section_share.2.refs_0_
  2.1 3.0 %collective-permute-start = (bf16[8,96,1024]{2,1,0:T(8,128)(2,1)S(1)}, bf16[8,96,1024]{2,1,0:T(8,128)(2,1)S(1)}, u32[]{:S(2)}, u32[]{:S(2)}) collective-permute-start(bf16[8,96,1024]{2,1,0:T(8,128)(2,1)S(1)} %section_share.2.refs_0_), channel_id=1, source_target_pairs={{0,2},{2,0},{1,3},{3,1},{4,6},{6,4},{5,7},{7,5},{8,10},{10,8},{9,1... | collective-permute-start | bytes 4718600 | tf_op jit(solution)/shard_map/ppermute | solution.py:747
  5.1 2.4 %section_share.3.refs_1_ = bf16[2,128,1024]{2,1,0:T(8,128)(2,1)} custom-call(s32[4]{0:T(128)S(1)} %pad_add_fusion.place.place_ref, bf16[4,128,1024]{2,1,0:T(8,128)(2,1)} %bitcast.15, bf16[8,96,1024]{2,1,0:T(8,128)(2,1)S(1)} %section_share.2.refs_0_), custom_call_target="tpu_custom_call" | custom-call | flops 1 | bytes 1 | tf_op jit(solution)/shard_map/section_share/pallas_call | solution.py:257
  8.5 2.2 %copy-done = bf16[1,2048,1024]{2,1,0:T(8,128)(2,1)S(1)} copy-done((bf16[1,2048,1024]{2,1,0:T(8,128)(2,1)S(1)}, bf16[1,2048,1024]{2,1,0:T(8,128)(2,1)}, u32[]{:S(2)}) %copy-start) | copy-done | bytes 4194328
  10.7 9.4 %own_half.2 = (bf16[16,96,1024]{2,1,0:T(8,128)(2,1)S(1)}, f32[16,96,1024]{2,1,0:T(8,128)S(1)}) custom-call(s32[4]{0:T(128)S(1)} %pad_add_fusion.place.place_ref, bf16[16,96,1024]{2,1,0:T(8,128)(2,1)} %source.3, bf16[2048,1024]{1,0:T(8,128)(2,1)S(1)} %bitcast.11, bf16[8,96,1024]{2,1,0:T(8,128)(2,1)S(1)} %section_share.2.refs_0_, ...), custom_call_target="tpu_custom_call" | custom-call | flops 1 | bytes 1 | tf_op jit(solution)/shard_map/own_half/pallas_call | solution.py:295
  20.2 3.6 %own_half.3 = (bf16[4,128,1024]{2,1,0:T(8,128)(2,1)S(1)}, f32[4,128,1024]{2,1,0:T(8,128)S(1)}) custom-call(s32[4]{0:T(128)S(1)} %pad_add_fusion.place.place_ref, bf16[4,128,1024]{2,1,0:T(8,128)(2,1)} %bitcast.16, bf16[2048,1024]{1,0:T(8,128)(2,1)S(1)} %bitcast.12, f32[16,96,1024]{2,1,0:T(8,128)S(1)} %get-tuple-element.41.refs_0_.pre_ref), custom_call_target="tpu_custom_call" | custom-call | flops 1 | bytes 1 | tf_op jit(solution)/shard_map/own_half/pallas_call | solution.py:295
  23.7 15.8 %collective-permute-done.got_ref.refs_0_ = bf16[8,96,1024]{2,1,0:T(8,128)(2,1)S(1)} collective-permute-done((bf16[8,96,1024]{2,1,0:T(8,128)(2,1)S(1)}, bf16[8,96,1024]{2,1,0:T(8,128)(2,1)S(1)}, u32[]{:S(2)}, u32[]{:S(2)}) %collective-permute-start) | collective-permute-done | bytes 1572896 | tf_op jit(solution)/shard_map/ppermute | solution.py:747
  42.9 6.5 %forward_rows.2 = (f32[16,96,1024]{2,1,0:T(8,128)S(1)}, f32[16,24,96]{2,1,0:T(8,128)S(1)}) custom-call(s32[4]{0:T(128)S(1)} %pad_add_fusion.place.place_ref, f32[16,96,1024]{2,1,0:T(8,128)S(1)} %get-tuple-element.41.refs_0_.pre_ref, bf16[8,96,1024]{2,1,0:T(8,128)(2,1)S(1)} %collective-permute-done.got_ref.refs_0_, ...), custom_call_target="tpu_custom_call", output_to_operand_aliasing={{0}: (1, {})} | custom-call | flops 1 | bytes 1 | tf_op jit(solution)/shard_map/forward_rows/pallas_call | solution.py:347
  51.5 2.6 %collective-permute-done.2.got_ref.refs_2_ = bf16[2,128,1024]{2,1,0:T(8,128)(2,1)S(1)} collective-permute-done((bf16[2,128,1024]{2,1,0:T(8,128)(2,1)}, bf16[2,128,1024]{2,1,0:T(8,128)(2,1)S(1)}, u32[]{:S(2)}, u32[]{:S(2)}) %collective-permute-start.2) | collective-permute-done | bytes 524320 | tf_op jit(solution)/shard_map/ppermute | solution.py:747
  56.0 2.7 %forward_rows.3 = (f32[4,128,1024]{2,1,0:T(8,128)S(1)}, f32[4,24,128]{2,1,0:T(8,128)S(1)}) custom-call(s32[4]{0:T(128)S(1)} %pad_add_fusion.place.place_ref, f32[4,128,1024]{2,1,0:T(8,128)S(1)} %get-tuple-element.42.pre_ref, bf16[2,128,1024]{2,1,0:T(8,128)(2,1)S(1)} %collective-permute-done.2.got_ref.refs_2_, ...), custom_call_target="tpu_custom_call", output_to_operand_aliasing={{0}: (1, {})} | custom-call | flops 1 | bytes 1 | tf_op jit(solution)/shard_map/forward_rows/pallas_call | solution.py:347
  63.4 1.8 collective-permute-start.9
  65.3 2.6 %collective-permute-start.8 = (f32[72,96]{1,0:T(8,128)S(1)}, f32[72,96]{1,0:T(8,128)S(1)}, u32[]{:S(2)}, u32[]{:S(2)}) collective-permute-start(f32[72,96]{1,0:T(8,128)S(1)} %get-tuple-element.50.refs_11_.refs_0_), channel_id=1, source_target_pairs={{0,8},{4,12},{8,0},{12,4},{1,9},{5,13},{9,1},{13,5},{2,10},{6,14},... | collective-permute-start | bytes 82952 | tf_op jit(solution)/shard_map/ppermute | solution.py:790
  73.5 2.3 %grad_chunk.8.refs_4_.refs_0_ = s16[2064,128]{1,0:T(8,128)(2,1)S(1)} custom-call(s32[4]{0:T(128)S(1)} %pad_add_fusion.place.place_ref, bf16[16,96,1024]{2,1,0:T(8,128)(2,1)S(1)} %get-tuple-element.55.refs_0_, bf16[4,128,1024]{2,1,0:T(8,128)(2,1)S(1)} %get-tuple-element.56.refs_1_, bf16[16,96,1024]{2,1,0:T(8,128)(2,1)S(1)} %online_back.1.refs_2_.refs_4_, ...), custom_call_target="tpu_custom_call" | custom-call | flops 1 | bytes 1 | tf_op jit(solution)/shard_map/grad_chunk/pallas_call | solution.py:231
  75.8 2.5 %collective-permute-start.13 = (s16[2064,128]{1,0:T(8,128)(2,1)S(1)}, s16[2064,128]{1,0:T(8,128)(2,1)S(1)}, u32[]{:S(2)}, u32[]{:S(2)}) collective-permute-start(s16[2064,128]{1,0:T(8,128)(2,1)S(1)} %grad_chunk.8.refs_4_.refs_0_), channel_id=1, source_target_pairs={{0,4},{12,8},{1,5},{13,9},{2,6},{14,10},{3,7},{15,11},{16,20},{28,... | collective-permute-start | bytes 1585160 | tf_op jit(solution)/shard_map/ppermute | solution.py:831
  78.3 2.3 %grad_chunk.9.refs_4_.refs_0_ = s16[2064,128]{1,0:T(8,128)(2,1)S(1)} custom-call(s32[4]{0:T(128)S(1)} %pad_add_fusion.place.place_ref, bf16[16,96,1024]{2,1,0:T(8,128)(2,1)S(1)} %get-tuple-element.55.refs_0_, bf16[4,128,1024]{2,1,0:T(8,128)(2,1)S(1)} %get-tuple-element.56.refs_1_, bf16[16,96,1024]{2,1,0:T(8,128)(2,1)S(1)} %online_back.1.refs_2_.refs_4_, ...), custom_call_target="tpu_custom_call" | custom-call | flops 1 | bytes 1 | tf_op jit(solution)/shard_map/grad_chunk/pallas_call | solution.py:231
  82.0 2.3 %grad_chunk.10.refs_4_.refs_0_ = s16[2064,128]{1,0:T(8,128)(2,1)S(1)} custom-call(s32[4]{0:T(128)S(1)} %pad_add_fusion.place.place_ref, bf16[16,96,1024]{2,1,0:T(8,128)(2,1)S(1)} %get-tuple-element.55.refs_0_, bf16[4,128,1024]{2,1,0:T(8,128)(2,1)S(1)} %get-tuple-element.56.refs_1_, bf16[16,96,1024]{2,1,0:T(8,128)(2,1)S(1)} %online_back.1.refs_2_.refs_4_, ...), custom_call_target="tpu_custom_call" | custom-call | flops 1 | bytes 1 | tf_op jit(solution)/shard_map/grad_chunk/pallas_call | solution.py:231
  84.3 2.4 %grad_chunk.11.refs_6_.refs_0_ = s16[2064,128]{1,0:T(8,128)(2,1)S(1)} custom-call(s32[4]{0:T(128)S(1)} %pad_add_fusion.place.place_ref, bf16[16,96,1024]{2,1,0:T(8,128)(2,1)S(1)} %get-tuple-element.55.refs_0_, bf16[4,128,1024]{2,1,0:T(8,128)(2,1)S(1)} %get-tuple-element.56.refs_1_, bf16[16,96,1024]{2,1,0:T(8,128)(2,1)S(1)} %online_back.1.refs_2_.refs_4_, ...), custom_call_target="tpu_custom_call" | custom-call | flops 1 | bytes 1 | tf_op jit(solution)/shard_map/grad_chunk/pallas_call | solution.py:231
  86.7 2.3 %grad_chunk.12.refs_6_.refs_0_ = s16[2064,128]{1,0:T(8,128)(2,1)S(1)} custom-call(s32[4]{0:T(128)S(1)} %pad_add_fusion.place.place_ref, bf16[8,96,1024]{2,1,0:T(8,128)(2,1)S(1)} %collective-permute-done.got_ref.refs_0_, bf16[8,96,1024]{2,1,0:T(8,128)(2,1)S(1)} %collective-permute-done.1.rest_ref.refs_1_, ...), custom_call_target="tpu_custom_call" | custom-call | flops 1 | bytes 1 | tf_op jit(solution)/shard_map/grad_chunk/pallas_call | solution.py:231
  89.1 2.3 %grad_chunk.13.refs_2_.refs_0_ = s16[2064,128]{1,0:T(8,128)(2,1)S(1)} custom-call(s32[4]{0:T(128)S(1)} %pad_add_fusion.place.place_ref, bf16[8,96,1024]{2,1,0:T(8,128)(2,1)S(1)} %collective-permute-done.got_ref.refs_0_, bf16[8,96,1024]{2,1,0:T(8,128)(2,1)S(1)} %collective-permute-done.1.rest_ref.refs_1_, ...), custom_call_target="tpu_custom_call" | custom-call | flops 1 | bytes 1 | tf_op jit(solution)/shard_map/grad_chunk/pallas_call | solution.py:231
  93.3 6.0 %collective-permute-start.16 = (s16[2064,128]{1,0:T(8,128)(2,1)S(1)}, s16[2064,128]{1,0:T(8,128)(2,1)S(1)}, u32[]{:S(2)}, u32[]{:S(2)}) collective-permute-start(s16[2064,128]{1,0:T(8,128)(2,1)S(1)} %grad_chunk.10.refs_4_.refs_0_), channel_id=1, source_target_pairs={{0,4},{12,8},{1,5},{13,9},{2,6},{14,10},{3,7},{15,11},{16,20},{28,... | collective-permute-start | bytes 1585160 | tf_op jit(solution)/shard_map/ppermute | solution.py:831
  99.3 2.4 %grad_chunk.14.refs_6_.refs_0_ = s16[2064,128]{1,0:T(8,128)(2,1)S(1)} custom-call(s32[4]{0:T(128)S(1)} %pad_add_fusion.place.place_ref, bf16[8,96,1024]{2,1,0:T(8,128)(2,1)S(1)} %collective-permute-done.got_ref.refs_0_, bf16[8,96,1024]{2,1,0:T(8,128)(2,1)S(1)} %collective-permute-done.1.rest_ref.refs_1_, ...), custom_call_target="tpu_custom_call" | custom-call | flops 1 | bytes 1 | tf_op jit(solution)/shard_map/grad_chunk/pallas_call | solution.py:231
  101.7 2.3 %grad_chunk.15.refs_2_.refs_0_ = s16[2064,128]{1,0:T(8,128)(2,1)S(1)} custom-call(s32[4]{0:T(128)S(1)} %pad_add_fusion.place.place_ref, bf16[8,96,1024]{2,1,0:T(8,128)(2,1)S(1)} %collective-permute-done.got_ref.refs_0_, bf16[8,96,1024]{2,1,0:T(8,128)(2,1)S(1)} %collective-permute-done.1.rest_ref.refs_1_, ...), custom_call_target="tpu_custom_call" | custom-call | flops 1 | bytes 1 | tf_op jit(solution)/shard_map/grad_chunk/pallas_call | solution.py:231
  108.3 4.8 %collective-permute-start.21 = (s16[2064,128]{1,0:T(8,128)(2,1)S(1)}, s16[2064,128]{1,0:T(8,128)(2,1)S(1)}, u32[]{:S(2)}, u32[]{:S(2)}) collective-permute-start(s16[2064,128]{1,0:T(8,128)(2,1)S(1)} %grad_chunk.11.refs_6_.refs_0_), channel_id=1, source_target_pairs={{0,4},{12,8},{1,5},{13,9},{2,6},{14,10},{3,7},{15,11},{16,20},{28,... | collective-permute-start | bytes 1585160 | tf_op jit(solution)/shard_map/ppermute | solution.py:840
  117.6 6.3 %collective-permute-start.18 = (s16[2064,128]{1,0:T(8,128)(2,1)S(1)}, s16[2064,128]{1,0:T(8,128)(2,1)S(1)}, u32[]{:S(2)}, u32[]{:S(2)}) collective-permute-start(s16[2064,128]{1,0:T(8,128)(2,1)S(1)} %grad_chunk.12.refs_6_.refs_0_), channel_id=1, source_target_pairs={{0,4},{12,8},{1,5},{13,9},{2,6},{14,10},{3,7},{15,11},{16,20},{28,... | collective-permute-start | bytes 1585160 | tf_op jit(solution)/shard_map/ppermute | solution.py:840
  130.0 6.1 %collective-permute-start.24 = (s16[2064,128]{1,0:T(8,128)(2,1)S(1)}, s16[2064,128]{1,0:T(8,128)(2,1)S(1)}, u32[]{:S(2)}, u32[]{:S(2)}) collective-permute-start(s16[2064,128]{1,0:T(8,128)(2,1)S(1)} %grad_chunk.13.refs_2_.refs_0_), channel_id=1, source_target_pairs={{0,4},{12,8},{1,5},{13,9},{2,6},{14,10},{3,7},{15,11},{16,20},{28,... | collective-permute-start | bytes 1585160 | tf_op jit(solution)/shard_map/ppermute | solution.py:840
  142.1 5.3 %collective-permute-start.30 = (s16[2064,128]{1,0:T(8,128)(2,1)S(1)}, s16[2064,128]{1,0:T(8,128)(2,1)S(1)}, u32[]{:S(2)}, u32[]{:S(2)}) collective-permute-start(s16[2064,128]{1,0:T(8,128)(2,1)S(1)} %grad_chunk.14.refs_6_.refs_0_), channel_id=1, source_target_pairs={{0,4},{12,8},{1,5},{13,9},{2,6},{14,10},{3,7},{15,11},{16,20},{28,... | collective-permute-start | bytes 1585160 | tf_op jit(solution)/shard_map/ppermute | solution.py:840
  153.5 5.6 %collective-permute-start.27 = (s16[2064,128]{1,0:T(8,128)(2,1)S(1)}, s16[2064,128]{1,0:T(8,128)(2,1)S(1)}, u32[]{:S(2)}, u32[]{:S(2)}) collective-permute-start(s16[2064,128]{1,0:T(8,128)(2,1)S(1)} %grad_chunk.15.refs_2_.refs_0_), channel_id=1, source_target_pairs={{0,4},{12,8},{1,5},{13,9},{2,6},{14,10},{3,7},{15,11},{16,20},{28,... | collective-permute-start | bytes 1585160 | tf_op jit(solution)/shard_map/ppermute | solution.py:840
  159.1 1.9 place_chunk.11
  173.2 5.1 %collective-permute-done.33.received = s16[2064,128]{1,0:T(8,128)(2,1)S(1)} collective-permute-done((s16[2064,128]{1,0:T(8,128)(2,1)S(1)}, s16[2064,128]{1,0:T(8,128)(2,1)S(1)}, u32[]{:S(2)}, u32[]{:S(2)}) %collective-permute-start.33) | collective-permute-done | bytes 528416 | tf_op jit(solution)/shard_map/ppermute | solution.py:837
  182.5 5.7 %collective-permute-done.36.received = s16[2064,128]{1,0:T(8,128)(2,1)S(1)} collective-permute-done((s16[2064,128]{1,0:T(8,128)(2,1)S(1)}, s16[2064,128]{1,0:T(8,128)(2,1)S(1)}, u32[]{:S(2)}, u32[]{:S(2)}) %collective-permute-start.36) | collective-permute-done | bytes 528416 | tf_op jit(solution)/shard_map/ppermute | solution.py:837
  189.9 10.3 %collective-permute-done.35.received = s16[2064,128]{1,0:T(8,128)(2,1)S(1)} collective-permute-done((s16[2064,128]{1,0:T(8,128)(2,1)S(1)}, s16[2064,128]{1,0:T(8,128)(2,1)S(1)}, u32[]{:S(2)}, u32[]{:S(2)}) %collective-permute-start.35) | collective-permute-done | bytes 528416 | tf_op jit(solution)/shard_map/ppermute | solution.py:837
  200.2 2.3 %place_chunk.15 = (f32[2048,1024]{1,0:T(8,128)}, f32[8,128]{1,0:T(8,128)}) custom-call(s32[4]{0:T(128)S(1)} %pad_add_fusion.place.place_ref, s16[2064,128]{1,0:T(8,128)(2,1)S(1)} %add_chunk.31.refs_0_.total, s16[2064,128]{1,0:T(8,128)(2,1)S(1)} %collective-permute-done.35.received, ...), custom_call_target="tpu_custom_call", output_to_operand_aliasing={{0}: (4, {})} | custom-call | flops 1 | bytes 1 | tf_op jit(solution)/shard_map/place_chunk/pallas_call | solution.py:641
  (131 shorter events, 66.6 us)
Async XLA Ops:
  2.1 37.4 %collective-permute-start = (bf16[8,96,1024]{2,1,0:T(8,128)(2,1)S(1)}, bf16[8,96,1024]{2,1,0:T(8,128)(2,1)S(1)}, u32[]{:S(2)}, u32[]{:S(2)}) collective-permute-start(bf16[8,96,1024]{2,1,0:T(8,128)(2,1)S(1)} %section_share.2.refs_0_), channel_id=1, source_target_pairs={{0,2},{2,0},{1,3},{3,1},{4,6},{6,4},{5,7},{7,5},{8,10},{10,8},{9,1... | collective-permute-start | bytes 4718600 | tf_op jit(solution)/shard_map/ppermute | solution.py:747
  39.5 14.5 %collective-permute-start.2 = (bf16[2,128,1024]{2,1,0:T(8,128)(2,1)}, bf16[2,128,1024]{2,1,0:T(8,128)(2,1)S(1)}, u32[]{:S(2)}, u32[]{:S(2)}) collective-permute-start(bf16[2,128,1024]{2,1,0:T(8,128)(2,1)} %section_share.3.refs_1_), channel_id=1, source_target_pairs={{0,2},{2,0},{1,3},{3,1},{4,6},{6,4},{5,7},{7,5},{8,10},{10,8},{9,1... | collective-permute-start | bytes 1572872 | tf_op jit(solution)/shard_map/ppermute | solution.py:747
  54.1 5.2 %collective-permute-start.5 = (f32[8,24,96]{2,1,0:T(8,128)S(1)}, f32[8,24,96]{2,1,0:T(8,128)S(1)}, u32[]{:S(2)}, u32[]{:S(2)}) collective-permute-start(f32[8,24,96]{2,1,0:T(8,128)S(1)} %get-tuple-element.47), channel_id=1, source_target_pairs={{0,2},{2,0},{1,3},{3,1},{4,6},{6,4},{5,7},{7,5},{8,10},{10,8},{9,1... | collective-permute-start | bytes 221192 | tf_op jit(solution)/shard_map/ppermute | solution.py:765
  59.3 4.2 %collective-permute-start.11 = (f32[4,24,128]{2,1,0:T(8,128)S(1)}, f32[4,24,128]{2,1,0:T(8,128)S(1)}, u32[]{:S(2)}, u32[]{:S(2)}) collective-permute-start(f32[4,24,128]{2,1,0:T(8,128)S(1)} %get-tuple-element.48.refs_8_.refs_0_), channel_id=1, source_target_pairs={{0,2},{2,0},{1,3},{3,1},{4,6},{6,4},{5,7},{7,5},{8,10},{10,8},{9,1... | collective-permute-start | bytes 147464 | tf_op jit(solution)/shard_map/ppermute | solution.py:770
  61.0 8.2 %collective-permute-start.10 = (f32[4,24,128]{2,1,0:T(8,128)S(1)}, f32[4,24,128]{2,1,0:T(8,128)S(1)}, u32[]{:S(2)}, u32[]{:S(2)}) collective-permute-start(f32[4,24,128]{2,1,0:T(8,128)S(1)} %get-tuple-element.48.refs_8_.refs_0_), channel_id=1, source_target_pairs={{0,1},{1,0},{2,3},{3,2},{4,5},{5,4},{6,7},{7,6},{8,9},{9,8},{10,11... | collective-permute-start | bytes 147464 | tf_op jit(solution)/shard_map/ppermute | solution.py:771
  63.4 5.8 %collective-permute-start.12 = (f32[4,24,128]{2,1,0:T(8,128)S(1)}, f32[4,24,128]{2,1,0:T(8,128)S(1)}, u32[]{:S(2)}, u32[]{:S(2)}) collective-permute-start(f32[4,24,128]{2,1,0:T(8,128)S(1)} %collective-permute-done.11.refs_2_), channel_id=1, source_target_pairs={{0,1},{1,0},{2,3},{3,2},{4,5},{5,4},{6,7},{7,6},{8,9},{9,8},{10,11... | collective-permute-start | bytes 147464 | tf_op jit(solution)/shard_map/ppermute | solution.py:791
  63.4 7.4 %collective-permute-start.9 = (f32[72,96]{1,0:T(8,128)S(1)}, f32[72,96]{1,0:T(8,128)S(1)}, u32[]{:S(2)}, u32[]{:S(2)}) collective-permute-start(f32[72,96]{1,0:T(8,128)S(1)} %get-tuple-element.50.refs_11_.refs_0_), channel_id=1, source_target_pairs={{0,4},{4,8},{8,12},{12,0},{1,5},{5,9},{9,13},{13,1},{2,6},{6,10},{... | collective-permute-start | bytes 82952 | tf_op jit(solution)/shard_map/ppermute | solution.py:790
  65.3 5.5 %collective-permute-start.8 = (f32[72,96]{1,0:T(8,128)S(1)}, f32[72,96]{1,0:T(8,128)S(1)}, u32[]{:S(2)}, u32[]{:S(2)}) collective-permute-start(f32[72,96]{1,0:T(8,128)S(1)} %get-tuple-element.50.refs_11_.refs_0_), channel_id=1, source_target_pairs={{0,8},{4,12},{8,0},{12,4},{1,9},{5,13},{9,1},{13,5},{2,10},{6,14},... | collective-permute-start | bytes 82952 | tf_op jit(solution)/shard_map/ppermute | solution.py:790
  75.8 15.6 %collective-permute-start.13 = (s16[2064,128]{1,0:T(8,128)(2,1)S(1)}, s16[2064,128]{1,0:T(8,128)(2,1)S(1)}, u32[]{:S(2)}, u32[]{:S(2)}) collective-permute-start(s16[2064,128]{1,0:T(8,128)(2,1)S(1)} %grad_chunk.8.refs_4_.refs_0_), channel_id=1, source_target_pairs={{0,4},{12,8},{1,5},{13,9},{2,6},{14,10},{3,7},{15,11},{16,20},{28,... | collective-permute-start | bytes 1585160 | tf_op jit(solution)/shard_map/ppermute | solution.py:831
  80.7 23.3 %collective-permute-start.14 = (s16[2064,128]{1,0:T(8,128)(2,1)S(1)}, s16[2064,128]{1,0:T(8,128)(2,1)S(1)}, u32[]{:S(2)}, u32[]{:S(2)}) collective-permute-start(s16[2064,128]{1,0:T(8,128)(2,1)S(1)} %grad_chunk.9.refs_4_.refs_0_), channel_id=1, source_target_pairs={{0,4},{12,8},{1,5},{13,9},{2,6},{14,10},{3,7},{15,11},{16,20},{28,... | collective-permute-start | bytes 1585160 | tf_op jit(solution)/shard_map/ppermute | solution.py:831
  92.6 13.3 %collective-permute-start.17 = (s16[2064,128]{1,0:T(8,128)(2,1)S(1)}, s16[2064,128]{1,0:T(8,128)(2,1)S(1)}, u32[]{:S(2)}, u32[]{:S(2)}) collective-permute-start(s16[2064,128]{1,0:T(8,128)(2,1)S(1)} %add_chunk.16.refs_6_.refs_0_), channel_id=1, source_target_pairs={{4,8},{8,4},{5,9},{9,5},{6,10},{10,6},{7,11},{11,7},{20,24},{24,20... | collective-permute-start | bytes 1585160 | tf_op jit(solution)/shard_map/ppermute | solution.py:834
  93.3 20.0 %collective-permute-start.16 = (s16[2064,128]{1,0:T(8,128)(2,1)S(1)}, s16[2064,128]{1,0:T(8,128)(2,1)S(1)}, u32[]{:S(2)}, u32[]{:S(2)}) collective-permute-start(s16[2064,128]{1,0:T(8,128)(2,1)S(1)} %grad_chunk.10.refs_4_.refs_0_), channel_id=1, source_target_pairs={{0,4},{12,8},{1,5},{13,9},{2,6},{14,10},{3,7},{15,11},{16,20},{28,... | collective-permute-start | bytes 1585160 | tf_op jit(solution)/shard_map/ppermute | solution.py:831
  105.2 10.0 %collective-permute-start.15 = (s16[2064,128]{1,0:T(8,128)(2,1)S(1)}, s16[2064,128]{1,0:T(8,128)(2,1)S(1)}, u32[]{:S(2)}, u32[]{:S(2)}) collective-permute-start(s16[2064,128]{1,0:T(8,128)(2,1)S(1)} %add_chunk.17.refs_2_.refs_0_), channel_id=1, source_target_pairs={{4,8},{8,4},{5,9},{9,5},{6,10},{10,6},{7,11},{11,7},{20,24},{24,20... | collective-permute-start | bytes 1585160 | tf_op jit(solution)/shard_map/ppermute | solution.py:834
  107.0 16.9 %collective-permute-start.22 = (s16[2064,128]{1,0:T(8,128)(2,1)S(1)}, s16[2064,128]{1,0:T(8,128)(2,1)S(1)}, u32[]{:S(2)}, u32[]{:S(2)}) collective-permute-start(s16[2064,128]{1,0:T(8,128)(2,1)S(1)} %add_chunk.18.refs_2_.total), channel_id=1, source_target_pairs={{4,0},{8,12},{5,1},{9,13},{6,2},{10,14},{7,3},{11,15},{20,16},{24,... | collective-permute-start | bytes 1585160 | tf_op jit(solution)/shard_map/ppermute | solution.py:837
  108.3 17.3 %collective-permute-start.21 = (s16[2064,128]{1,0:T(8,128)(2,1)S(1)}, s16[2064,128]{1,0:T(8,128)(2,1)S(1)}, u32[]{:S(2)}, u32[]{:S(2)}) collective-permute-start(s16[2064,128]{1,0:T(8,128)(2,1)S(1)} %grad_chunk.11.refs_6_.refs_0_), channel_id=1, source_target_pairs={{0,4},{12,8},{1,5},{13,9},{2,6},{14,10},{3,7},{15,11},{16,20},{28,... | collective-permute-start | bytes 1585160 | tf_op jit(solution)/shard_map/ppermute | solution.py:840
  114.5 13.1 %collective-permute-start.20 = (s16[2064,128]{1,0:T(8,128)(2,1)S(1)}, s16[2064,128]{1,0:T(8,128)(2,1)S(1)}, u32[]{:S(2)}, u32[]{:S(2)}) collective-permute-start(s16[2064,128]{1,0:T(8,128)(2,1)S(1)} %add_chunk.19.refs_2_.refs_0_), channel_id=1, source_target_pairs={{4,8},{8,4},{5,9},{9,5},{6,10},{10,6},{7,11},{11,7},{20,24},{24,20... | collective-permute-start | bytes 1585160 | tf_op jit(solution)/shard_map/ppermute | solution.py:834
  116.3 19.8 %collective-permute-start.19 = (s16[2064,128]{1,0:T(8,128)(2,1)S(1)}, s16[2064,128]{1,0:T(8,128)(2,1)S(1)}, u32[]{:S(2)}, u32[]{:S(2)}) collective-permute-start(s16[2064,128]{1,0:T(8,128)(2,1)S(1)} %add_chunk.20.refs_0_.total), channel_id=1, source_target_pairs={{4,0},{8,12},{5,1},{9,13},{6,2},{10,14},{7,3},{11,15},{20,16},{24,... | collective-permute-start | bytes 1585160 | tf_op jit(solution)/shard_map/ppermute | solution.py:837
  117.6 20.2 %collective-permute-start.18 = (s16[2064,128]{1,0:T(8,128)(2,1)S(1)}, s16[2064,128]{1,0:T(8,128)(2,1)S(1)}, u32[]{:S(2)}, u32[]{:S(2)}) collective-permute-start(s16[2064,128]{1,0:T(8,128)(2,1)S(1)} %grad_chunk.12.refs_6_.refs_0_), channel_id=1, source_target_pairs={{0,4},{12,8},{1,5},{13,9},{2,6},{14,10},{3,7},{15,11},{16,20},{28,... | collective-permute-start | bytes 1585160 | tf_op jit(solution)/shard_map/ppermute | solution.py:840
  126.8 12.9 %collective-permute-start.26 = (s16[2064,128]{1,0:T(8,128)(2,1)S(1)}, s16[2064,128]{1,0:T(8,128)(2,1)S(1)}, u32[]{:S(2)}, u32[]{:S(2)}) collective-permute-start(s16[2064,128]{1,0:T(8,128)(2,1)S(1)} %add_chunk.21.refs_2_.refs_0_), channel_id=1, source_target_pairs={{4,8},{8,4},{5,9},{9,5},{6,10},{10,6},{7,11},{11,7},{20,24},{24,20... | collective-permute-start | bytes 1585160 | tf_op jit(solution)/shard_map/ppermute | solution.py:834
  128.7 18.7 %collective-permute-start.25 = (s16[2064,128]{1,0:T(8,128)(2,1)S(1)}, s16[2064,128]{1,0:T(8,128)(2,1)S(1)}, u32[]{:S(2)}, u32[]{:S(2)}) collective-permute-start(s16[2064,128]{1,0:T(8,128)(2,1)S(1)} %add_chunk.22.refs_0_.total), channel_id=1, source_target_pairs={{4,0},{8,12},{5,1},{9,13},{6,2},{10,14},{7,3},{11,15},{20,16},{24,... | collective-permute-start | bytes 1585160 | tf_op jit(solution)/shard_map/ppermute | solution.py:837
  130.0 19.1 %collective-permute-start.24 = (s16[2064,128]{1,0:T(8,128)(2,1)S(1)}, s16[2064,128]{1,0:T(8,128)(2,1)S(1)}, u32[]{:S(2)}, u32[]{:S(2)}) collective-permute-start(s16[2064,128]{1,0:T(8,128)(2,1)S(1)} %grad_chunk.13.refs_2_.refs_0_), channel_id=1, source_target_pairs={{0,4},{12,8},{1,5},{13,9},{2,6},{14,10},{3,7},{15,11},{16,20},{28,... | collective-permute-start | bytes 1585160 | tf_op jit(solution)/shard_map/ppermute | solution.py:840
  139.0 12.0 %collective-permute-start.23 = (s16[2064,128]{1,0:T(8,128)(2,1)S(1)}, s16[2064,128]{1,0:T(8,128)(2,1)S(1)}, u32[]{:S(2)}, u32[]{:S(2)}) collective-permute-start(s16[2064,128]{1,0:T(8,128)(2,1)S(1)} %add_chunk.23.refs_2_.refs_0_), channel_id=1, source_target_pairs={{4,8},{8,4},{5,9},{9,5},{6,10},{10,6},{7,11},{11,7},{20,24},{24,20... | collective-permute-start | bytes 1585160 | tf_op jit(solution)/shard_map/ppermute | solution.py:834
  140.8 18.2 %collective-permute-start.31 = (s16[2064,128]{1,0:T(8,128)(2,1)S(1)}, s16[2064,128]{1,0:T(8,128)(2,1)S(1)}, u32[]{:S(2)}, u32[]{:S(2)}) collective-permute-start(s16[2064,128]{1,0:T(8,128)(2,1)S(1)} %add_chunk.24.refs_0_.total), channel_id=1, source_target_pairs={{4,0},{8,12},{5,1},{9,13},{6,2},{10,14},{7,3},{11,15},{20,16},{24,... | collective-permute-start | bytes 1585160 | tf_op jit(solution)/shard_map/ppermute | solution.py:837
  142.1 18.9 %collective-permute-start.30 = (s16[2064,128]{1,0:T(8,128)(2,1)S(1)}, s16[2064,128]{1,0:T(8,128)(2,1)S(1)}, u32[]{:S(2)}, u32[]{:S(2)}) collective-permute-start(s16[2064,128]{1,0:T(8,128)(2,1)S(1)} %grad_chunk.14.refs_6_.refs_0_), channel_id=1, source_target_pairs={{0,4},{12,8},{1,5},{13,9},{2,6},{14,10},{3,7},{15,11},{16,20},{28,... | collective-permute-start | bytes 1585160 | tf_op jit(solution)/shard_map/ppermute | solution.py:840
  150.3 12.6 %collective-permute-start.29 = (s16[2064,128]{1,0:T(8,128)(2,1)S(1)}, s16[2064,128]{1,0:T(8,128)(2,1)S(1)}, u32[]{:S(2)}, u32[]{:S(2)}) collective-permute-start(s16[2064,128]{1,0:T(8,128)(2,1)S(1)} %add_chunk.25.refs_2_.refs_0_), channel_id=1, source_target_pairs={{4,8},{8,4},{5,9},{9,5},{6,10},{10,6},{7,11},{11,7},{20,24},{24,20... | collective-permute-start | bytes 1585160 | tf_op jit(solution)/shard_map/ppermute | solution.py:834
  152.2 14.5 %collective-permute-start.28 = (s16[2064,128]{1,0:T(8,128)(2,1)S(1)}, s16[2064,128]{1,0:T(8,128)(2,1)S(1)}, u32[]{:S(2)}, u32[]{:S(2)}) collective-permute-start(s16[2064,128]{1,0:T(8,128)(2,1)S(1)} %add_chunk.26.refs_0_.total), channel_id=1, source_target_pairs={{4,0},{8,12},{5,1},{9,13},{6,2},{10,14},{7,3},{11,15},{20,16},{24,... | collective-permute-start | bytes 1585160 | tf_op jit(solution)/shard_map/ppermute | solution.py:837
  153.5 15.4 %collective-permute-start.27 = (s16[2064,128]{1,0:T(8,128)(2,1)S(1)}, s16[2064,128]{1,0:T(8,128)(2,1)S(1)}, u32[]{:S(2)}, u32[]{:S(2)}) collective-permute-start(s16[2064,128]{1,0:T(8,128)(2,1)S(1)} %grad_chunk.15.refs_2_.refs_0_), channel_id=1, source_target_pairs={{0,4},{12,8},{1,5},{13,9},{2,6},{14,10},{3,7},{15,11},{16,20},{28,... | collective-permute-start | bytes 1585160 | tf_op jit(solution)/shard_map/ppermute | solution.py:840
  162.2 8.6 %collective-permute-start.34 = (s16[2064,128]{1,0:T(8,128)(2,1)S(1)}, s16[2064,128]{1,0:T(8,128)(2,1)S(1)}, u32[]{:S(2)}, u32[]{:S(2)}) collective-permute-start(s16[2064,128]{1,0:T(8,128)(2,1)S(1)} %add_chunk.27.refs_2_.refs_0_), channel_id=1, source_target_pairs={{4,8},{8,4},{5,9},{9,5},{6,10},{10,6},{7,11},{11,7},{20,24},{24,20... | collective-permute-start | bytes 1585160 | tf_op jit(solution)/shard_map/ppermute | solution.py:834
  164.1 14.3 %collective-permute-start.33 = (s16[2064,128]{1,0:T(8,128)(2,1)S(1)}, s16[2064,128]{1,0:T(8,128)(2,1)S(1)}, u32[]{:S(2)}, u32[]{:S(2)}) collective-permute-start(s16[2064,128]{1,0:T(8,128)(2,1)S(1)} %add_chunk.28.refs_0_.total), channel_id=1, source_target_pairs={{4,0},{8,12},{5,1},{9,13},{6,2},{10,14},{7,3},{11,15},{20,16},{24,... | collective-permute-start | bytes 1585160 | tf_op jit(solution)/shard_map/ppermute | solution.py:837
  170.1 10.0 %collective-permute-start.32 = (s16[2064,128]{1,0:T(8,128)(2,1)S(1)}, s16[2064,128]{1,0:T(8,128)(2,1)S(1)}, u32[]{:S(2)}, u32[]{:S(2)}) collective-permute-start(s16[2064,128]{1,0:T(8,128)(2,1)S(1)} %add_chunk.29.refs_2_.refs_0_), channel_id=1, source_target_pairs={{4,8},{8,4},{5,9},{9,5},{6,10},{10,6},{7,11},{11,7},{20,24},{24,20... | collective-permute-start | bytes 1585160 | tf_op jit(solution)/shard_map/ppermute | solution.py:834
  171.9 16.3 %collective-permute-start.36 = (s16[2064,128]{1,0:T(8,128)(2,1)S(1)}, s16[2064,128]{1,0:T(8,128)(2,1)S(1)}, u32[]{:S(2)}, u32[]{:S(2)}) collective-permute-start(s16[2064,128]{1,0:T(8,128)(2,1)S(1)} %add_chunk.30.refs_0_.total), channel_id=1, source_target_pairs={{4,0},{8,12},{5,1},{9,13},{6,2},{10,14},{7,3},{11,15},{20,16},{24,... | collective-permute-start | bytes 1585160 | tf_op jit(solution)/shard_map/ppermute | solution.py:837
  181.2 19.0 %collective-permute-start.35 = (s16[2064,128]{1,0:T(8,128)(2,1)S(1)}, s16[2064,128]{1,0:T(8,128)(2,1)S(1)}, u32[]{:S(2)}, u32[]{:S(2)}) collective-permute-start(s16[2064,128]{1,0:T(8,128)(2,1)S(1)} %add_chunk.31.refs_0_.total), channel_id=1, source_target_pairs={{4,0},{8,12},{5,1},{9,13},{6,2},{10,14},{7,3},{11,15},{20,16},{24,... | collective-permute-start | bytes 1585160 | tf_op jit(solution)/shard_map/ppermute | solution.py:837
  (19 other events, 134.5 us)

commit v4 on v3

--- a/solution.py
+++ b/solution.py
@@ -194,7 +194,7 @@
 ADD_BLOCKS = 2
 ROW_GROUPS = 4
 GRAD_CHUNKS = 8
-GRAD_LEAD = 6
+GRAD_LEAD = 7
 SEND_LEAD = 3
 LANES = 128
 CODE_LIMIT = 32512.0

time: 203 us -> 206 us (1.015)
  starting transfers between devices: 68.2 us -> 70.7 us
    ppermute x5, starting transfers between devices: 28 us -> 32.8 us  [line_plan(): inward[ahead] = lax.ppermute(after(messages[ahead], last), 'dp', TO_CENTER)]
    ppermute x3, starting transfers between devices: 9.83 us -> 7.48 us  [line_plan(): inward[k] = lax.ppermute(last, 'dp', TO_CENTER)]
  transfers between devices with their start and end apart: 37 -> 37, of which waited for: 14 -> 13; matrix products, arithmetic and copies ran while one was open for 0% -> 0% of each run, Pallas kernels for 37% -> 36%
where the time goes in v4:
time: 206 us; the launch traced here: 205 us
  Pallas kernels  82.5 us (40%)
  starting transfers between devices  70.7 us (34%)
  waiting for transfers between devices  48 us (23%)
  local copies, waits for them, and re-layouts  3.02 us (1%)
    pallas_call x28, Pallas kernels, vmem_call(): pl.pallas_call(run, in_specs=[SMEM] + [VMEM] * len(operands), out_specs=[...  41.6 us
    ppermute x5, starting transfers between devices, line_plan(): inward[ahead] = lax.ppermute(after(messages[ahead], last), 'dp', TO_CENTER)  32.8 us
    ppermute x8, waiting for transfers between devices, line_plan(): outward[k] = lax.ppermute(last, 'dp', FROM_CENTER)  23.2 us
    ppermute x2, waiting for transfers between devices, line_plan(): got = [lax.ppermute(half, 'mp', SWAP) for half in halves]  18.3 us
    pallas_call x8, Pallas kernels, place_chunk(): pl.pallas_call(functools.partial(place_body, hidden_count // LANES, rows,...  14.3 us
    pallas_call x2, Pallas kernels, own_half(): pl.pallas_call(own_half_body, in_specs=[SMEM, HBM] + [VMEM] * len(operand...  13 us
    ppermute x8, starting transfers between devices, line_plan(): outward[k] = lax.ppermute(last, 'dp', FROM_CENTER)  10.3 us
    pallas_call x2, Pallas kernels, forward(): pl.pallas_call(forward_body, in_specs=[SMEM] + [VMEM] * len(operands), ou...  9.16 us
  transfers between devices with their start and end apart: 37, of which 13 were waited for; matrix products, arithmetic and copies ran while one was open for 0% of the time, Pallas kernels for 36%

profile of v4, /device:TPU:0, one launch (start us, length us, event | category | flops | bytes accessed | tf_op | source)
XLA Modules:
  0.0 205.4 jit_solution(4450607670153934074)
XLA Ops:
  0.1 2.0 section_share.2.refs_0_
  2.1 3.0 %collective-permute-start = (bf16[8,96,1024]{2,1,0:T(8,128)(2,1)S(1)}, bf16[8,96,1024]{2,1,0:T(8,128)(2,1)S(1)}, u32[]{:S(2)}, u32[]{:S(2)}) collective-permute-start(bf16[8,96,1024]{2,1,0:T(8,128)(2,1)S(1)} %section_share.2.refs_0_), channel_id=1, source_target_pairs={{0,2},{2,0},{1,3},{3,1},{4,6},{6,4},{5,7},{7,5},{8,10},{10,8},{9,1... | collective-permute-start | bytes 4718600 | tf_op jit(solution)/shard_map/ppermute | solution.py:747
  5.1 2.4 %section_share.3.refs_1_ = bf16[2,128,1024]{2,1,0:T(8,128)(2,1)} custom-call(s32[4]{0:T(128)S(1)} %pad_add_fusion.place.place_ref, bf16[4,128,1024]{2,1,0:T(8,128)(2,1)} %bitcast.15, bf16[8,96,1024]{2,1,0:T(8,128)(2,1)S(1)} %section_share.2.refs_0_), custom_call_target="tpu_custom_call" | custom-call | flops 1 | bytes 1 | tf_op jit(solution)/shard_map/section_share/pallas_call | solution.py:257
  8.5 2.2 %copy-done = bf16[1,2048,1024]{2,1,0:T(8,128)(2,1)S(1)} copy-done((bf16[1,2048,1024]{2,1,0:T(8,128)(2,1)S(1)}, bf16[1,2048,1024]{2,1,0:T(8,128)(2,1)}, u32[]{:S(2)}) %copy-start) | copy-done | bytes 4194328
  10.7 9.4 %own_half.2 = (bf16[16,96,1024]{2,1,0:T(8,128)(2,1)S(1)}, f32[16,96,1024]{2,1,0:T(8,128)S(1)}) custom-call(s32[4]{0:T(128)S(1)} %pad_add_fusion.place.place_ref, bf16[16,96,1024]{2,1,0:T(8,128)(2,1)} %source.3, bf16[2048,1024]{1,0:T(8,128)(2,1)S(1)} %bitcast.11, bf16[8,96,1024]{2,1,0:T(8,128)(2,1)S(1)} %section_share.2.refs_0_, ...), custom_call_target="tpu_custom_call" | custom-call | flops 1 | bytes 1 | tf_op jit(solution)/shard_map/own_half/pallas_call | solution.py:295
  20.2 3.6 %own_half.3 = (bf16[4,128,1024]{2,1,0:T(8,128)(2,1)S(1)}, f32[4,128,1024]{2,1,0:T(8,128)S(1)}) custom-call(s32[4]{0:T(128)S(1)} %pad_add_fusion.place.place_ref, bf16[4,128,1024]{2,1,0:T(8,128)(2,1)} %bitcast.16, bf16[2048,1024]{1,0:T(8,128)(2,1)S(1)} %bitcast.12, f32[16,96,1024]{2,1,0:T(8,128)S(1)} %get-tuple-element.41.refs_0_.pre_ref), custom_call_target="tpu_custom_call" | custom-call | flops 1 | bytes 1 | tf_op jit(solution)/shard_map/own_half/pallas_call | solution.py:295
  23.7 15.8 %collective-permute-done.got_ref.refs_0_ = bf16[8,96,1024]{2,1,0:T(8,128)(2,1)S(1)} collective-permute-done((bf16[8,96,1024]{2,1,0:T(8,128)(2,1)S(1)}, bf16[8,96,1024]{2,1,0:T(8,128)(2,1)S(1)}, u32[]{:S(2)}, u32[]{:S(2)}) %collective-permute-start) | collective-permute-done | bytes 1572896 | tf_op jit(solution)/shard_map/ppermute | solution.py:747
  42.9 6.5 %forward_rows.2 = (f32[16,96,1024]{2,1,0:T(8,128)S(1)}, f32[16,24,96]{2,1,0:T(8,128)S(1)}) custom-call(s32[4]{0:T(128)S(1)} %pad_add_fusion.place.place_ref, f32[16,96,1024]{2,1,0:T(8,128)S(1)} %get-tuple-element.41.refs_0_.pre_ref, bf16[8,96,1024]{2,1,0:T(8,128)(2,1)S(1)} %collective-permute-done.got_ref.refs_0_, ...), custom_call_target="tpu_custom_call", output_to_operand_aliasing={{0}: (1, {})} | custom-call | flops 1 | bytes 1 | tf_op jit(solution)/shard_map/forward_rows/pallas_call | solution.py:347
  51.5 2.6 %collective-permute-done.2.got_ref.refs_2_ = bf16[2,128,1024]{2,1,0:T(8,128)(2,1)S(1)} collective-permute-done((bf16[2,128,1024]{2,1,0:T(8,128)(2,1)}, bf16[2,128,1024]{2,1,0:T(8,128)(2,1)S(1)}, u32[]{:S(2)}, u32[]{:S(2)}) %collective-permute-start.2) | collective-permute-done | bytes 524320 | tf_op jit(solution)/shard_map/ppermute | solution.py:747
  56.0 2.7 %forward_rows.3 = (f32[4,128,1024]{2,1,0:T(8,128)S(1)}, f32[4,24,128]{2,1,0:T(8,128)S(1)}) custom-call(s32[4]{0:T(128)S(1)} %pad_add_fusion.place.place_ref, f32[4,128,1024]{2,1,0:T(8,128)S(1)} %get-tuple-element.42.pre_ref, bf16[2,128,1024]{2,1,0:T(8,128)(2,1)S(1)} %collective-permute-done.2.got_ref.refs_2_, ...), custom_call_target="tpu_custom_call", output_to_operand_aliasing={{0}: (1, {})} | custom-call | flops 1 | bytes 1 | tf_op jit(solution)/shard_map/forward_rows/pallas_call | solution.py:347
  65.3 2.6 %collective-permute-start.8 = (f32[72,96]{1,0:T(8,128)S(1)}, f32[72,96]{1,0:T(8,128)S(1)}, u32[]{:S(2)}, u32[]{:S(2)}) collective-permute-start(f32[72,96]{1,0:T(8,128)S(1)} %get-tuple-element.50.refs_11_.refs_0_), channel_id=1, source_target_pairs={{0,8},{4,12},{8,0},{12,4},{1,9},{5,13},{9,1},{13,5},{2,10},{6,14},... | collective-permute-start | bytes 82952 | tf_op jit(solution)/shard_map/ppermute | solution.py:790
  73.5 2.3 %grad_chunk.8.refs_4_.refs_0_ = s16[2064,128]{1,0:T(8,128)(2,1)S(1)} custom-call(s32[4]{0:T(128)S(1)} %pad_add_fusion.place.place_ref, bf16[16,96,1024]{2,1,0:T(8,128)(2,1)S(1)} %get-tuple-element.55.refs_0_, bf16[4,128,1024]{2,1,0:T(8,128)(2,1)S(1)} %get-tuple-element.56.refs_1_, bf16[16,96,1024]{2,1,0:T(8,128)(2,1)S(1)} %online_back.1.refs_2_.refs_4_, ...), custom_call_target="tpu_custom_call" | custom-call | flops 1 | bytes 1 | tf_op jit(solution)/shard_map/grad_chunk/pallas_call | solution.py:231
  75.8 2.5 %collective-permute-start.13 = (s16[2064,128]{1,0:T(8,128)(2,1)S(1)}, s16[2064,128]{1,0:T(8,128)(2,1)S(1)}, u32[]{:S(2)}, u32[]{:S(2)}) collective-permute-start(s16[2064,128]{1,0:T(8,128)(2,1)S(1)} %grad_chunk.8.refs_4_.refs_0_), channel_id=1, source_target_pairs={{0,4},{12,8},{1,5},{13,9},{2,6},{14,10},{3,7},{15,11},{16,20},{28,... | collective-permute-start | bytes 1585160 | tf_op jit(solution)/shard_map/ppermute | solution.py:831
  78.3 2.3 %grad_chunk.9.refs_4_.refs_0_ = s16[2064,128]{1,0:T(8,128)(2,1)S(1)} custom-call(s32[4]{0:T(128)S(1)} %pad_add_fusion.place.place_ref, bf16[16,96,1024]{2,1,0:T(8,128)(2,1)S(1)} %get-tuple-element.55.refs_0_, bf16[4,128,1024]{2,1,0:T(8,128)(2,1)S(1)} %get-tuple-element.56.refs_1_, bf16[16,96,1024]{2,1,0:T(8,128)(2,1)S(1)} %online_back.1.refs_2_.refs_4_, ...), custom_call_target="tpu_custom_call" | custom-call | flops 1 | bytes 1 | tf_op jit(solution)/shard_map/grad_chunk/pallas_call | solution.py:231
  82.0 2.4 %grad_chunk.10.refs_4_.refs_0_ = s16[2064,128]{1,0:T(8,128)(2,1)S(1)} custom-call(s32[4]{0:T(128)S(1)} %pad_add_fusion.place.place_ref, bf16[16,96,1024]{2,1,0:T(8,128)(2,1)S(1)} %get-tuple-element.55.refs_0_, bf16[4,128,1024]{2,1,0:T(8,128)(2,1)S(1)} %get-tuple-element.56.refs_1_, bf16[16,96,1024]{2,1,0:T(8,128)(2,1)S(1)} %online_back.1.refs_2_.refs_4_, ...), custom_call_target="tpu_custom_call" | custom-call | flops 1 | bytes 1 | tf_op jit(solution)/shard_map/grad_chunk/pallas_call | solution.py:231
  84.4 2.3 %grad_chunk.11.refs_6_.refs_0_ = s16[2064,128]{1,0:T(8,128)(2,1)S(1)} custom-call(s32[4]{0:T(128)S(1)} %pad_add_fusion.place.place_ref, bf16[16,96,1024]{2,1,0:T(8,128)(2,1)S(1)} %get-tuple-element.55.refs_0_, bf16[4,128,1024]{2,1,0:T(8,128)(2,1)S(1)} %get-tuple-element.56.refs_1_, bf16[16,96,1024]{2,1,0:T(8,128)(2,1)S(1)} %online_back.1.refs_2_.refs_4_, ...), custom_call_target="tpu_custom_call" | custom-call | flops 1 | bytes 1 | tf_op jit(solution)/shard_map/grad_chunk/pallas_call | solution.py:231
  86.7 2.3 %grad_chunk.12.refs_6_.refs_0_ = s16[2064,128]{1,0:T(8,128)(2,1)S(1)} custom-call(s32[4]{0:T(128)S(1)} %pad_add_fusion.place.place_ref, bf16[8,96,1024]{2,1,0:T(8,128)(2,1)S(1)} %collective-permute-done.got_ref.refs_0_, bf16[8,96,1024]{2,1,0:T(8,128)(2,1)S(1)} %collective-permute-done.1.rest_ref.refs_1_, ...), custom_call_target="tpu_custom_call" | custom-call | flops 1 | bytes 1 | tf_op jit(solution)/shard_map/grad_chunk/pallas_call | solution.py:231
  89.0 2.3 %grad_chunk.13.refs_6_.refs_0_ = s16[2064,128]{1,0:T(8,128)(2,1)S(1)} custom-call(s32[4]{0:T(128)S(1)} %pad_add_fusion.place.place_ref, bf16[8,96,1024]{2,1,0:T(8,128)(2,1)S(1)} %collective-permute-done.got_ref.refs_0_, bf16[8,96,1024]{2,1,0:T(8,128)(2,1)S(1)} %collective-permute-done.1.rest_ref.refs_1_, ...), custom_call_target="tpu_custom_call" | custom-call | flops 1 | bytes 1 | tf_op jit(solution)/shard_map/grad_chunk/pallas_call | solution.py:231
  91.4 2.4 %grad_chunk.14.refs_2_.refs_0_ = s16[2064,128]{1,0:T(8,128)(2,1)S(1)} custom-call(s32[4]{0:T(128)S(1)} %pad_add_fusion.place.place_ref, bf16[8,96,1024]{2,1,0:T(8,128)(2,1)S(1)} %collective-permute-done.got_ref.refs_0_, bf16[8,96,1024]{2,1,0:T(8,128)(2,1)S(1)} %collective-permute-done.1.rest_ref.refs_1_, ...), custom_call_target="tpu_custom_call" | custom-call | flops 1 | bytes 1 | tf_op jit(solution)/shard_map/grad_chunk/pallas_call | solution.py:231
  95.6 3.6 %collective-permute-start.16 = (s16[2064,128]{1,0:T(8,128)(2,1)S(1)}, s16[2064,128]{1,0:T(8,128)(2,1)S(1)}, u32[]{:S(2)}, u32[]{:S(2)}) collective-permute-start(s16[2064,128]{1,0:T(8,128)(2,1)S(1)} %grad_chunk.10.refs_4_.refs_0_), channel_id=1, source_target_pairs={{0,4},{12,8},{1,5},{13,9},{2,6},{14,10},{3,7},{15,11},{16,20},{28,... | collective-permute-start | bytes 1585160 | tf_op jit(solution)/shard_map/ppermute | solution.py:831
  99.3 2.3 %grad_chunk.15.refs_2_.refs_0_ = s16[2064,128]{1,0:T(8,128)(2,1)S(1)} custom-call(s32[4]{0:T(128)S(1)} %pad_add_fusion.place.place_ref, bf16[8,96,1024]{2,1,0:T(8,128)(2,1)S(1)} %collective-permute-done.got_ref.refs_0_, bf16[8,96,1024]{2,1,0:T(8,128)(2,1)S(1)} %collective-permute-done.1.rest_ref.refs_1_, ...), custom_call_target="tpu_custom_call" | custom-call | flops 1 | bytes 1 | tf_op jit(solution)/shard_map/grad_chunk/pallas_call | solution.py:231
  106.3 9.2 %collective-permute-start.21 = (s16[2064,128]{1,0:T(8,128)(2,1)S(1)}, s16[2064,128]{1,0:T(8,128)(2,1)S(1)}, u32[]{:S(2)}, u32[]{:S(2)}) collective-permute-start(s16[2064,128]{1,0:T(8,128)(2,1)S(1)} %grad_chunk.11.refs_6_.refs_0_), channel_id=1, source_target_pairs={{0,4},{12,8},{1,5},{13,9},{2,6},{14,10},{3,7},{15,11},{16,20},{28,... | collective-permute-start | bytes 1585160 | tf_op jit(solution)/shard_map/ppermute | solution.py:840
  119.9 7.0 %collective-permute-start.18 = (s16[2064,128]{1,0:T(8,128)(2,1)S(1)}, s16[2064,128]{1,0:T(8,128)(2,1)S(1)}, u32[]{:S(2)}, u32[]{:S(2)}) collective-permute-start(s16[2064,128]{1,0:T(8,128)(2,1)S(1)} %grad_chunk.12.refs_6_.refs_0_), channel_id=1, source_target_pairs={{0,4},{12,8},{1,5},{13,9},{2,6},{14,10},{3,7},{15,11},{16,20},{28,... | collective-permute-start | bytes 1585160 | tf_op jit(solution)/shard_map/ppermute | solution.py:840
  132.9 5.3 %collective-permute-start.24 = (s16[2064,128]{1,0:T(8,128)(2,1)S(1)}, s16[2064,128]{1,0:T(8,128)(2,1)S(1)}, u32[]{:S(2)}, u32[]{:S(2)}) collective-permute-start(s16[2064,128]{1,0:T(8,128)(2,1)S(1)} %grad_chunk.13.refs_6_.refs_0_), channel_id=1, source_target_pairs={{0,4},{12,8},{1,5},{13,9},{2,6},{14,10},{3,7},{15,11},{16,20},{28,... | collective-permute-start | bytes 1585160 | tf_op jit(solution)/shard_map/ppermute | solution.py:840
  144.2 5.3 %collective-permute-start.30 = (s16[2064,128]{1,0:T(8,128)(2,1)S(1)}, s16[2064,128]{1,0:T(8,128)(2,1)S(1)}, u32[]{:S(2)}, u32[]{:S(2)}) collective-permute-start(s16[2064,128]{1,0:T(8,128)(2,1)S(1)} %grad_chunk.14.refs_2_.refs_0_), channel_id=1, source_target_pairs={{0,4},{12,8},{1,5},{13,9},{2,6},{14,10},{3,7},{15,11},{16,20},{28,... | collective-permute-start | bytes 1585160 | tf_op jit(solution)/shard_map/ppermute | solution.py:840
  155.5 6.1 %collective-permute-start.27 = (s16[2064,128]{1,0:T(8,128)(2,1)S(1)}, s16[2064,128]{1,0:T(8,128)(2,1)S(1)}, u32[]{:S(2)}, u32[]{:S(2)}) collective-permute-start(s16[2064,128]{1,0:T(8,128)(2,1)S(1)} %grad_chunk.15.refs_2_.refs_0_), channel_id=1, source_target_pairs={{0,4},{12,8},{1,5},{13,9},{2,6},{14,10},{3,7},{15,11},{16,20},{28,... | collective-permute-start | bytes 1585160 | tf_op jit(solution)/shard_map/ppermute | solution.py:840
  161.7 1.9 place_chunk.11
  167.9 2.2 %collective-permute-done.28.received = s16[2064,128]{1,0:T(8,128)(2,1)S(1)} collective-permute-done((s16[2064,128]{1,0:T(8,128)(2,1)S(1)}, s16[2064,128]{1,0:T(8,128)(2,1)S(1)}, u32[]{:S(2)}, u32[]{:S(2)}) %collective-permute-start.28) | collective-permute-done | bytes 528416 | tf_op jit(solution)/shard_map/ppermute | solution.py:837
  176.1 6.1 %collective-permute-done.33.received = s16[2064,128]{1,0:T(8,128)(2,1)S(1)} collective-permute-done((s16[2064,128]{1,0:T(8,128)(2,1)S(1)}, s16[2064,128]{1,0:T(8,128)(2,1)S(1)}, u32[]{:S(2)}, u32[]{:S(2)}) %collective-permute-start.33) | collective-permute-done | bytes 528416 | tf_op jit(solution)/shard_map/ppermute | solution.py:837
  186.4 7.2 %collective-permute-done.36.received = s16[2064,128]{1,0:T(8,128)(2,1)S(1)} collective-permute-done((s16[2064,128]{1,0:T(8,128)(2,1)S(1)}, s16[2064,128]{1,0:T(8,128)(2,1)S(1)}, u32[]{:S(2)}, u32[]{:S(2)}) %collective-permute-start.36) | collective-permute-done | bytes 528416 | tf_op jit(solution)/shard_map/ppermute | solution.py:837
  195.2 7.8 %collective-permute-done.35.received = s16[2064,128]{1,0:T(8,128)(2,1)S(1)} collective-permute-done((s16[2064,128]{1,0:T(8,128)(2,1)S(1)}, s16[2064,128]{1,0:T(8,128)(2,1)S(1)}, u32[]{:S(2)}, u32[]{:S(2)}) %collective-permute-start.35) | collective-permute-done | bytes 528416 | tf_op jit(solution)/shard_map/ppermute | solution.py:837
  203.0 2.3 %place_chunk.15 = (f32[2048,1024]{1,0:T(8,128)}, f32[8,128]{1,0:T(8,128)}) custom-call(s32[4]{0:T(128)S(1)} %pad_add_fusion.place.place_ref, s16[2064,128]{1,0:T(8,128)(2,1)S(1)} %add_chunk.31.refs_0_.total, s16[2064,128]{1,0:T(8,128)(2,1)S(1)} %collective-permute-done.35.received, ...), custom_call_target="tpu_custom_call", output_to_operand_aliasing={{0}: (4, {})} | custom-call | flops 1 | bytes 1 | tf_op jit(solution)/shard_map/place_chunk/pallas_call | solution.py:641
  (131 shorter events, 66.7 us)
Async XLA Ops:
  2.1 37.4 %collective-permute-start = (bf16[8,96,1024]{2,1,0:T(8,128)(2,1)S(1)}, bf16[8,96,1024]{2,1,0:T(8,128)(2,1)S(1)}, u32[]{:S(2)}, u32[]{:S(2)}) collective-permute-start(bf16[8,96,1024]{2,1,0:T(8,128)(2,1)S(1)} %section_share.2.refs_0_), channel_id=1, source_target_pairs={{0,2},{2,0},{1,3},{3,1},{4,6},{6,4},{5,7},{7,5},{8,10},{10,8},{9,1... | collective-permute-start | bytes 4718600 | tf_op jit(solution)/shard_map/ppermute | solution.py:747
  39.5 14.5 %collective-permute-start.2 = (bf16[2,128,1024]{2,1,0:T(8,128)(2,1)}, bf16[2,128,1024]{2,1,0:T(8,128)(2,1)S(1)}, u32[]{:S(2)}, u32[]{:S(2)}) collective-permute-start(bf16[2,128,1024]{2,1,0:T(8,128)(2,1)} %section_share.3.refs_1_), channel_id=1, source_target_pairs={{0,2},{2,0},{1,3},{3,1},{4,6},{6,4},{5,7},{7,5},{8,10},{10,8},{9,1... | collective-permute-start | bytes 1572872 | tf_op jit(solution)/shard_map/ppermute | solution.py:747
  54.1 5.2 %collective-permute-start.5 = (f32[8,24,96]{2,1,0:T(8,128)S(1)}, f32[8,24,96]{2,1,0:T(8,128)S(1)}, u32[]{:S(2)}, u32[]{:S(2)}) collective-permute-start(f32[8,24,96]{2,1,0:T(8,128)S(1)} %get-tuple-element.47), channel_id=1, source_target_pairs={{0,2},{2,0},{1,3},{3,1},{4,6},{6,4},{5,7},{7,5},{8,10},{10,8},{9,1... | collective-permute-start | bytes 221192 | tf_op jit(solution)/shard_map/ppermute | solution.py:765
  59.3 4.2 %collective-permute-start.11 = (f32[4,24,128]{2,1,0:T(8,128)S(1)}, f32[4,24,128]{2,1,0:T(8,128)S(1)}, u32[]{:S(2)}, u32[]{:S(2)}) collective-permute-start(f32[4,24,128]{2,1,0:T(8,128)S(1)} %get-tuple-element.48.refs_8_.refs_0_), channel_id=1, source_target_pairs={{0,2},{2,0},{1,3},{3,1},{4,6},{6,4},{5,7},{7,5},{8,10},{10,8},{9,1... | collective-permute-start | bytes 147464 | tf_op jit(solution)/shard_map/ppermute | solution.py:770
  61.0 8.2 %collective-permute-start.10 = (f32[4,24,128]{2,1,0:T(8,128)S(1)}, f32[4,24,128]{2,1,0:T(8,128)S(1)}, u32[]{:S(2)}, u32[]{:S(2)}) collective-permute-start(f32[4,24,128]{2,1,0:T(8,128)S(1)} %get-tuple-element.48.refs_8_.refs_0_), channel_id=1, source_target_pairs={{0,1},{1,0},{2,3},{3,2},{4,5},{5,4},{6,7},{7,6},{8,9},{9,8},{10,11... | collective-permute-start | bytes 147464 | tf_op jit(solution)/shard_map/ppermute | solution.py:771
  63.4 5.8 %collective-permute-start.12 = (f32[4,24,128]{2,1,0:T(8,128)S(1)}, f32[4,24,128]{2,1,0:T(8,128)S(1)}, u32[]{:S(2)}, u32[]{:S(2)}) collective-permute-start(f32[4,24,128]{2,1,0:T(8,128)S(1)} %collective-permute-done.11.refs_2_), channel_id=1, source_target_pairs={{0,1},{1,0},{2,3},{3,2},{4,5},{5,4},{6,7},{7,6},{8,9},{9,8},{10,11... | collective-permute-start | bytes 147464 | tf_op jit(solution)/shard_map/ppermute | solution.py:791
  63.4 7.4 %collective-permute-start.9 = (f32[72,96]{1,0:T(8,128)S(1)}, f32[72,96]{1,0:T(8,128)S(1)}, u32[]{:S(2)}, u32[]{:S(2)}) collective-permute-start(f32[72,96]{1,0:T(8,128)S(1)} %get-tuple-element.50.refs_11_.refs_0_), channel_id=1, source_target_pairs={{0,4},{4,8},{8,12},{12,0},{1,5},{5,9},{9,13},{13,1},{2,6},{6,10},{... | collective-permute-start | bytes 82952 | tf_op jit(solution)/shard_map/ppermute | solution.py:790
  65.3 5.5 %collective-permute-start.8 = (f32[72,96]{1,0:T(8,128)S(1)}, f32[72,96]{1,0:T(8,128)S(1)}, u32[]{:S(2)}, u32[]{:S(2)}) collective-permute-start(f32[72,96]{1,0:T(8,128)S(1)} %get-tuple-element.50.refs_11_.refs_0_), channel_id=1, source_target_pairs={{0,8},{4,12},{8,0},{12,4},{1,9},{5,13},{9,1},{13,5},{2,10},{6,14},... | collective-permute-start | bytes 82952 | tf_op jit(solution)/shard_map/ppermute | solution.py:790
  75.8 18.0 %collective-permute-start.13 = (s16[2064,128]{1,0:T(8,128)(2,1)S(1)}, s16[2064,128]{1,0:T(8,128)(2,1)S(1)}, u32[]{:S(2)}, u32[]{:S(2)}) collective-permute-start(s16[2064,128]{1,0:T(8,128)(2,1)S(1)} %grad_chunk.8.refs_4_.refs_0_), channel_id=1, source_target_pairs={{0,4},{12,8},{1,5},{13,9},{2,6},{14,10},{3,7},{15,11},{16,20},{28,... | collective-permute-start | bytes 1585160 | tf_op jit(solution)/shard_map/ppermute | solution.py:831
  80.7 21.3 %collective-permute-start.14 = (s16[2064,128]{1,0:T(8,128)(2,1)S(1)}, s16[2064,128]{1,0:T(8,128)(2,1)S(1)}, u32[]{:S(2)}, u32[]{:S(2)}) collective-permute-start(s16[2064,128]{1,0:T(8,128)(2,1)S(1)} %grad_chunk.9.refs_4_.refs_0_), channel_id=1, source_target_pairs={{0,4},{12,8},{1,5},{13,9},{2,6},{14,10},{3,7},{15,11},{16,20},{28,... | collective-permute-start | bytes 1585160 | tf_op jit(solution)/shard_map/ppermute | solution.py:831
  94.9 8.9 %collective-permute-start.17 = (s16[2064,128]{1,0:T(8,128)(2,1)S(1)}, s16[2064,128]{1,0:T(8,128)(2,1)S(1)}, u32[]{:S(2)}, u32[]{:S(2)}) collective-permute-start(s16[2064,128]{1,0:T(8,128)(2,1)S(1)} %add_chunk.16.refs_6_.refs_0_), channel_id=1, source_target_pairs={{4,8},{8,4},{5,9},{9,5},{6,10},{10,6},{7,11},{11,7},{20,24},{24,20... | collective-permute-start | bytes 1585160 | tf_op jit(solution)/shard_map/ppermute | solution.py:834
  95.6 19.9 %collective-permute-start.16 = (s16[2064,128]{1,0:T(8,128)(2,1)S(1)}, s16[2064,128]{1,0:T(8,128)(2,1)S(1)}, u32[]{:S(2)}, u32[]{:S(2)}) collective-permute-start(s16[2064,128]{1,0:T(8,128)(2,1)S(1)} %grad_chunk.10.refs_4_.refs_0_), channel_id=1, source_target_pairs={{0,4},{12,8},{1,5},{13,9},{2,6},{14,10},{3,7},{15,11},{16,20},{28,... | collective-permute-start | bytes 1585160 | tf_op jit(solution)/shard_map/ppermute | solution.py:831
  103.1 14.2 %collective-permute-start.15 = (s16[2064,128]{1,0:T(8,128)(2,1)S(1)}, s16[2064,128]{1,0:T(8,128)(2,1)S(1)}, u32[]{:S(2)}, u32[]{:S(2)}) collective-permute-start(s16[2064,128]{1,0:T(8,128)(2,1)S(1)} %add_chunk.17.refs_2_.refs_0_), channel_id=1, source_target_pairs={{4,8},{8,4},{5,9},{9,5},{6,10},{10,6},{7,11},{11,7},{20,24},{24,20... | collective-permute-start | bytes 1585160 | tf_op jit(solution)/shard_map/ppermute | solution.py:834
  105.0 21.8 %collective-permute-start.22 = (s16[2064,128]{1,0:T(8,128)(2,1)S(1)}, s16[2064,128]{1,0:T(8,128)(2,1)S(1)}, u32[]{:S(2)}, u32[]{:S(2)}) collective-permute-start(s16[2064,128]{1,0:T(8,128)(2,1)S(1)} %add_chunk.18.refs_2_.total), channel_id=1, source_target_pairs={{4,0},{8,12},{5,1},{9,13},{6,2},{10,14},{7,3},{11,15},{20,16},{24,... | collective-permute-start | bytes 1585160 | tf_op jit(solution)/shard_map/ppermute | solution.py:837
  106.3 22.2 %collective-permute-start.21 = (s16[2064,128]{1,0:T(8,128)(2,1)S(1)}, s16[2064,128]{1,0:T(8,128)(2,1)S(1)}, u32[]{:S(2)}, u32[]{:S(2)}) collective-permute-start(s16[2064,128]{1,0:T(8,128)(2,1)S(1)} %grad_chunk.11.refs_6_.refs_0_), channel_id=1, source_target_pairs={{0,4},{12,8},{1,5},{13,9},{2,6},{14,10},{3,7},{15,11},{16,20},{28,... | collective-permute-start | bytes 1585160 | tf_op jit(solution)/shard_map/ppermute | solution.py:840
  116.7 13.7 %collective-permute-start.20 = (s16[2064,128]{1,0:T(8,128)(2,1)S(1)}, s16[2064,128]{1,0:T(8,128)(2,1)S(1)}, u32[]{:S(2)}, u32[]{:S(2)}) collective-permute-start(s16[2064,128]{1,0:T(8,128)(2,1)S(1)} %add_chunk.19.refs_2_.refs_0_), channel_id=1, source_target_pairs={{4,8},{8,4},{5,9},{9,5},{6,10},{10,6},{7,11},{11,7},{20,24},{24,20... | collective-permute-start | bytes 1585160 | tf_op jit(solution)/shard_map/ppermute | solution.py:834
  118.6 19.6 %collective-permute-start.19 = (s16[2064,128]{1,0:T(8,128)(2,1)S(1)}, s16[2064,128]{1,0:T(8,128)(2,1)S(1)}, u32[]{:S(2)}, u32[]{:S(2)}) collective-permute-start(s16[2064,128]{1,0:T(8,128)(2,1)S(1)} %add_chunk.20.refs_0_.total), channel_id=1, source_target_pairs={{4,0},{8,12},{5,1},{9,13},{6,2},{10,14},{7,3},{11,15},{20,16},{24,... | collective-permute-start | bytes 1585160 | tf_op jit(solution)/shard_map/ppermute | solution.py:837
  119.9 20.0 %collective-permute-start.18 = (s16[2064,128]{1,0:T(8,128)(2,1)S(1)}, s16[2064,128]{1,0:T(8,128)(2,1)S(1)}, u32[]{:S(2)}, u32[]{:S(2)}) collective-permute-start(s16[2064,128]{1,0:T(8,128)(2,1)S(1)} %grad_chunk.12.refs_6_.refs_0_), channel_id=1, source_target_pairs={{0,4},{12,8},{1,5},{13,9},{2,6},{14,10},{3,7},{15,11},{16,20},{28,... | collective-permute-start | bytes 1585160 | tf_op jit(solution)/shard_map/ppermute | solution.py:840
  129.7 12.0 %collective-permute-start.26 = (s16[2064,128]{1,0:T(8,128)(2,1)S(1)}, s16[2064,128]{1,0:T(8,128)(2,1)S(1)}, u32[]{:S(2)}, u32[]{:S(2)}) collective-permute-start(s16[2064,128]{1,0:T(8,128)(2,1)S(1)} %add_chunk.21.refs_2_.refs_0_), channel_id=1, source_target_pairs={{4,8},{8,4},{5,9},{9,5},{6,10},{10,6},{7,11},{11,7},{20,24},{24,20... | collective-permute-start | bytes 1585160 | tf_op jit(solution)/shard_map/ppermute | solution.py:834
  131.6 17.9 %collective-permute-start.25 = (s16[2064,128]{1,0:T(8,128)(2,1)S(1)}, s16[2064,128]{1,0:T(8,128)(2,1)S(1)}, u32[]{:S(2)}, u32[]{:S(2)}) collective-permute-start(s16[2064,128]{1,0:T(8,128)(2,1)S(1)} %add_chunk.22.refs_0_.total), channel_id=1, source_target_pairs={{4,0},{8,12},{5,1},{9,13},{6,2},{10,14},{7,3},{11,15},{20,16},{24,... | collective-permute-start | bytes 1585160 | tf_op jit(solution)/shard_map/ppermute | solution.py:837
  132.9 18.3 %collective-permute-start.24 = (s16[2064,128]{1,0:T(8,128)(2,1)S(1)}, s16[2064,128]{1,0:T(8,128)(2,1)S(1)}, u32[]{:S(2)}, u32[]{:S(2)}) collective-permute-start(s16[2064,128]{1,0:T(8,128)(2,1)S(1)} %grad_chunk.13.refs_6_.refs_0_), channel_id=1, source_target_pairs={{0,4},{12,8},{1,5},{13,9},{2,6},{14,10},{3,7},{15,11},{16,20},{28,... | collective-permute-start | bytes 1585160 | tf_op jit(solution)/shard_map/ppermute | solution.py:840
  141.0 12.0 %collective-permute-start.23 = (s16[2064,128]{1,0:T(8,128)(2,1)S(1)}, s16[2064,128]{1,0:T(8,128)(2,1)S(1)}, u32[]{:S(2)}, u32[]{:S(2)}) collective-permute-start(s16[2064,128]{1,0:T(8,128)(2,1)S(1)} %add_chunk.23.refs_2_.refs_0_), channel_id=1, source_target_pairs={{4,8},{8,4},{5,9},{9,5},{6,10},{10,6},{7,11},{11,7},{20,24},{24,20... | collective-permute-start | bytes 1585160 | tf_op jit(solution)/shard_map/ppermute | solution.py:834
  142.9 18.8 %collective-permute-start.31 = (s16[2064,128]{1,0:T(8,128)(2,1)S(1)}, s16[2064,128]{1,0:T(8,128)(2,1)S(1)}, u32[]{:S(2)}, u32[]{:S(2)}) collective-permute-start(s16[2064,128]{1,0:T(8,128)(2,1)S(1)} %add_chunk.24.refs_0_.total), channel_id=1, source_target_pairs={{4,0},{8,12},{5,1},{9,13},{6,2},{10,14},{7,3},{11,15},{20,16},{24,... | collective-permute-start | bytes 1585160 | tf_op jit(solution)/shard_map/ppermute | solution.py:837
  144.2 19.4 %collective-permute-start.30 = (s16[2064,128]{1,0:T(8,128)(2,1)S(1)}, s16[2064,128]{1,0:T(8,128)(2,1)S(1)}, u32[]{:S(2)}, u32[]{:S(2)}) collective-permute-start(s16[2064,128]{1,0:T(8,128)(2,1)S(1)} %grad_chunk.14.refs_2_.refs_0_), channel_id=1, source_target_pairs={{0,4},{12,8},{1,5},{13,9},{2,6},{14,10},{3,7},{15,11},{16,20},{28,... | collective-permute-start | bytes 1585160 | tf_op jit(solution)/shard_map/ppermute | solution.py:840
  152.4 13.1 %collective-permute-start.29 = (s16[2064,128]{1,0:T(8,128)(2,1)S(1)}, s16[2064,128]{1,0:T(8,128)(2,1)S(1)}, u32[]{:S(2)}, u32[]{:S(2)}) collective-permute-start(s16[2064,128]{1,0:T(8,128)(2,1)S(1)} %add_chunk.25.refs_2_.refs_0_), channel_id=1, source_target_pairs={{4,8},{8,4},{5,9},{9,5},{6,10},{10,6},{7,11},{11,7},{20,24},{24,20... | collective-permute-start | bytes 1585160 | tf_op jit(solution)/shard_map/ppermute | solution.py:834
  154.2 15.9 %collective-permute-start.28 = (s16[2064,128]{1,0:T(8,128)(2,1)S(1)}, s16[2064,128]{1,0:T(8,128)(2,1)S(1)}, u32[]{:S(2)}, u32[]{:S(2)}) collective-permute-start(s16[2064,128]{1,0:T(8,128)(2,1)S(1)} %add_chunk.26.refs_0_.total), channel_id=1, source_target_pairs={{4,0},{8,12},{5,1},{9,13},{6,2},{10,14},{7,3},{11,15},{20,16},{24,... | collective-permute-start | bytes 1585160 | tf_op jit(solution)/shard_map/ppermute | solution.py:837
  155.5 16.3 %collective-permute-start.27 = (s16[2064,128]{1,0:T(8,128)(2,1)S(1)}, s16[2064,128]{1,0:T(8,128)(2,1)S(1)}, u32[]{:S(2)}, u32[]{:S(2)}) collective-permute-start(s16[2064,128]{1,0:T(8,128)(2,1)S(1)} %grad_chunk.15.refs_2_.refs_0_), channel_id=1, source_target_pairs={{0,4},{12,8},{1,5},{13,9},{2,6},{14,10},{3,7},{15,11},{16,20},{28,... | collective-permute-start | bytes 1585160 | tf_op jit(solution)/shard_map/ppermute | solution.py:840
  164.8 8.9 %collective-permute-start.34 = (s16[2064,128]{1,0:T(8,128)(2,1)S(1)}, s16[2064,128]{1,0:T(8,128)(2,1)S(1)}, u32[]{:S(2)}, u32[]{:S(2)}) collective-permute-start(s16[2064,128]{1,0:T(8,128)(2,1)S(1)} %add_chunk.27.refs_2_.refs_0_), channel_id=1, source_target_pairs={{4,8},{8,4},{5,9},{9,5},{6,10},{10,6},{7,11},{11,7},{20,24},{24,20... | collective-permute-start | bytes 1585160 | tf_op jit(solution)/shard_map/ppermute | solution.py:834
  166.6 15.6 %collective-permute-start.33 = (s16[2064,128]{1,0:T(8,128)(2,1)S(1)}, s16[2064,128]{1,0:T(8,128)(2,1)S(1)}, u32[]{:S(2)}, u32[]{:S(2)}) collective-permute-start(s16[2064,128]{1,0:T(8,128)(2,1)S(1)} %add_chunk.28.refs_0_.total), channel_id=1, source_target_pairs={{4,0},{8,12},{5,1},{9,13},{6,2},{10,14},{7,3},{11,15},{20,16},{24,... | collective-permute-start | bytes 1585160 | tf_op jit(solution)/shard_map/ppermute | solution.py:837
  173.0 10.9 %collective-permute-start.32 = (s16[2064,128]{1,0:T(8,128)(2,1)S(1)}, s16[2064,128]{1,0:T(8,128)(2,1)S(1)}, u32[]{:S(2)}, u32[]{:S(2)}) collective-permute-start(s16[2064,128]{1,0:T(8,128)(2,1)S(1)} %add_chunk.29.refs_2_.refs_0_), channel_id=1, source_target_pairs={{4,8},{8,4},{5,9},{9,5},{6,10},{10,6},{7,11},{11,7},{20,24},{24,20... | collective-permute-start | bytes 1585160 | tf_op jit(solution)/shard_map/ppermute | solution.py:834
  174.8 18.7 %collective-permute-start.36 = (s16[2064,128]{1,0:T(8,128)(2,1)S(1)}, s16[2064,128]{1,0:T(8,128)(2,1)S(1)}, u32[]{:S(2)}, u32[]{:S(2)}) collective-permute-start(s16[2064,128]{1,0:T(8,128)(2,1)S(1)} %add_chunk.30.refs_0_.total), channel_id=1, source_target_pairs={{4,0},{8,12},{5,1},{9,13},{6,2},{10,14},{7,3},{11,15},{20,16},{24,... | collective-permute-start | bytes 1585160 | tf_op jit(solution)/shard_map/ppermute | solution.py:837
  185.1 17.9 %collective-permute-start.35 = (s16[2064,128]{1,0:T(8,128)(2,1)S(1)}, s16[2064,128]{1,0:T(8,128)(2,1)S(1)}, u32[]{:S(2)}, u32[]{:S(2)}) collective-permute-start(s16[2064,128]{1,0:T(8,128)(2,1)S(1)} %add_chunk.31.refs_0_.total), channel_id=1, source_target_pairs={{4,0},{8,12},{5,1},{9,13},{6,2},{10,14},{7,3},{11,15},{20,16},{24,... | collective-permute-start | bytes 1585160 | tf_op jit(solution)/shard_map/ppermute | solution.py:837
  (19 other events, 134.5 us)
